TPU v7x, 32 devices: a whole 2x2x4 slice. The times are simulated.
32 devices in a mesh: section: 2 (over core), dp: 4 (over z), ctx: 4 (over y, x).
Axes of the slice: x: 2, y: 2, z: 4, core: 2. Of those that a mesh axis runs over, the one named last changes fastest.
Arguments:
- inputs: bfloat16 [2, 4, 1024, 960], P(None, 'dp', 'ctx'), may hold values from -6 to 6
- segment_ids: int32 [2, 4, 1024], P(None, 'dp'), may hold values from 0 to 11, as said below
- cotangent: bfloat16 [2, 4, 1024, 960], P(None, 'dp', 'ctx'), may hold values from -6 to 6
- gain_attn: bfloat16 [960], replicated, may hold values from 0.099609375 to 1.8984375
- w_query: bfloat16 [960, 960], replicated, may hold values from -0.1875 to 0.1875
- w_key: bfloat16 [960, 320], replicated, may hold values from -0.1875 to 0.1875
- w_value: bfloat16 [960, 320], replicated, may hold values from -0.1875 to 0.1875
- w_out: bfloat16 [960, 960], replicated, may hold values from -0.75 to 0.75
- gain_ffn: bfloat16 [960], replicated, may hold values from 0.099609375 to 1.8984375
- w_gate: bfloat16 [960, 2560], replicated, may hold values from -0.1875 to 0.1875
- w_up: bfloat16 [960, 2560], replicated, may hold values from -0.1875 to 0.1875
- w_down: bfloat16 [2560, 960], replicated, may hold values from -0.125 to 0.125
Outputs:
- activations: bfloat16 [2, 2, 4, 1024, 960], P('section', None, 'dp', 'ctx')
- input_grads: float32 [2, 2, 4, 1024, 960], P('section', None, 'dp', 'ctx')
- grad_gain_attn: float32 [960], P('dp')
- grad_w_query: float32 [960, 960], P('dp')
- grad_w_key: float32 [960, 320], P('dp')
- grad_w_value: float32 [960, 320], P('dp')
- grad_w_out: float32 [960, 960], P('dp')
- grad_gain_ffn: float32 [960], P('dp')
- grad_w_gate: float32 [960, 2560], P('dp')
- grad_w_up: float32 [960, 2560], P('dp')
- grad_w_down: float32 [2560, 960], P('dp')
Inputs may be any that keep to these rules, and one draw needn't show every extreme that they name: `segment_ids`: document numbers never fall along a row, start at 0. On each index of dp, one of its rows of the micro-batches, drawn from the seed, holds a document that begins within its first 256 tokens and ends within its last 256.
All inputs are finite; a program needn't handle non-finite values.
Results may differ from a plain program's by a relative error of at most 0.035.
Values may be sent and summed in bfloat16 or wider, within the bound.
A program may use at most 256 MiB of HBM per device.

v0:
```python
import math

import jax
import jax.numpy as jnp
from jax import lax
from jax.sharding import PartitionSpec as P

HEADS = 15
KV_HEADS = 5
HEAD_DIM = 64


epsilon = 1e-05
score_scale = 0.125
mask_floor = -1e30


def shifted(x, axis, by):
    count = lax.axis_size(axis)
    pairs = [(i, i + by) for i in range(count) if 0 <= i + by < count]
    return lax.ppermute(x, axis, pairs)


def rms_forward(values, gain_vec):
    inverse = lax.rsqrt(jnp.mean(values * values, -1, keepdims=True) + epsilon)
    return (values * inverse * gain_vec, inverse)


def rms_backward(values, gain_vec, inverse, grad_normed):
    weighted = grad_normed * gain_vec
    grad_gain = jnp.sum(grad_normed * values * inverse, axis=(0, 1))
    cubed = inverse * inverse * inverse
    grad_values = inverse * weighted - values * cubed * jnp.mean(
        weighted * values, -1, keepdims=True
    )
    return (grad_values, grad_gain)


def rotate(values, cos_table, sine_table):
    halfway = values.shape[-1] // 2
    former = values[..., :halfway]
    latter = values[..., halfway:]
    cos_part = cos_table[None, :, None, :]
    sine_part = sine_table[None, :, None, :]
    return jnp.concatenate(
        [former * cos_part - latter * sine_part, latter * cos_part + former * sine_part], -1
    )


def block_scores(queries, key_part, query_seg, key_seg, query_pos, offset):
    block_rows = key_part.shape[1]
    scores = (
        jnp.einsum("rckgd,rnkd->rkgcn", queries, key_part, preferred_element_type=jnp.float32)
        * score_scale
    )
    key_pos = offset + jnp.arange(block_rows, dtype=jnp.int32)
    allowed = (query_seg[:, :, None] == key_seg[:, None, :]) & (
        key_pos[None, None, :] <= query_pos[None, :, None]
    )
    return (scores, allowed[:, None, None, :, :])


def select_by(flag, former_val, latter_val):
    return jax.tree.map(
        lambda left_val, right_val: jnp.where(flag, left_val, right_val), former_val, latter_val
    )


def body(
    inputs,
    segment_ids,
    cotangent,
    gain_attn,
    w_query,
    w_key,
    w_value,
    w_out,
    gain_ffn,
    w_gate,
    w_up,
    w_down,
):
    micro_count, row_count, tok_local, model_width = inputs.shape
    kv_width = w_key.shape[1]
    group_size = HEADS // KV_HEADS
    section_index = lax.axis_index("section")
    on_first = section_index == 0
    on_last = section_index == 1
    ctx_index = lax.axis_index("ctx")
    first_token = ctx_index * tok_local
    query_pos = first_token + jnp.arange(tok_local, dtype=jnp.int32)
    halfway = HEAD_DIM // 2
    frequency = 10000.0 ** (-2.0 * jnp.arange(halfway, dtype=jnp.float32) / HEAD_DIM)
    angles = query_pos.astype(jnp.float32)[:, None] * frequency[None, :]
    cos_table = jnp.cos(angles)
    sine_table = jnp.sin(angles)
    w_pair = jnp.concatenate([w_key, w_value], 1)
    head_shape = (row_count, tok_local, KV_HEADS, group_size, HEAD_DIM)
    state_shape = (row_count, KV_HEADS, group_size, tok_local)

    def front(hidden, segments):
        query_seg = lax.dynamic_slice_in_dim(segments, first_token, tok_local, 1)
        normed, inverse = rms_forward(hidden, gain_attn)
        normed_low = normed.astype(jnp.bfloat16)
        query_pre = jnp.einsum(
            "rcd,de->rce", normed_low, w_query, preferred_element_type=jnp.float32
        )
        pair_pre = jnp.einsum("rcd,de->rce", normed_low, w_pair, preferred_element_type=jnp.float32)
        queries = rotate(
            query_pre.reshape(row_count, tok_local, HEADS, HEAD_DIM), cos_table, sine_table
        )
        queries = queries.astype(jnp.bfloat16).reshape(head_shape)
        key_rot = rotate(
            pair_pre[..., :kv_width].reshape(row_count, tok_local, KV_HEADS, HEAD_DIM),
            cos_table,
            sine_table,
        )
        packed = jnp.concatenate(
            [key_rot.reshape(row_count, tok_local, kv_width), pair_pre[..., kv_width:]], -1
        )
        return (query_seg, inverse, normed_low, queries, packed.astype(jnp.bfloat16))

    def attend_forward(queries, packed, segments, query_seg):
        start_state = (
            jnp.full(state_shape, mask_floor, jnp.float32),
            jnp.zeros(state_shape, jnp.float32),
            jnp.zeros(state_shape + (HEAD_DIM,), jnp.float32),
        )
        arrived = lax.all_gather(packed, "ctx", axis=1, tiled=True)
        piece_rows = arrived.shape[1]
        block_rows = math.gcd(piece_rows, 512)

        def fold_inner_step(step_index, loop_state):
            run_max, run_sum, run_acc = loop_state
            offset = step_index * block_rows
            key_block = lax.dynamic_slice_in_dim(arrived, step_index * block_rows, block_rows, 1)
            key_part = key_block[..., :kv_width].reshape(row_count, block_rows, KV_HEADS, HEAD_DIM)
            value_part = key_block[..., kv_width:].reshape(
                row_count, block_rows, KV_HEADS, HEAD_DIM
            )
            key_seg = lax.dynamic_slice_in_dim(segments, offset, block_rows, 1)
            scores, allowed = block_scores(queries, key_part, query_seg, key_seg, query_pos, offset)
            masked = jnp.where(allowed, scores, mask_floor)
            new_max = jnp.maximum(run_max, jnp.max(masked, -1))
            weights = jnp.where(allowed, jnp.exp(masked - new_max[..., None]), 0.0)
            rescale = jnp.exp(run_max - new_max)
            run_sum = run_sum * rescale + jnp.sum(weights, -1)
            run_acc = run_acc * rescale[..., None] + jnp.einsum(
                "rkgcn,rnkd->rkgcd",
                weights.astype(jnp.bfloat16),
                value_part,
                preferred_element_type=jnp.float32,
            )
            return (new_max, run_sum, run_acc)

        run_max, run_sum, run_acc = lax.fori_loop(
            0, piece_rows // block_rows, fold_inner_step, start_state
        )
        return (run_acc / run_sum[..., None], run_max + jnp.log(run_sum))

    def rear(hidden, attended):
        attn_low = (
            attended.transpose(0, 3, 1, 2, 4)
            .reshape(row_count, tok_local, HEADS * HEAD_DIM)
            .astype(jnp.bfloat16)
        )
        middle = hidden + jnp.einsum(
            "rce,ed->rcd", attn_low, w_out, preferred_element_type=jnp.float32
        )
        normed_ffn, inverse_ffn = rms_forward(middle, gain_ffn)
        ffn_low = normed_ffn.astype(jnp.bfloat16)
        gate_pre = jnp.einsum("rcd,df->rcf", ffn_low, w_gate, preferred_element_type=jnp.float32)
        upward = jnp.einsum("rcd,df->rcf", ffn_low, w_up, preferred_element_type=jnp.float32)
        inner_act = (jax.nn.silu(gate_pre) * upward).astype(jnp.bfloat16)
        output = middle + jnp.einsum(
            "rcf,fd->rcd", inner_act, w_down, preferred_element_type=jnp.float32
        )
        return (output, (attn_low, middle, inverse_ffn, ffn_low, gate_pre, upward, inner_act))

    tick_inputs = []
    tick_outputs = []
    tick_stash = []
    incoming = jnp.zeros((row_count, tok_local, model_width), jnp.bfloat16)
    for moment in range(micro_count + 1):
        early_index = min(moment, micro_count - 1)
        late_index = max(moment - 1, 0)
        hidden = jnp.where(on_first, inputs[early_index], incoming).astype(jnp.float32)
        segments = jnp.where(on_first, segment_ids[early_index], segment_ids[late_index])
        forward_query_seg, forward_inverse, forward_normed_low, forward_queries, forward_packed = (
            front(hidden, segments)
        )
        forward_attended, forward_log_sum = attend_forward(
            forward_queries, forward_packed, segments, forward_query_seg
        )
        forward_output, forward_saved = rear(hidden, forward_attended)
        output = forward_output
        stash = (forward_attended, forward_log_sum)
        output_low = output.astype(jnp.bfloat16)
        tick_inputs.append(hidden)
        tick_outputs.append(output_low)
        tick_stash.append(stash)
        if moment < micro_count:
            incoming = shifted(output_low, "section", 1)
    kept_inputs = [
        select_by(on_first, tick_inputs[number], tick_inputs[number + 1])
        for number in range(micro_count)
    ]
    kept_stash = [
        select_by(on_first, tick_stash[number], tick_stash[number + 1])
        for number in range(micro_count)
    ]
    act_list = [
        select_by(on_first, tick_outputs[number], tick_outputs[number + 1])
        for number in range(micro_count)
    ]
    grad_sums = None
    grad_list = []
    incoming_grad = jnp.zeros((row_count, tok_local, model_width), jnp.bfloat16)
    for moment in range(micro_count + 1):
        early_index = min(moment, micro_count - 1)
        late_index = max(moment - 1, 0)
        hidden = select_by(on_last, kept_inputs[early_index], kept_inputs[late_index])
        segments = jnp.where(on_last, segment_ids[early_index], segment_ids[late_index])
        stash = select_by(on_last, kept_stash[early_index], kept_stash[late_index])
        grad_out = jnp.where(
            on_last, cotangent[early_index].astype(jnp.float32), incoming_grad.astype(jnp.float32)
        )
        tick_valid = jnp.where(on_last, float(moment < micro_count), float(moment >= 1))
        (
            backward_query_seg,
            backward_inverse,
            backward_normed_low,
            backward_queries,
            backward_packed,
        ) = front(hidden, segments)
        backward_attended, log_sum = attend_forward(
            backward_queries, backward_packed, segments, backward_query_seg
        )
        backward_output, saved = rear(hidden, backward_attended)
        (
            backward_attn_low,
            backward_middle,
            backward_inverse_ffn,
            backward_ffn_low,
            backward_gate_pre,
            backward_upward,
            backward_inner_act,
        ) = saved
        grad_low = grad_out.astype(jnp.bfloat16)
        grad_inner = jnp.einsum("rcd,fd->rcf", grad_low, w_down, preferred_element_type=jnp.float32)
        backward_sum_down = jnp.einsum(
            "rcf,rcd->fd", backward_inner_act, grad_low, preferred_element_type=jnp.float32
        )
        sigmoid = jax.nn.sigmoid(backward_gate_pre)
        grad_gate = (
            grad_inner * backward_upward * sigmoid * (1.0 + backward_gate_pre * (1.0 - sigmoid))
        ).astype(jnp.bfloat16)
        grad_up = (grad_inner * backward_gate_pre * sigmoid).astype(jnp.bfloat16)
        backward_sum_gate = jnp.einsum(
            "rcd,rcf->df", backward_ffn_low, grad_gate, preferred_element_type=jnp.float32
        )
        backward_sum_up = jnp.einsum(
            "rcd,rcf->df", backward_ffn_low, grad_up, preferred_element_type=jnp.float32
        )
        grad_norm_ffn = jnp.einsum(
            "rcf,df->rcd", grad_gate, w_gate, preferred_element_type=jnp.float32
        ) + jnp.einsum("rcf,df->rcd", grad_up, w_up, preferred_element_type=jnp.float32)
        grad_mid_norm, backward_sum_gain_ffn = rms_backward(
            backward_middle, gain_ffn, backward_inverse_ffn, grad_norm_ffn
        )
        grad_middle = grad_out + grad_mid_norm
        grad_branch = grad_middle.astype(jnp.bfloat16)
        backward_sum_out = jnp.einsum(
            "rce,rcd->ed", backward_attn_low, grad_branch, preferred_element_type=jnp.float32
        )
        grad_attn = jnp.einsum(
            "rcd,ed->rce", grad_branch, w_out, preferred_element_type=jnp.float32
        ).astype(jnp.bfloat16)
        grad_heads = grad_attn.reshape(head_shape).transpose(0, 2, 3, 1, 4)
        row_delta = jnp.sum(grad_heads.astype(jnp.float32) * backward_attended, -1)
        query_start = jnp.zeros(state_shape + (HEAD_DIM,), jnp.float32)
        fold_grad_query = query_start
        piece_arrived = lax.all_gather(backward_packed, "ctx", axis=1, tiled=True)
        grad_query = fold_grad_query
        piece_piece_rows = piece_arrived.shape[1]
        piece_block_rows = math.gcd(piece_piece_rows, 512)

        def piece_inner_step(step_index, loop_state):
            grad_query, local_pair = loop_state
            inside = step_index * piece_block_rows
            key_block = lax.dynamic_slice_in_dim(piece_arrived, inside, piece_block_rows, 1)
            key_part = key_block[..., :kv_width].reshape(
                row_count, piece_block_rows, KV_HEADS, HEAD_DIM
            )
            value_part = key_block[..., kv_width:].reshape(
                row_count, piece_block_rows, KV_HEADS, HEAD_DIM
            )
            key_seg = lax.dynamic_slice_in_dim(segments, inside, piece_block_rows, 1)
            scores, allowed = block_scores(
                backward_queries, key_part, backward_query_seg, key_seg, query_pos, inside
            )
            chances = jnp.where(
                allowed, jnp.exp(jnp.where(allowed, scores, mask_floor) - log_sum[..., None]), 0.0
            )
            grad_chance = jnp.einsum(
                "rkgcd,rnkd->rkgcn", grad_heads, value_part, preferred_element_type=jnp.float32
            )
            grad_scores = (chances * (grad_chance - row_delta[..., None])).astype(jnp.bfloat16)
            grad_query = grad_query + score_scale * jnp.einsum(
                "rkgcn,rnkd->rkgcd", grad_scores, key_part, preferred_element_type=jnp.float32
            )
            grad_key = score_scale * jnp.einsum(
                "rkgcn,rckgd->rnkd",
                grad_scores,
                backward_queries,
                preferred_element_type=jnp.float32,
            )
            grad_value = jnp.einsum(
                "rkgcn,rkgcd->rnkd",
                chances.astype(jnp.bfloat16),
                grad_heads,
                preferred_element_type=jnp.float32,
            )
            update = jnp.concatenate(
                [
                    grad_key.reshape(row_count, piece_block_rows, kv_width),
                    grad_value.reshape(row_count, piece_block_rows, kv_width),
                ],
                -1,
            )
            current = lax.dynamic_slice_in_dim(local_pair, inside, piece_block_rows, 1)
            local_pair = lax.dynamic_update_slice_in_dim(local_pair, current + update, inside, 1)
            return (grad_query, local_pair)

        local_start = jnp.zeros((row_count, piece_piece_rows, 2 * kv_width), jnp.float32)
        fold_grad_query, fold_local_pair = lax.fori_loop(
            0, piece_piece_rows // piece_block_rows, piece_inner_step, (grad_query, local_start)
        )
        grad_pair = fold_local_pair
        grad_query, grad_pair = (fold_grad_query, grad_pair)
        pair_share = lax.psum_scatter(
            grad_pair.astype(jnp.bfloat16), "ctx", scatter_dimension=1, tiled=True
        ).astype(jnp.float32)
        query_tok = grad_query.transpose(0, 3, 1, 2, 4).reshape(
            row_count, tok_local, HEADS, HEAD_DIM
        )
        query_back = rotate(query_tok, cos_table, -sine_table).reshape(
            row_count, tok_local, HEADS * HEAD_DIM
        )
        query_back = query_back.astype(jnp.bfloat16)
        key_back = rotate(
            pair_share[..., :kv_width].reshape(row_count, tok_local, KV_HEADS, HEAD_DIM),
            cos_table,
            -sine_table,
        )
        pair_low = jnp.concatenate(
            [key_back.reshape(row_count, tok_local, kv_width), pair_share[..., kv_width:]], -1
        )
        pair_low = pair_low.astype(jnp.bfloat16)
        backward_sum_query = jnp.einsum(
            "rcd,rce->de", backward_normed_low, query_back, preferred_element_type=jnp.float32
        )
        sum_pair = jnp.einsum(
            "rcd,rce->de", backward_normed_low, pair_low, preferred_element_type=jnp.float32
        )
        grad_normed = jnp.einsum(
            "rce,de->rcd", query_back, w_query, preferred_element_type=jnp.float32
        ) + jnp.einsum("rce,de->rcd", pair_low, w_pair, preferred_element_type=jnp.float32)
        grad_front, backward_sum_gain_attn = rms_backward(
            hidden, gain_attn, backward_inverse, grad_normed
        )
        tick_grads = (
            backward_sum_gain_attn,
            backward_sum_query,
            sum_pair[:, :kv_width],
            sum_pair[:, kv_width:],
            backward_sum_out,
            backward_sum_gain_ffn,
            backward_sum_gate,
            backward_sum_up,
            backward_sum_down,
        )
        grad_hidden, tick_grads = (grad_middle + grad_front, tick_grads)
        tick_grads = tuple((tick_valid * member for member in tick_grads))
        if grad_sums is None:
            grad_sums = tick_grads
        else:
            grad_sums = tuple(
                (accumulated + addition for accumulated, addition in zip(grad_sums, tick_grads))
            )
        grad_low = grad_hidden.astype(jnp.bfloat16)
        grad_list.append((grad_hidden, grad_low.astype(jnp.float32)))
        if moment < micro_count:
            incoming_grad = shifted(grad_low, "section", -1)
    grad_rows = [
        jnp.where(on_last, grad_list[number][1], grad_list[number + 1][0])
        for number in range(micro_count)
    ]
    (
        sum_gain_attn,
        sum_query,
        sum_key,
        sum_value,
        sum_out,
        sum_gain_ffn,
        sum_gate,
        sum_up,
        sum_down,
    ) = grad_sums
    shares = (
        lax.psum_scatter(
            sum_gain_attn.astype(jnp.bfloat16), "dp", scatter_dimension=0, tiled=True
        ).astype(jnp.float32),
        lax.psum_scatter(
            sum_query.astype(jnp.bfloat16), "dp", scatter_dimension=0, tiled=True
        ).astype(jnp.float32),
        lax.psum_scatter(
            sum_key.astype(jnp.bfloat16), "dp", scatter_dimension=0, tiled=True
        ).astype(jnp.float32),
        lax.psum_scatter(
            sum_value.astype(jnp.bfloat16), "dp", scatter_dimension=0, tiled=True
        ).astype(jnp.float32),
        lax.psum_scatter(
            sum_out.astype(jnp.bfloat16), "dp", scatter_dimension=0, tiled=True
        ).astype(jnp.float32),
        lax.psum_scatter(
            sum_gain_ffn.astype(jnp.bfloat16), "dp", scatter_dimension=0, tiled=True
        ).astype(jnp.float32),
        lax.psum_scatter(
            sum_gate.astype(jnp.bfloat16), "dp", scatter_dimension=0, tiled=True
        ).astype(jnp.float32),
        lax.psum_scatter(sum_up.astype(jnp.bfloat16), "dp", scatter_dimension=0, tiled=True).astype(
            jnp.float32
        ),
        lax.psum_scatter(
            sum_down.astype(jnp.bfloat16), "dp", scatter_dimension=0, tiled=True
        ).astype(jnp.float32),
    )
    totals = (
        lax.psum(shares[0].astype(jnp.bfloat16), ("section", "ctx")).astype(jnp.float32),
        lax.psum(shares[1].astype(jnp.bfloat16), ("section", "ctx")).astype(jnp.float32),
        lax.psum(shares[2].astype(jnp.bfloat16), ("section", "ctx")).astype(jnp.float32),
        lax.psum(shares[3].astype(jnp.bfloat16), ("section", "ctx")).astype(jnp.float32),
        lax.psum(shares[4].astype(jnp.bfloat16), ("section", "ctx")).astype(jnp.float32),
        lax.psum(shares[5].astype(jnp.bfloat16), ("section", "ctx")).astype(jnp.float32),
        lax.psum(shares[6].astype(jnp.bfloat16), ("section", "ctx")).astype(jnp.float32),
        lax.psum(shares[7].astype(jnp.bfloat16), ("section", "ctx")).astype(jnp.float32),
        lax.psum(shares[8].astype(jnp.bfloat16), ("section", "ctx")).astype(jnp.float32),
    )
    activations = jnp.stack(act_list)[None]
    input_grads = jnp.stack(grad_rows)[None]
    return (
        activations,
        input_grads,
        totals[0],
        totals[1],
        totals[2],
        totals[3],
        totals[4],
        totals[5],
        totals[6],
        totals[7],
        totals[8],
    )


def solution(mesh):
    placed = (
        P(None, "dp", "ctx", None),
        P(None, "dp", None),
        P(None, "dp", "ctx", None),
        P(),
        P(),
        P(),
        P(),
        P(),
        P(),
        P(),
        P(),
        P(),
    )
    return jax.shard_map(
        body,
        mesh=mesh,
        in_specs=placed,
        out_specs=(
            P("section", None, "dp", "ctx", None),
            P("section", None, "dp", "ctx", None),
            P("dp"),
            P("dp", None),
            P("dp", None),
            P("dp", None),
            P("dp", None),
            P("dp"),
            P("dp", None),
            P("dp", None),
            P("dp", None),
        ),
        check_vma=False,
    )
```

profile of v0, /device:TPU:0, one launch (start us, length us, event | category | flops | bytes accessed | tf_op | source)
XLA Modules:
  0.0 1217.5 jit_solution(399792968337785735)
XLA Ops:
  27.9 23.8 %all-gather.7.cloned.1.call-done = bf16[1,1024,640]{2,1,0:T(8,128)(2,1)} async-done(((bf16[1,256,640]{2,1,0:T(8,128)(2,1)}), bf16[1,1024,640]{2,1,0:T(8,128)(2,1)}) %all-gather.7.cloned.1.call-update) | async-done | bytes 1310736 | tf_op jit(solution)/shard_map/all_gather | solution.py:129
  51.8 32.0 %while.156 = (s32[]{:T(128)}, f32[1,5,3,256]{3,2,1,0:T(4,128)S(1)}, f32[1,5,3,256]{3,2,1,0:T(4,128)S(1)}, f32[1,5,3,256,64]{3,4,2,1,0:T(8,128)}, s32[1,256]{1,0:...) while((s32[]{:T(128)}, f32[1,5,3,256]{3,2,1,0:T(4,128)S(1)}, ...), condition=%wide.region_4.5_spmd.clone, body=%wide.region_1.4_spmd.clone.sunk | while | flops 530029824 | bytes 53703948 | solution.py:156
  93.5 9.0 fusion.220
  113.9 24.9 %all-gather.9.cloned.1.call-done = bf16[1,1024,640]{2,1,0:T(8,128)(2,1)} async-done(((bf16[1,256,640]{2,1,0:T(8,128)(2,1)}), bf16[1,1024,640]{2,1,0:T(8,128)(2,1)}) %all-gather.9.cloned.1.call-update) | async-done | bytes 1310736 | tf_op jit(solution)/shard_map/all_gather | solution.py:129
  138.7 32.0 %while.157 = (s32[]{:T(128)}, f32[1,5,3,256]{3,2,1,0:T(4,128)S(1)}, f32[1,5,3,256]{3,2,1,0:T(4,128)S(1)}, f32[1,5,3,256,64]{3,4,2,1,0:T(8,128)}, s32[1,256]{1,0:...) while((s32[]{:T(128)}, f32[1,5,3,256]{3,2,1,0:T(4,128)S(1)}, ...), condition=%wide.region_10.11_spmd.clone, body=%wide.region_7.10_spmd.clone.sunk | while | flops 530029824 | bytes 53703948 | solution.py:156
  180.5 8.2 fusion.217
  199.8 26.4 %all-gather.13.cloned.1.call-done = bf16[1,1024,640]{2,1,0:T(8,128)(2,1)} async-done(((bf16[1,256,640]{2,1,0:T(8,128)(2,1)}), bf16[1,1024,640]{2,1,0:T(8,128)(2,1)}) %all-gather.13.cloned.1.call-update) | async-done | bytes 1310736 | tf_op jit(solution)/shard_map/all_gather | solution.py:129
  228.7 30.5 %while.159 = (s32[]{:T(128)}, f32[1,5,3,256]{3,2,1,0:T(4,128)S(1)}, f32[1,5,3,256]{3,2,1,0:T(4,128)S(1)}, f32[1,5,3,256,64]{3,4,2,1,0:T(8,128)}, s32[1,256]{1,0:...) while((s32[]{:T(128)}, f32[1,5,3,256]{3,2,1,0:T(4,128)S(1)}, ...), condition=%wide.region_22.23_spmd.clone, body=%wide.region_19.22_spmd.clone.sunk | while | flops 530029824 | bytes 52393228 | solution.py:156
  279.6 35.4 %while.160 = (s32[]{:T(128)}, f32[1,5,3,256,64]{3,4,2,1,0:T(8,128)}, f32[1,1024,640]{1,2,0:T(8,128)}, s32[1,256]{1,0:T(1,128)S(1)}, s32[1,1024]{1,0:T(1,128)S(1)...) while((s32[]{:T(128)}, f32[1,5,3,256,64]{3,4,2,1,0:T(8,128)}, ...), condition=%wide.region_27.28_spmd.clone, body=%wide.region_26.27_spmd.clone.sunk | while | flops 1283834624 | bytes 63039756 | solution.py:336
  323.0 24.5 %reduce-scatter.13.cloned.1.call-done = bf16[1,256,640]{1,2,0:T(8,128)(2,1)} async-done(((bf16[1,1024,640]{1,2,0:T(8,128)(2,1)}), bf16[1,256,640]{1,2,0:T(8,128)(2,1)}) %reduce-scatter.13.cloned.1.call-update) | async-done | bytes 327696 | tf_op jit(solution)/shard_map/reduce_scatter | solution.py:341
  382.5 14.4 %all-gather.15.cloned.1.call-done = bf16[1,1024,640]{2,1,0:T(8,128)(2,1)} async-done(((bf16[1,256,640]{2,1,0:T(8,128)(2,1)}), bf16[1,1024,640]{2,1,0:T(8,128)(2,1)}) %all-gather.15.cloned.1.call-update) | async-done | bytes 1310736 | tf_op jit(solution)/shard_map/all_gather | solution.py:129
  399.3 29.1 %while.161 = (s32[]{:T(128)}, f32[1,5,3,256]{3,2,1,0:T(4,128)S(1)}, f32[1,5,3,256]{3,2,1,0:T(4,128)S(1)}, f32[1,5,3,256,64]{3,4,2,1,0:T(8,128)}, s32[1,256]{1,0:...) while((s32[]{:T(128)}, f32[1,5,3,256]{3,2,1,0:T(4,128)S(1)}, ...), condition=%wide.region_34.35_spmd.clone, body=%wide.region_31.34_spmd.clone.sunk | while | flops 530029824 | bytes 52393228 | solution.py:156
  451.8 29.1 %while.163 = (s32[]{:T(128)}, f32[1,5,3,256]{3,2,1,0:T(4,128)S(1)}, f32[1,5,3,256]{3,2,1,0:T(4,128)S(1)}, f32[1,5,3,256,64]{3,4,2,1,0:T(8,128)}, s32[1,256]{1,0:...) while((s32[]{:T(128)}, f32[1,5,3,256]{3,2,1,0:T(4,128)S(1)}, ...), condition=%wide.region_46.47_spmd.clone, body=%wide.region_43.46_spmd.clone.sunk | while | flops 530029824 | bytes 52393228 | solution.py:156
  492.1 35.5 %while.162 = (s32[]{:T(128)}, f32[1,5,3,256,64]{3,4,2,1,0:T(8,128)}, f32[1,1024,640]{1,2,0:T(8,128)}, s32[1,256]{1,0:T(1,128)S(1)}, s32[1,1024]{1,0:T(1,128)S(1)...) while((s32[]{:T(128)}, f32[1,5,3,256,64]{3,4,2,1,0:T(8,128)}, ...), condition=%wide.region_39.40_spmd.clone, body=%wide.region_38.39_spmd.clone.sunk | while | flops 1283834624 | bytes 65067332 | solution.py:336
  540.0 20.2 %reduce-scatter.15.cloned.1.call-done = bf16[1,256,640]{1,2,0:T(8,128)(2,1)} async-done(((bf16[1,1024,640]{1,2,0:T(8,128)(2,1)}), bf16[1,256,640]{1,2,0:T(8,128)(2,1)}) %reduce-scatter.15.cloned.1.call-update) | async-done | bytes 327696 | tf_op jit(solution)/shard_map/reduce_scatter | solution.py:341
  587.7 35.5 %while.164 = (s32[]{:T(128)}, f32[1,5,3,256,64]{3,4,2,1,0:T(8,128)}, f32[1,1024,640]{1,2,0:T(8,128)}, s32[1,256]{1,0:T(1,128)S(1)}, s32[1,1024]{1,0:T(1,128)S(1)...) while((s32[]{:T(128)}, f32[1,5,3,256,64]{3,4,2,1,0:T(8,128)}, ...), condition=%wide.region_51.52_spmd.clone, body=%wide.region_50.51_spmd.clone.sunk | while | flops 1283834624 | bytes 63101220 | solution.py:336
  626.5 7.8 fusion.205
  641.8 9.5 add_convert_fusion
  651.3 7.8 copy.190
  689.9 7.9 fusion.390
  722.2 32.1 %while.158 = (s32[]{:T(128)}, f32[1,5,3,256]{3,2,1,0:T(4,128)S(1)}, f32[1,5,3,256]{3,2,1,0:T(4,128)S(1)}, f32[1,5,3,256,64]{3,4,2,1,0:T(8,128)}, s32[1,256]{1,0:...) while((s32[]{:T(128)}, f32[1,5,3,256]{3,2,1,0:T(4,128)S(1)}, ...), condition=%wide.region_16.17_spmd.clone, body=%wide.region_13.16_spmd.clone.sunk | while | flops 530029824 | bytes 53703948 | solution.py:156
  763.1 20.8 %reduce-scatter.31.cloned.1.call-done = bf16[640,960]{1,0:T(8,128)(2,1)} async-done(((bf16[2560,960]{1,0:T(8,128)(2,1)}), bf16[640,960]{1,0:T(8,128)(2,1)}) %reduce-scatter.31.cloned.1.call-update) | async-done | bytes 1228816
  786.5 42.3 %reduce-scatter.25.cloned.1.call-done = bf16[240,960]{1,0:T(8,128)(2,1)} async-done(((bf16[960,960]{1,0:T(8,128)(2,1)}), bf16[240,960]{1,0:T(8,128)(2,1)}) %reduce-scatter.25.cloned.1.call-update) | async-done | bytes 460816 | tf_op jit(solution)/shard_map/reduce_scatter | solution.py:423
  828.8 43.4 %reduce-scatter.19.cloned.1.call-done = bf16[240,960]{1,0:T(8,128)(2,1)} async-done(((bf16[960,960]{1,0:T(8,128)(2,1)}), bf16[240,960]{1,0:T(8,128)(2,1)}) %reduce-scatter.19.cloned.1.call-update) | async-done | bytes 460816 | tf_op jit(solution)/shard_map/reduce_scatter | solution.py:414
  872.2 25.1 %reduce-scatter.21.cloned.1.call-done = bf16[240,320]{1,0:T(8,128)(2,1)} async-done(((bf16[960,320]{1,0:T(8,128)(2,1)}), bf16[240,320]{1,0:T(8,128)(2,1)}) %reduce-scatter.21.cloned.1.call-update) | async-done | bytes 153616 | tf_op jit(solution)/shard_map/reduce_scatter | solution.py:417
  897.3 24.7 %reduce-scatter.23.cloned.1.call-done = bf16[240,320]{1,0:T(8,128)(2,1)} async-done(((bf16[960,320]{1,0:T(8,128)(2,1)}), bf16[240,320]{1,0:T(8,128)(2,1)}) %reduce-scatter.23.cloned.1.call-update) | async-done | bytes 153616 | tf_op jit(solution)/shard_map/reduce_scatter | solution.py:420
  922.0 89.8 %reduce-scatter.29.cloned.1.call-done = bf16[240,2560]{1,0:T(8,128)(2,1)} async-done(((bf16[960,2560]{1,0:T(8,128)(2,1)}), bf16[240,2560]{1,0:T(8,128)(2,1)}) %reduce-scatter.29.cloned.1.call-update) | async-done | bytes 1228816 | tf_op jit(solution)/shard_map/reduce_scatter | solution.py:432
  1011.8 91.3 %reduce-scatter.27.cloned.1.call-done = bf16[240,2560]{1,0:T(8,128)(2,1)} async-done(((bf16[960,2560]{1,0:T(8,128)(2,1)}), bf16[240,2560]{1,0:T(8,128)(2,1)}) %reduce-scatter.27.cloned.1.call-update) | async-done | bytes 1228816 | tf_op jit(solution)/shard_map/reduce_scatter | solution.py:429
  1103.1 8.4 fusion.222
  1118.5 11.5 all-reduce.4
  1130.1 14.7 %all-reduce.2 = (bf16[240]{0:T(256)(128)(2,1)S(1)}, bf16[240]{0:T(256)(128)(2,1)S(1)}) all-reduce(bf16[240]{0:T(256)(128)(2,1)S(1)} %dynamic-slice.5, bf16[240]{0:T(256)(128)(2,1)S(1)} %dynamic-slice.7), channel_id=1, replica_groups=mesh['section'=2,'dp'=4,'ctx'=4] {'section','ctx'}, use_global_device_ids=true, to_apply=%region_58.59 | all-reduce | flops 480 | bytes 1920 | tf_op jit(solution)/shard_map/psum | solution.py:440
  1149.3 51.2 %all-reduce.7.cloned.1.call-done = (bf16[240,320]{1,0:T(8,128)(2,1)}, bf16[240,320]{1,0:T(8,128)(2,1)}, bf16[240,960]{1,0:T(8,128)(2,1)}, bf16[240,960]{1,0:T(8,...) async-done(((bf16[240,320]{1,0:T(8,128)(2,1)}, bf16[240,320]{1,0:T(8,128)(2,1)}, bf16[240,960]{1,0:T(8,128)(2,1)}, ...) | async-done | bytes 4915216 | tf_op jit(solution)/shard_map/psum | solution.py:442
  (944 shorter events, 589.2 us)
Async XLA Ops:
  7.2 77.9 %copy-start = (bf16[960,960]{1,0:T(8,128)(2,1)S(1)}, bf16[960,960]{1,0:T(8,128)(2,1)}, u32[]{:S(2)}) copy-start(bf16[960,960]{1,0:T(8,128)(2,1)} %param.37) | copy-start | bytes 5529604
  7.2 44.6 %all-gather.7.cloned.1.call-start = ((), (), s32[]{:S(2)}) async-start(), calls=%async_computation.10 | async-start | bytes 1638400 | tf_op jit(solution)/shard_map/all_gather | solution.py:129
  9.3 182.7 %copy-start.136 = (f32[960]{0:T(1024)}, f32[960]{0:T(1024)S(1)}, u32[]{:S(2)}) copy-start(f32[960]{0:T(1024)S(1)} %convert_element_type.724) | copy-start | bytes 11524
  17.0 182.5 %copy-start.64 = (f32[256,32]{0,1:T(8,128)}, f32[256,32]{0,1:T(8,128)S(1)}, u32[]{:S(2)}) copy-start(f32[256,32]{0,1:T(8,128)S(1)} %get-tuple-element.2450) | copy-start | bytes 98308
  17.0 182.5 %copy-start.80 = (f32[256,32]{0,1:T(8,128)}, f32[256,32]{0,1:T(8,128)S(1)}, u32[]{:S(2)}) copy-start(f32[256,32]{0,1:T(8,128)S(1)} %get-tuple-element.2449) | copy-start | bytes 98308
  20.1 118.6 %all-gather.9.cloned.1.call-start = ((), (), s32[]{:S(2)}) async-start(), calls=%async_computation.11 | async-start | bytes 1638400 | tf_op jit(solution)/shard_map/all_gather | solution.py:129
  24.0 251.5 %copy-start.98 = (f32[960]{0:T(1024)}, f32[960]{0:T(1024)S(1)}, u32[]{:S(2)}) copy-start(f32[960]{0:T(1024)S(1)} %convert_element_type.733) | copy-start | bytes 11524
  102.5 3.4 collective-permute-start
  109.7 116.5 %all-gather.13.cloned.1.call-start = ((), (), s32[]{:S(2)}) async-start(), calls=%async_computation.13 | async-start | bytes 1638400 | tf_op jit(solution)/shard_map/all_gather | solution.py:129
  188.6 3.4 collective-permute-start.1
  197.2 150.3 %reduce-scatter.13.cloned.1.call-start = ((), (), s32[]{:S(2)}) async-start(), calls=%async_computation.14 | async-start | bytes 1638400 | tf_op jit(solution)/shard_map/reduce_scatter | solution.py:341
  228.6 31.8 %copy-start.61 = (bf16[1,256,960]{1,2,0:T(8,128)(2,1)S(1)}, bf16[1,256,960]{1,2,0:T(8,128)(2,1)}, u32[]{:S(2)}) copy-start(bf16[1,256,960]{1,2,0:T(8,128)(2,1)} %copy-done.60) | copy-start | bytes 1474564
  318.1 78.8 %all-gather.15.cloned.1.call-start = ((), (), s32[]{:S(2)}) async-start(), calls=%async_computation.15 | async-start | bytes 1638400 | tf_op jit(solution)/shard_map/all_gather | solution.py:129
  318.7 34.3 %copy-start.148 = (f32[256]{0:T(256)}, f32[256]{0:T(256)S(1)}, u32[]{:S(2)}) copy-start(f32[256]{0:T(256)S(1)} %get-tuple-element.2456) | copy-start | bytes 3076
  319.7 29.0 %copy-start.153 = (f32[256]{0:T(256)S(1)}, f32[256]{0:T(256)}, u32[]{:S(2)}) copy-start(f32[256]{0:T(256)} %copy-done.152) | copy-start | bytes 3076
  367.9 81.4 %all-gather.17.cloned.1.call-start = ((), (), s32[]{:S(2)}) async-start(), calls=%async_computation.17 | async-start | bytes 1638400 | tf_op jit(solution)/shard_map/all_gather | solution.py:129
  370.5 68.4 %collective-permute-start.2 = (bf16[1,256,960]{1,2,0:T(8,128)(2,1)}, bf16[1,256,960]{1,2,0:T(8,128)(2,1)}, u32[]{:S(2)}, u32[]{:S(2)}) collective-permute-start(bf16[1,256,960]{1,2,0:T(8,128)(2,1)} %get-tuple-element.2405), channel_id=1, source_target_pairs={{16,0},{17,1},{18,2},{19,3},{20,4},{21,5},{22,6},{23,7},{24,8},{25... | collective-permute-start | bytes 1474568 | tf_op jit(solution)/shard_map/ppermute | solution.py:21
  382.4 177.8 %reduce-scatter.15.cloned.1.call-start = ((), (), s32[]{:S(2)}) async-start(), calls=%async_computation.16 | async-start | bytes 1638400 | tf_op jit(solution)/shard_map/reduce_scatter | solution.py:341
  530.8 146.9 %reduce-scatter.17.cloned.1.call-start = ((), (), s32[]{:S(2)}) async-start(), calls=%async_computation.18 | async-start | bytes 1638400 | tf_op jit(solution)/shard_map/reduce_scatter | solution.py:341
  566.1 6.3 collective-permute-start.3
  626.4 95.7 %all-gather.11.cloned.1.call-start = ((), (), s32[]{:S(2)}) async-start(), calls=%async_computation.12 | async-start | bytes 1638400 | tf_op jit(solution)/shard_map/all_gather | solution.py:129
  636.5 147.3 %reduce-scatter.31.cloned.1.call-start = ((), (), s32[]{:S(2)}) async-start(), calls=%async_computation.25 | async-start | bytes 6553600
  659.2 169.6 %reduce-scatter.25.cloned.1.call-start = ((), (), s32[]{:S(2)}) async-start(), calls=%async_computation.22 | async-start | bytes 2457600 | tf_op jit(solution)/shard_map/reduce_scatter | solution.py:423
  665.6 206.6 %reduce-scatter.19.cloned.1.call-start = ((), (), s32[]{:S(2)}) async-start(), calls=%async_computation.19 | async-start | bytes 2457600 | tf_op jit(solution)/shard_map/reduce_scatter | solution.py:414
  671.5 225.8 %reduce-scatter.21.cloned.1.call-start = ((), (), s32[]{:S(2)}) async-start(), calls=%async_computation.20 | async-start | bytes 921600 | tf_op jit(solution)/shard_map/reduce_scatter | solution.py:417
  683.1 238.9 %reduce-scatter.23.cloned.1.call-start = ((), (), s32[]{:S(2)}) async-start(), calls=%async_computation.21 | async-start | bytes 921600 | tf_op jit(solution)/shard_map/reduce_scatter | solution.py:420
  689.9 321.9 %reduce-scatter.29.cloned.1.call-start = ((), (), s32[]{:S(2)}) async-start(), calls=%async_computation.24 | async-start | bytes 6144000 | tf_op jit(solution)/shard_map/reduce_scatter | solution.py:432
  704.1 398.9 %reduce-scatter.27.cloned.1.call-start = ((), (), s32[]{:S(2)}) async-start(), calls=%async_computation.23 | async-start | bytes 6144000 | tf_op jit(solution)/shard_map/reduce_scatter | solution.py:429
  718.6 481.8 %all-reduce.7.cloned.1.call-start = ((), (), s32[]{:S(2)}) async-start(), calls=%async_computation.26 | async-start | bytes 10076160 | tf_op jit(solution)/shard_map/psum | solution.py:442
  763.1 340.0 %copy-start.128 = (bf16[1,256,960]{1,2,0:T(8,128)(2,1)S(1)}, bf16[1,256,960]{1,2,0:T(8,128)(2,1)}, u32[]{:S(2)}) copy-start(bf16[1,256,960]{1,2,0:T(8,128)(2,1)} %copy-done.127) | copy-start | bytes 1474564
  1113.9 32.1 %copy-start.30 = (f32[1,256,960]{1,2,0:T(8,128)S(1)}, f32[1,256,960]{1,2,0:T(8,128)}, u32[]{:S(2)}) copy-start(f32[1,256,960]{1,2,0:T(8,128)} %copy-done.28) | copy-start | bytes 2949124
  1113.9 32.1 %copy-start.158 = (f32[256]{0:T(256)S(1)}, f32[256]{0:T(256)}, u32[]{:S(2)}) copy-start(f32[256]{0:T(256)} %get-tuple-element.2451) | copy-start | bytes 3076
  (208 other events, 1053.7 us)
Sparse Core Ops, SparseCore 0:
  20.2 31.4 all-gather.6
  109.8 28.8 all-gather.8
  197.3 28.8 all-gather.12
  318.2 29.2 reduce-scatter.12
  368.1 28.7 all-gather.14
  399.2 28.7 all-gather.16
  530.9 29.3 reduce-scatter.14
  626.5 30.1 reduce-scatter.16
  659.1 28.7 all-gather.10
  690.1 93.7 reduce-scatter.30
  786.8 41.9 reduce-scatter.24
  831.5 40.6 reduce-scatter.18
  875.1 22.1 reduce-scatter.20
  900.0 21.9 reduce-scatter.22
  924.2 87.5 reduce-scatter.28
  1014.0 88.9 reduce-scatter.26
  1107.8 92.6 all-reduce.6
where the time goes:
time: 1230 us; the launch traced here: 1220 us
  waiting for transfers between devices  525 us (43%)
  matrix products  420 us (34%)
  other arithmetic  117 us (10%)
  local copies, waits for them, and re-layouts  99.3 us (8%)
  blocking collectives  26.2 us (2%)
  between operations  17.8 us (1%)
    reduce_scatter x1, waiting for transfers between devices, body(): lax.psum_scatter(sum_gate.astype(jnp.bfloat16), 'dp', scatter_dimension=0...  91.3 us
    reduce_scatter x1, waiting for transfers between devices, body(): lax.psum_scatter(sum_up.astype(jnp.bfloat16), 'dp', scatter_dimension=0,...  89.8 us
    all_gather x6, waiting for transfers between devices, attend_forward(): arrived = lax.all_gather(packed, 'ctx', axis=1, tiled=True)  89.5 us
    dot_general x12, matrix products, fold_inner_step(): jnp.einsum('rkgcn,rnkd->rkgcd', weights.astype(jnp.bfloat16), value_part,...  78.4 us
    dot_general x18, matrix products, block_scores(): jnp.einsum('rckgd,rnkd->rkgcn', queries, key_part, preferred_element_type...  67.5 us
    psum x1, waiting for transfers between devices, body(): lax.psum(shares[2].astype(jnp.bfloat16), ('section', 'ctx'))  51.2 us
    reduce_scatter x3, waiting for transfers between devices, body(): lax.psum_scatter(grad_pair.astype(jnp.bfloat16), 'ctx', scatter_dimension...  44.8 us
    reduce_scatter x1, waiting for transfers between devices, body(): lax.psum_scatter(sum_query.astype(jnp.bfloat16), 'dp', scatter_dimension=...  43.4 us
  transfers between devices with their start and end apart: 21, of which 16 were waited for; matrix products, arithmetic and copies ran while one was open for 20% of the time, Pallas kernels for 0%

commit v1 on v0

--- a/solution.py
+++ b/solution.py
@@ -13,12 +13,6 @@
 epsilon = 1e-05
 score_scale = 0.125
 mask_floor = -1e30
-
-
-def shifted(x, axis, by):
-    count = lax.axis_size(axis)
-    pairs = [(i, i + by) for i in range(count) if 0 <= i + by < count]
-    return lax.ppermute(x, axis, pairs)
 
 
 def rms_forward(values, gain_vec):
@@ -58,12 +52,6 @@
         key_pos[None, None, :] <= query_pos[None, :, None]
     )
     return (scores, allowed[:, None, None, :, :])
-
-
-def select_by(flag, former_val, latter_val):
-    return jax.tree.map(
-        lambda left_val, right_val: jnp.where(flag, left_val, right_val), former_val, latter_val
-    )
 
 
 def body(
@@ -85,7 +73,6 @@
     group_size = HEADS // KV_HEADS
     section_index = lax.axis_index("section")
     on_first = section_index == 0
-    on_last = section_index == 1
     ctx_index = lax.axis_index("ctx")
     first_token = ctx_index * tok_local
     query_pos = first_token + jnp.arange(tok_local, dtype=jnp.int32)
@@ -120,13 +107,12 @@
         )
         return (query_seg, inverse, normed_low, queries, packed.astype(jnp.bfloat16))
 
-    def attend_forward(queries, packed, segments, query_seg):
+    def attend_forward(queries, arrived, segments, query_seg):
         start_state = (
             jnp.full(state_shape, mask_floor, jnp.float32),
             jnp.zeros(state_shape, jnp.float32),
             jnp.zeros(state_shape + (HEAD_DIM,), jnp.float32),
         )
-        arrived = lax.all_gather(packed, "ctx", axis=1, tiled=True)
         piece_rows = arrived.shape[1]
         block_rows = math.gcd(piece_rows, 512)
 
@@ -177,66 +163,35 @@
         )
         return (output, (attn_low, middle, inverse_ffn, ffn_low, gate_pre, upward, inner_act))
 
-    tick_inputs = []
-    tick_outputs = []
-    tick_stash = []
-    incoming = jnp.zeros((row_count, tok_local, model_width), jnp.bfloat16)
-    for moment in range(micro_count + 1):
-        early_index = min(moment, micro_count - 1)
-        late_index = max(moment - 1, 0)
-        hidden = jnp.where(on_first, inputs[early_index], incoming).astype(jnp.float32)
-        segments = jnp.where(on_first, segment_ids[early_index], segment_ids[late_index])
-        forward_query_seg, forward_inverse, forward_normed_low, forward_queries, forward_packed = (
-            front(hidden, segments)
-        )
-        forward_attended, forward_log_sum = attend_forward(
-            forward_queries, forward_packed, segments, forward_query_seg
-        )
-        forward_output, forward_saved = rear(hidden, forward_attended)
-        output = forward_output
-        stash = (forward_attended, forward_log_sum)
-        output_low = output.astype(jnp.bfloat16)
-        tick_inputs.append(hidden)
-        tick_outputs.append(output_low)
-        tick_stash.append(stash)
-        if moment < micro_count:
-            incoming = shifted(output_low, "section", 1)
-    kept_inputs = [
-        select_by(on_first, tick_inputs[number], tick_inputs[number + 1])
-        for number in range(micro_count)
-    ]
-    kept_stash = [
-        select_by(on_first, tick_stash[number], tick_stash[number + 1])
-        for number in range(micro_count)
-    ]
-    act_list = [
-        select_by(on_first, tick_outputs[number], tick_outputs[number + 1])
-        for number in range(micro_count)
-    ]
-    grad_sums = None
-    grad_list = []
-    incoming_grad = jnp.zeros((row_count, tok_local, model_width), jnp.bfloat16)
-    for moment in range(micro_count + 1):
-        early_index = min(moment, micro_count - 1)
-        late_index = max(moment - 1, 0)
-        hidden = select_by(on_last, kept_inputs[early_index], kept_inputs[late_index])
-        segments = jnp.where(on_last, segment_ids[early_index], segment_ids[late_index])
-        stash = select_by(on_last, kept_stash[early_index], kept_stash[late_index])
-        grad_out = jnp.where(
-            on_last, cotangent[early_index].astype(jnp.float32), incoming_grad.astype(jnp.float32)
-        )
-        tick_valid = jnp.where(on_last, float(moment < micro_count), float(moment >= 1))
+
+    assert micro_count == lax.axis_size("section")
+
+    def mine(stacked):
+        return lax.dynamic_index_in_dim(stacked, section_index, 0, keepdims=False)
+
+    segments = mine(segment_ids)
+
+    def forward(hidden):
+        query_seg, inverse, normed_low, queries, packed = front(hidden, segments)
+        arrived = lax.all_gather(packed, "ctx", axis=1, tiled=True)
+        attended, log_sum = attend_forward(queries, arrived, segments, query_seg)
+        output, saved = rear(hidden, attended)
+        return output.astype(jnp.bfloat16), (
+            hidden, query_seg, inverse, normed_low, queries, arrived, attended, log_sum, saved
+        )
+
+    def backward(grad_out, kept):
         (
+            hidden,
             backward_query_seg,
             backward_inverse,
             backward_normed_low,
             backward_queries,
-            backward_packed,
-        ) = front(hidden, segments)
-        backward_attended, log_sum = attend_forward(
-            backward_queries, backward_packed, segments, backward_query_seg
-        )
-        backward_output, saved = rear(hidden, backward_attended)
+            piece_arrived,
+            backward_attended,
+            log_sum,
+            saved,
+        ) = kept
         (
             backward_attn_low,
             backward_middle,
@@ -280,7 +235,6 @@
         row_delta = jnp.sum(grad_heads.astype(jnp.float32) * backward_attended, -1)
         query_start = jnp.zeros(state_shape + (HEAD_DIM,), jnp.float32)
         fold_grad_query = query_start
-        piece_arrived = lax.all_gather(backward_packed, "ctx", axis=1, tiled=True)
         grad_query = fold_grad_query
         piece_piece_rows = piece_arrived.shape[1]
         piece_block_rows = math.gcd(piece_piece_rows, 512)
@@ -380,22 +334,21 @@
             backward_sum_up,
             backward_sum_down,
         )
-        grad_hidden, tick_grads = (grad_middle + grad_front, tick_grads)
-        tick_grads = tuple((tick_valid * member for member in tick_grads))
-        if grad_sums is None:
-            grad_sums = tick_grads
-        else:
-            grad_sums = tuple(
-                (accumulated + addition for accumulated, addition in zip(grad_sums, tick_grads))
-            )
-        grad_low = grad_hidden.astype(jnp.bfloat16)
-        grad_list.append((grad_hidden, grad_low.astype(jnp.float32)))
-        if moment < micro_count:
-            incoming_grad = shifted(grad_low, "section", -1)
-    grad_rows = [
-        jnp.where(on_last, grad_list[number][1], grad_list[number + 1][0])
-        for number in range(micro_count)
-    ]
+        return grad_middle + grad_front, tick_grads
+
+    def exchange(for_first, for_last):
+        kept = jnp.where(on_first, for_first, for_last)
+        sent = jnp.where(on_first, for_last, for_first)
+        got = lax.ppermute(sent, "section", [(0, 1), (1, 0)])
+        return jnp.where(
+            on_first, jnp.stack([kept, got]), jnp.stack([got, kept])
+        )
+
+    first_low, first_kept = forward(mine(inputs).astype(jnp.float32))
+    second_low, second_kept = forward(first_low.astype(jnp.float32))
+    grad_mid, second_grads = backward(mine(cotangent).astype(jnp.float32), second_kept)
+    grad_mid_low = grad_mid.astype(jnp.bfloat16)
+    grad_in, first_grads = backward(grad_mid_low.astype(jnp.float32), first_kept)
     (
         sum_gain_attn,
         sum_query,
@@ -406,7 +359,7 @@
         sum_gate,
         sum_up,
         sum_down,
-    ) = grad_sums
+    ) = tuple(one + other for one, other in zip(second_grads, first_grads))
     shares = (
         lax.psum_scatter(
             sum_gain_attn.astype(jnp.bfloat16), "dp", scatter_dimension=0, tiled=True
@@ -447,8 +400,8 @@
         lax.psum(shares[7].astype(jnp.bfloat16), ("section", "ctx")).astype(jnp.float32),
         lax.psum(shares[8].astype(jnp.bfloat16), ("section", "ctx")).astype(jnp.float32),
     )
-    activations = jnp.stack(act_list)[None]
-    input_grads = jnp.stack(grad_rows)[None]
+    activations = exchange(first_low, second_low)[None]
+    input_grads = exchange(grad_in.astype(jnp.bfloat16), grad_mid_low).astype(jnp.float32)[None]
     return (
         activations,
         input_grads,

time: 1230 us -> 892 us (0.73)
  matrix products: 420 us -> 188 us
  other arithmetic: 117 us -> 61 us
  local copies, waits for them, and re-layouts: 99.3 us -> 59 us
    dot_general x12 -> x4, matrix products: 78.4 us -> 14.7 us  [fold_inner_step(): jnp.einsum('rkgcn,rnkd->rkgcd', weights.astype(jnp.bfloat16), value_part,...]
    dot_general x36 -> x24, matrix products: 118 us -> 58 us  [the longest x2 9.74 us: backward(): jnp.einsum('rcd,fd->rcf', grad_low, w_down, preferred_element_type=jnp.fl...]
    unnamed x18 -> x13, waiting for transfers between devices: 21.1 us -> 75.2 us
    dot_general x18 -> x8, matrix products: 67.5 us -> 22.9 us  [block_scores(): jnp.einsum('rckgd,rnkd->rkgcn', queries, key_part, preferred_element_type...]
    all_gather x6 -> x2, waiting for transfers between devices: 89.5 us -> 51.4 us  [forward(): arrived = lax.all_gather(packed, 'ctx', axis=1, tiled=True)]
    dot_general x3 -> x2, matrix products: 25.5 us -> 6.15 us  [rear(): jnp.einsum('rcf,fd->rcd', inner_act, w_down, preferred_element_type=jnp.f...]
    reduce_scatter x3 -> x2, waiting for transfers between devices: 44.8 us -> 26.5 us  [backward(): lax.psum_scatter(grad_pair.astype(jnp.bfloat16), 'ctx', scatter_dimension...]
    dynamic_update_slice x6 -> x4, other arithmetic: 16.4 us -> 1.45 us  [piece_inner_step(): lax.dynamic_update_slice_in_dim(local_pair, current + update, inside, 1)]
  transfers between devices with their start and end apart: 21 -> 14, of which waited for: 16 -> 12; matrix products, arithmetic and copies ran while one was open for 20% -> 8% of each run, Pallas kernels for 0% -> 0%
where the time goes in v1:
time: 892 us; the launch traced here: 884 us
  waiting for transfers between devices  530 us (59%)
  matrix products  188 us (21%)
  other arithmetic  61 us (7%)
  local copies, waits for them, and re-layouts  59 us (7%)
  blocking collectives  26.5 us (3%)
  between operations  17.1 us (2%)
    reduce_scatter x1, waiting for transfers between devices, body(): lax.psum_scatter(sum_up.astype(jnp.bfloat16), 'dp', scatter_dimension=0,...  91.4 us
    reduce_scatter x1, waiting for transfers between devices, body(): lax.psum_scatter(sum_gate.astype(jnp.bfloat16), 'dp', scatter_dimension=0...  89.8 us
    unnamed x13, waiting for transfers between devices  75.2 us
    psum x1, waiting for transfers between devices, body(): lax.psum(shares[2].astype(jnp.bfloat16), ('section', 'ctx'))  59.3 us
    all_gather x2, waiting for transfers between devices, forward(): arrived = lax.all_gather(packed, 'ctx', axis=1, tiled=True)  51.4 us
    reduce_scatter x1, waiting for transfers between devices, body(): lax.psum_scatter(sum_out.astype(jnp.bfloat16), 'dp', scatter_dimension=0,...  43.6 us
    reduce_scatter x1, waiting for transfers between devices, body(): lax.psum_scatter(sum_query.astype(jnp.bfloat16), 'dp', scatter_dimension=...  42.4 us
    unnamed x215, local copies, waits for them, and re-layouts  29.7 us
  transfers between devices with their start and end apart: 14, of which 12 were waited for; matrix products, arithmetic and copies ran while one was open for 8% of the time, Pallas kernels for 0%

profile of v1, /device:TPU:0, one launch (start us, length us, event | category | flops | bytes accessed | tf_op | source)
XLA Modules:
  0.0 883.8 jit_solution(16112627605377466316)
XLA Ops:
  29.9 25.1 %all-gather.3.cloned.1.call-done = bf16[1,1024,640]{2,1,0:T(8,128)(2,1)} async-done(((bf16[1,256,640]{2,1,0:T(8,128)(2,1)}), bf16[1,1024,640]{2,1,0:T(8,128)(2,1)}) %all-gather.3.cloned.1.call-update) | async-done | bytes 1310736 | tf_op jit(solution)/shard_map/all_gather | solution.py:176
  57.4 30.3 %while.68 = (s32[]{:T(128)}, f32[1,5,3,256]{3,2,1,0:T(4,128)S(1)}, f32[1,5,3,256]{3,2,1,0:T(4,128)S(1)}, f32[1,5,3,256,64]{3,4,2,1,0:T(8,128)}, s32[1,256]{1,0:T...) while((s32[]{:T(128)}, f32[1,5,3,256]{3,2,1,0:T(4,128)S(1)}, ...), condition=%wide.region_4.5_spmd.clone, body=%wide.region_1.4_spmd.clone.sunk | while | flops 530029824 | bytes 60257536 | solution.py:142
  63.4 5.3 fusion.291
  77.8 5.3 fusion.291
  107.1 26.3 %all-gather.5.cloned.1.call-done = bf16[1,1024,640]{2,1,0:T(8,128)(2,1)} async-done(((bf16[1,256,640]{2,1,0:T(8,128)(2,1)}), bf16[1,1024,640]{2,1,0:T(8,128)(2,1)}) %all-gather.5.cloned.1.call-update) | async-done | bytes 1310736 | tf_op jit(solution)/shard_map/all_gather | solution.py:176
  136.0 30.1 %while.69 = (s32[]{:T(128)}, f32[1,5,3,256]{3,2,1,0:T(4,128)S(1)}, f32[1,5,3,256]{3,2,1,0:T(4,128)S(1)}, f32[1,5,3,256,64]{3,4,2,1,0:T(8,128)}, s32[1,256]{1,0:T...) while((s32[]{:T(128)}, f32[1,5,3,256]{3,2,1,0:T(4,128)S(1)}, ...), condition=%wide.region_10.11_spmd.clone, body=%wide.region_7.10_spmd.clone.sunk | while | flops 530029824 | bytes 60257536 | solution.py:142
  137.4 4.5 fusion.296
  142.0 5.3 fusion.298
  156.4 5.3 fusion.298
  168.7 5.1 fusion.164
  186.4 39.8 %while.70 = (s32[]{:T(128)}, f32[1,5,3,256,64]{3,4,2,1,0:T(8,128)}, f32[1,1024,640]{1,2,0:T(8,128)}, s32[1,256]{1,0:T(1,128)S(1)}, s32[1,1024]{1,0:T(1,128)S(1)}...) while((s32[]{:T(128)}, f32[1,5,3,256,64]{3,4,2,1,0:T(8,128)}, ...), condition=%wide.region_15.16_spmd.clone, body=%wide.region_14.15_spmd.clone.sunk | while | flops 1283834624 | bytes 115468640 | solution.py:290
  197.1 5.4 fusion.313
  217.2 5.4 fusion.313
  234.5 24.4 %reduce-scatter.12.cloned.1.call-done = bf16[1,256,640]{1,2,0:T(8,128)(2,1)} async-done(((bf16[1,1024,640]{1,2,0:T(8,128)(2,1)}), bf16[1,256,640]{1,2,0:T(8,128)(2,1)}) %reduce-scatter.12.cloned.1.call-update) | async-done | bytes 327696 | tf_op jit(solution)/shard_map/reduce_scatter | solution.py:295
  263.6 5.7 multiply_convert_fusion
  276.2 41.7 %while.71 = (s32[]{:T(128)}, f32[1,5,3,256,64]{3,4,2,1,0:T(8,128)}, f32[1,1024,640]{1,2,0:T(8,128)}, s32[1,256]{1,0:T(1,128)S(1)}, s32[1,1024]{1,0:T(1,128)S(1)}...) while((s32[]{:T(128)}, f32[1,5,3,256,64]{3,4,2,1,0:T(8,128)}, ...), condition=%wide.region_21.22_spmd.clone, body=%wide.region_20.21_spmd.clone.sunk | while | flops 1283834624 | bytes 119523808 | solution.py:290
  279.1 5.0 fusion.327
  288.0 5.5 fusion.329
  299.7 5.0 fusion.327
  308.9 5.5 fusion.329
  327.8 7.9 copy.106
  372.0 74.4 %reduce-scatter.28.cloned.1.call-done = bf16[640,960]{1,0:T(8,128)(2,1)} async-done(((bf16[2560,960]{1,0:T(8,128)(2,1)}), bf16[640,960]{1,0:T(8,128)(2,1)}) %reduce-scatter.28.cloned.1.call-update) | async-done | bytes 1228816
  448.8 42.4 %reduce-scatter.16.cloned.1.call-done = bf16[240,960]{1,0:T(8,128)(2,1)} async-done(((bf16[960,960]{1,0:T(8,128)(2,1)}), bf16[240,960]{1,0:T(8,128)(2,1)}) %reduce-scatter.16.cloned.1.call-update) | async-done | bytes 460816 | tf_op jit(solution)/shard_map/reduce_scatter | solution.py:367
  491.1 43.6 %reduce-scatter.22.cloned.1.call-done = bf16[240,960]{1,0:T(8,128)(2,1)} async-done(((bf16[960,960]{1,0:T(8,128)(2,1)}), bf16[240,960]{1,0:T(8,128)(2,1)}) %reduce-scatter.22.cloned.1.call-update) | async-done | bytes 460816 | tf_op jit(solution)/shard_map/reduce_scatter | solution.py:376
  534.7 25.1 %reduce-scatter.18.cloned.1.call-done = bf16[240,320]{1,0:T(8,128)(2,1)} async-done(((bf16[960,320]{1,0:T(8,128)(2,1)}), bf16[240,320]{1,0:T(8,128)(2,1)}) %reduce-scatter.18.cloned.1.call-update) | async-done | bytes 153616 | tf_op jit(solution)/shard_map/reduce_scatter | solution.py:370
  559.8 24.9 %reduce-scatter.20.cloned.1.call-done = bf16[240,320]{1,0:T(8,128)(2,1)} async-done(((bf16[960,320]{1,0:T(8,128)(2,1)}), bf16[240,320]{1,0:T(8,128)(2,1)}) %reduce-scatter.20.cloned.1.call-update) | async-done | bytes 153616 | tf_op jit(solution)/shard_map/reduce_scatter | solution.py:373
  584.7 89.8 %reduce-scatter.24.cloned.1.call-done = bf16[240,2560]{1,0:T(8,128)(2,1)} async-done(((bf16[960,2560]{1,0:T(8,128)(2,1)}), bf16[240,2560]{1,0:T(8,128)(2,1)}) %reduce-scatter.24.cloned.1.call-update) | async-done | bytes 1228816 | tf_op jit(solution)/shard_map/reduce_scatter | solution.py:382
  674.5 91.4 %reduce-scatter.26.cloned.1.call-done = bf16[240,2560]{1,0:T(8,128)(2,1)} async-done(((bf16[960,2560]{1,0:T(8,128)(2,1)}), bf16[240,2560]{1,0:T(8,128)(2,1)}) %reduce-scatter.26.cloned.1.call-update) | async-done | bytes 1228816 | tf_op jit(solution)/shard_map/reduce_scatter | solution.py:385
  765.9 4.7 select_bitcast_fusion.3
  775.0 11.0 %all-reduce.4 = (bf16[960]{0:T(1024)(128)(2,1)S(1)}, bf16[960]{0:T(1024)(128)(2,1)S(1)}) all-reduce(bf16[960]{0:T(1024)(128)(2,1)S(1)} %add_convert_fusion.13, bf16[960]{0:T(1024)(128)(2,1)S(1)} %add_convert_fusion.12), channel_id=4, replica_groups=mesh['section'=2,'dp'=4,'ctx'=4] {'dp'}, use_global_device_ids=true, to_apply=%region_26.27.clone | all-reduce | flops 1920 | bytes 7680
  786.1 15.5 %all-reduce.2 = (bf16[240]{0:T(256)(128)(2,1)S(1)}, bf16[240]{0:T(256)(128)(2,1)S(1)}) all-reduce(bf16[240]{0:T(256)(128)(2,1)S(1)} %dynamic-slice.3, bf16[240]{0:T(256)(128)(2,1)S(1)} %dynamic-slice.5), channel_id=1, replica_groups=mesh['section'=2,'dp'=4,'ctx'=4] {'section','ctx'}, use_global_device_ids=true, to_apply=%region_27.28 | all-reduce | flops 480 | bytes 1920 | tf_op jit(solution)/shard_map/psum | solution.py:393
  804.2 59.3 %all-reduce.7.cloned.1.call-done = (bf16[240,320]{1,0:T(8,128)(2,1)}, bf16[240,320]{1,0:T(8,128)(2,1)}, bf16[240,960]{1,0:T(8,128)(2,1)}, bf16[240,960]{1,0:T(8,...) async-done(((bf16[240,320]{1,0:T(8,128)(2,1)}, bf16[240,320]{1,0:T(8,128)(2,1)}, bf16[240,960]{1,0:T(8,128)(2,1)}, ...) | async-done | bytes 4915216 | tf_op jit(solution)/shard_map/psum | solution.py:395
  (500 shorter events, 231.9 us)
Async XLA Ops:
  7.2 82.1 %copy-start = (bf16[960,960]{1,0:T(8,128)(2,1)S(1)}, bf16[960,960]{1,0:T(8,128)(2,1)}, u32[]{:S(2)}) copy-start(bf16[960,960]{1,0:T(8,128)(2,1)} %param.27) | copy-start | bytes 5529604
  7.2 47.8 %all-gather.3.cloned.1.call-start = ((), (), s32[]{:S(2)}) async-start(), calls=%async_computation.9 | async-start | bytes 1638400 | tf_op jit(solution)/shard_map/all_gather | solution.py:176
  9.2 95.3 %copy-start.82 = (f32[960]{0:T(1024)}, f32[960]{0:T(1024)S(1)}, u32[]{:S(2)}) copy-start(f32[960]{0:T(1024)S(1)} %convert_element_type.402) | copy-start | bytes 11524
  11.0 16.4 %copy-start.86 = (f32[256]{0:T(256)}, f32[256]{0:T(256)S(1)}, u32[]{:S(2)}) copy-start(f32[256]{0:T(256)S(1)} %get-tuple-element.1150) | copy-start | bytes 3076
  12.1 8.3 copy-start.27
  18.6 88.2 %copy-start.44 = (f32[256,32]{0,1:T(8,128)}, f32[256,32]{0,1:T(8,128)S(1)}, u32[]{:S(2)}) copy-start(f32[256,32]{0,1:T(8,128)S(1)} %get-tuple-element.1148) | copy-start | bytes 98308
  23.3 110.0 %all-gather.5.cloned.1.call-start = ((), (), s32[]{:S(2)}) async-start(), calls=%async_computation.10 | async-start | bytes 1638400 | tf_op jit(solution)/shard_map/all_gather | solution.py:176
  91.5 8.5 copy-start.40
  92.4 7.6 slice-start.10
  101.5 66.0 %copy-start.31 = (bf16[256,960]{0,1:T(8,128)(2,1)}, bf16[256,960]{0,1:T(8,128)(2,1)S(1)}, u32[]{:S(2)}) copy-start(bf16[256,960]{0,1:T(8,128)(2,1)S(1)} %get-tuple-element.1162) | copy-start | bytes 1474564
  104.4 154.5 %reduce-scatter.12.cloned.1.call-start = ((), (), s32[]{:S(2)}) async-start(), calls=%async_computation.11 | async-start | bytes 1638400 | tf_op jit(solution)/shard_map/reduce_scatter | solution.py:295
  167.5 7.9 slice-start.12
  168.4 14.8 %copy-start.39 = (f32[256,960]{0,1:T(8,128)}, f32[256,960]{0,1:T(8,128)S(1)}, u32[]{:S(2)}) copy-start(f32[256,960]{0,1:T(8,128)S(1)} %get-tuple-element.1164) | copy-start | bytes 2949124
  229.4 121.1 %reduce-scatter.14.cloned.1.call-start = ((), (), s32[]{:S(2)}) async-start(), calls=%async_computation.12 | async-start | bytes 1638400 | tf_op jit(solution)/shard_map/reduce_scatter | solution.py:295
  231.3 28.8 %copy-start.29 = (bf16[960,640]{0,1:T(8,128)(2,1)S(1)}, bf16[960,640]{0,1:T(8,128)(2,1)}, u32[]{:S(2)}) copy-start(bf16[960,640]{0,1:T(8,128)(2,1)} %copy-done.27) | copy-start | bytes 3686404
  231.3 28.8 %copy-start.83 = (f32[960]{0:T(1024)S(1)}, f32[960]{0:T(1024)}, u32[]{:S(2)}) copy-start(f32[960]{0:T(1024)} %copy-done.82) | copy-start | bytes 11524
  231.3 28.9 %copy-start.85 = (f32[256]{0:T(256)S(1)}, f32[256]{0:T(256)}, u32[]{:S(2)}) copy-start(f32[256]{0:T(256)} %copy-done.84) | copy-start | bytes 3076
  260.1 9.2 %slice-start.2 = ((s8[4915200]{0:T(1024)(128)(4,1)}), s8[4194304]{0:T(1024)(128)(4,1)S(1)}, s32[]{:S(2)}) async-start(s8[4915200]{0:T(1024)(128)(4,1)} %bitcast.626), calls=%async_computation.23 | async-start | bytes 8388608
  260.1 10.7 %slice-start.8 = ((s8[4915200]{0:T(1024)(128)(4,1)}), s8[4194304]{0:T(1024)(128)(4,1)S(1)}, s32[]{:S(2)}) async-start(s8[4915200]{0:T(1024)(128)(4,1)} %bitcast.638), calls=%async_computation.29 | async-start | bytes 8388608
  263.5 60.5 %copy-start.21 = (bf16[256,960]{0,1:T(8,128)(2,1)}, bf16[256,960]{0,1:T(8,128)(2,1)S(1)}, u32[]{:S(2)}) copy-start(bf16[256,960]{0,1:T(8,128)(2,1)S(1)} %fusion.117) | copy-start | bytes 1474564
  321.0 125.4 %reduce-scatter.28.cloned.1.call-start = ((), (), s32[]{:S(2)}) async-start(), calls=%async_computation.19 | async-start | bytes 6553600
  335.7 155.4 %reduce-scatter.16.cloned.1.call-start = ((), (), s32[]{:S(2)}) async-start(), calls=%async_computation.13 | async-start | bytes 2457600 | tf_op jit(solution)/shard_map/reduce_scatter | solution.py:367
  340.9 193.8 %reduce-scatter.22.cloned.1.call-start = ((), (), s32[]{:S(2)}) async-start(), calls=%async_computation.16 | async-start | bytes 2457600 | tf_op jit(solution)/shard_map/reduce_scatter | solution.py:376
  345.2 214.5 %reduce-scatter.18.cloned.1.call-start = ((), (), s32[]{:S(2)}) async-start(), calls=%async_computation.14 | async-start | bytes 921600 | tf_op jit(solution)/shard_map/reduce_scatter | solution.py:370
  356.1 228.6 %reduce-scatter.20.cloned.1.call-start = ((), (), s32[]{:S(2)}) async-start(), calls=%async_computation.15 | async-start | bytes 921600 | tf_op jit(solution)/shard_map/reduce_scatter | solution.py:373
  356.8 317.6 %reduce-scatter.24.cloned.1.call-start = ((), (), s32[]{:S(2)}) async-start(), calls=%async_computation.17 | async-start | bytes 6144000 | tf_op jit(solution)/shard_map/reduce_scatter | solution.py:382
  363.5 402.3 %reduce-scatter.26.cloned.1.call-start = ((), (), s32[]{:S(2)}) async-start(), calls=%async_computation.18 | async-start | bytes 6144000 | tf_op jit(solution)/shard_map/reduce_scatter | solution.py:385
  370.1 493.4 %all-reduce.7.cloned.1.call-start = ((), (), s32[]{:S(2)}) async-start(), calls=%async_computation.20 | async-start | bytes 10076160 | tf_op jit(solution)/shard_map/psum | solution.py:395
  448.8 317.1 %copy-start.35 = (bf16[256,960]{0,1:T(8,128)(2,1)S(1)}, bf16[256,960]{0,1:T(8,128)(2,1)}, u32[]{:S(2)}) copy-start(bf16[256,960]{0,1:T(8,128)(2,1)} %copy-done.31) | copy-start | bytes 1474564
  770.6 3.2 collective-permute-start
  773.8 29.0 %collective-permute-start.1 = (bf16[1,256,960]{1,2,0:T(8,128)(2,1)S(1)}, bf16[1,256,960]{1,2,0:T(8,128)(2,1)S(1)}, u32[]{:S(2)}, u32[]{:S(2)}) collective-permute-start(bf16[1,256,960]{1,2,0:T(8,128)(2,1)S(1)} %select_bitcast_fusion), channel_id=1, source_target_pairs={{0,16},{16,0},{1,17},{17,1},{2,18},{18,2},{3,19},{19,3},{4,20},{20... | collective-permute-start | bytes 1474568 | tf_op jit(solution)/shard_map/ppermute | solution.py:342
  863.5 7.9 copy-start.79
  (112 other events, 351.7 us)
Sparse Core Ops, SparseCore 0:
  23.5 31.4 all-gather.2
  104.5 28.7 all-gather.4
  229.5 29.3 reduce-scatter.11
  321.1 29.3 reduce-scatter.13
  352.6 93.7 reduce-scatter.27
  449.1 41.9 reduce-scatter.15
  494.0 40.6 reduce-scatter.21
  537.6 22.1 reduce-scatter.17
  562.6 21.9 reduce-scatter.19
  586.8 87.5 reduce-scatter.23
  676.9 88.9 reduce-scatter.25
  770.6 92.8 all-reduce.6

commit v2 on v1

--- a/solution.py
+++ b/solution.py
@@ -1,13 +1,18 @@
+import functools
 import math
 
 import jax
 import jax.numpy as jnp
 from jax import lax
+from jax.experimental import pallas as pl
+from jax.experimental.pallas import tpu as pltpu
 from jax.sharding import PartitionSpec as P
 
 HEADS = 15
 KV_HEADS = 5
 HEAD_DIM = 64
+LANES = 128
+MESH = pl.DeviceIdType.MESH
 
 
 epsilon = 1e-05
@@ -52,6 +57,315 @@
         key_pos[None, None, :] <= query_pos[None, :, None]
     )
     return (scores, allowed[:, None, None, :, :])
+
+
+def up_to(value, step):
+    return -(-value // step) * step
+
+
+class Plan:
+    def __init__(self, dp, ctx, width, hidden, kv_width):
+        self.dp, self.ctx = dp, ctx
+        self.cx = 1 << (ctx.bit_length() // 2) if ctx & (ctx - 1) == 0 else ctx
+        self.cy = ctx // self.cx
+        self.low = max(dp // 2, 1)
+        self.rows = up_to(width // dp, 16)
+        self.down_rows = up_to(hidden // dp // 2, 16)
+        self.up_tiles = hidden // LANES
+        self.width_tiles = up_to(width, LANES) // LANES
+        self.pair_tiles = (width + kv_width) // LANES
+        chunks = []
+        for kind, count, rows, step in (
+            ("ffn", self.up_tiles, self.rows, 4),
+            ("down", self.width_tiles, self.down_rows, 4),
+            ("attn", self.width_tiles - 1, self.rows, 4),
+            ("mixed", self.pair_tiles - self.width_tiles + 1, self.rows, 4),
+        ):
+            for start in range(0, count, step):
+                tiles = min(step, count - start)
+                extra = 16 if kind == "mixed" else 0
+                piece = up_to(up_to(tiles * rows + extra, ctx) // ctx, 16)
+                chunks.append((kind, start, tiles, rows, piece))
+        self.chunks = chunks
+        self.offsets = [sum(c[4] for c in chunks[:i]) for i in range(len(chunks))]
+        self.total = sum(c[4] for c in chunks)
+
+    def spans(self, index, first, count):
+        piece = self.chunks[index][4]
+        out, done = [], 0
+        while done < count:
+            at = first + done
+            size = min(count - done, piece - at % piece)
+            out.append((at // piece, self.offsets[index] + at % piece, done, size))
+            done += size
+        return out
+
+
+def reduce_kernel(
+    plan, ffn_x, ffn_dy, down_x, down_dy, attn_x, attn_dy, pair_dy, extra, out,
+    sent, partner, own, rx1, ry1, rx2, ry2, rz,
+    sem_ps, sem_pr, sem_x1, sem_y1, sem_x2, sem_y2, sem_z, sem_g, sem_f,
+):
+    dp, cx, cy, low = plan.dp, plan.cx, plan.cy, plan.low
+    section, row, ctx = (lax.axis_index(name) for name in ("section", "dp", "ctx"))
+    px, py = lax.rem(ctx, cx), lax.div(ctx, cx)
+    mate = 1 - section
+    chunks, count = plan.chunks, len(plan.chunks)
+
+    def at(index):
+        return pl.ds(plan.offsets[index], chunks[index][4])
+
+    def turn(base, step, size):
+        return lax.rem(base + step, size)
+
+    barrier = pltpu.get_barrier_semaphore()
+    friends = [(mate, row, ctx)]
+    friends += [(section, turn(row, k, dp), ctx) for k in range(1, dp)]
+    friends += [(section, row, turn(ctx, k, plan.ctx)) for k in range(1, plan.ctx)]
+    for friend in friends:
+        pl.semaphore_signal(barrier, 1, device_id=friend, device_id_type=MESH)
+    pl.semaphore_wait(barrier, len(friends))
+
+    def remote(source, target, sems, place, device):
+        return pltpu.make_async_remote_copy(
+            source, target, sems[0].at[place], sems[1].at[place], device_id=device, device_id_type=MESH
+        )
+
+    def products(index, half, finish):
+        kind, start, tiles, rows, piece = chunks[index]
+
+        def shard(j, carry):
+            if kind == "ffn":
+                value = jnp.dot(
+                    ffn_x[j], ffn_dy[half, :, start * LANES : (start + tiles) * LANES],
+                    preferred_element_type=jnp.float32,
+                )
+            elif kind == "down":
+                value = jnp.dot(
+                    down_x[half, j], down_dy[:, start * LANES : (start + tiles) * LANES],
+                    preferred_element_type=jnp.float32,
+                )
+            elif kind == "attn":
+                value = jnp.dot(
+                    attn_x[half, j], attn_dy[half, :, start * LANES : (start + tiles) * LANES],
+                    preferred_element_type=jnp.float32,
+                )
+            else:
+                value = jnp.dot(
+                    attn_x[0, j], pair_dy[half], preferred_element_type=jnp.float32
+                )
+                last = plan.width_tiles - 1
+                mixed = jnp.dot(
+                    attn_x[half, j], attn_dy[half, :, last * LANES :], preferred_element_type=jnp.float32
+                )
+                value = jnp.concatenate([value[:, :LANES] + mixed, value[:, LANES:]], 1)
+            for tile in range(tiles):
+                finish(j, tile * rows, value[:, tile * LANES : (tile + 1) * LANES])
+            if kind == "mixed":
+                finish(j, tiles * rows, extra[half, j])
+            return carry
+
+        lax.fori_loop(0, dp, shard, 0)
+
+    def make_partner(index):
+        if index >= 2:
+            send_partner(index - 2).wait_send()
+        slot = index % 2
+        base = plan.offsets[index]
+
+        def finish(j, first, value):
+            for p, place, inside, size in plan.spans(index, first, value.shape[0]):
+                sent[slot, j, p, place - base : place - base + size, :] = value[
+                    inside : inside + size
+                ].astype(jnp.bfloat16)
+
+        products(index, mate, finish)
+        send_partner(index).start()
+
+    def send_partner(index):
+        piece = chunks[index][4]
+        return remote(
+            sent.at[index % 2, :, :, pl.ds(0, piece)], partner.at[:, :, at(index)],
+            (sem_ps, sem_pr), index, (mate, row, ctx),
+        )
+
+    def make_own(index):
+        send_partner(index).wait_recv()
+
+        def finish(j, first, value):
+            for p, place, inside, size in plan.spans(index, first, value.shape[0]):
+                rows = pl.ds(place, size)
+                own[j, p // cx, p % cx, rows, :] = (
+                    value[inside : inside + size] + partner[j, p, rows, :].astype(jnp.float32)
+                ).astype(jnp.bfloat16)
+
+        products(index, section, finish)
+        for copy in first_copies(index):
+            copy.start()
+
+    def first_copies(index):
+        rows, copies = at(index), []
+        for k in range(1, cx):
+            other = turn(px, k, cx)
+            copies.append(remote(
+                own.at[pl.ds(0, low), :, other, rows], rx1.at[k - 1, :, :, rows],
+                (sem_x1.at[0], sem_x1.at[1]), (index, k - 1), (section, row, py * cx + other),
+            ))
+        if dp > low:
+            for k in range(1, cy):
+                other = turn(py, k, cy)
+                copies.append(remote(
+                    own.at[pl.ds(low, dp - low), other, :, rows], ry1.at[k - 1, :, :, rows],
+                    (sem_y1.at[0], sem_y1.at[1]), (index, k - 1), (section, row, other * cx + px),
+                ))
+        return copies
+
+    def second_copies(index):
+        rows, copies = at(index), []
+        for k in range(1, cy):
+            other = turn(py, k, cy)
+            copies.append(remote(
+                own.at[pl.ds(0, low), other, px, rows], ry2.at[k - 1, :, rows],
+                (sem_y2.at[0], sem_y2.at[1]), (index, k - 1), (section, row, other * cx + px),
+            ))
+        if dp > low:
+            for k in range(1, cx):
+                other = turn(px, k, cx)
+                copies.append(remote(
+                    own.at[pl.ds(low, dp - low), py, other, rows], rx2.at[k - 1, :, rows],
+                    (sem_x2.at[0], sem_x2.at[1]), (index, k - 1), (section, row, py * cx + other),
+                ))
+        return copies
+
+    def add_first(index):
+        rows = at(index)
+        for copy in first_copies(index):
+            copy.wait()
+        for j in range(low):
+            for other in range(cy):
+                total = own[j, other, px, rows, :].astype(jnp.float32)
+                for k in range(cx - 1):
+                    total = total + rx1[k, j, other, rows, :].astype(jnp.float32)
+                own[j, other, px, rows, :] = total.astype(jnp.bfloat16)
+        for j in range(low, dp):
+            for other in range(cx):
+                total = own[j, py, other, rows, :].astype(jnp.float32)
+                for k in range(cy - 1):
+                    total = total + ry1[k, j - low, other, rows, :].astype(jnp.float32)
+                own[j, py, other, rows, :] = total.astype(jnp.bfloat16)
+        for copy in second_copies(index):
+            copy.start()
+
+    def z_copies(index):
+        rows, copies = at(index), []
+        for k in range(1, dp):
+            other = turn(row, k, dp)
+            copies.append(remote(
+                own.at[other, py, px, rows], rz.at[k - 1, rows],
+                (sem_z.at[0], sem_z.at[1]), (index, k - 1), (section, other, ctx),
+            ))
+        return copies
+
+    def add_second(index):
+        rows = at(index)
+        for copy in second_copies(index):
+            copy.wait()
+        for j in range(dp):
+            total = own[j, py, px, rows, :].astype(jnp.float32)
+            if j < low:
+                for k in range(cy - 1):
+                    total = total + ry2[k, j, rows, :].astype(jnp.float32)
+            else:
+                for k in range(cx - 1):
+                    total = total + rx2[k, j - low, rows, :].astype(jnp.float32)
+            own[j, py, px, rows, :] = total.astype(jnp.bfloat16)
+        for copy in z_copies(index):
+            copy.start()
+
+    def gather_copies(index):
+        rows, copies = at(index), []
+        for k in range(1, plan.ctx):
+            other = turn(ctx, k, plan.ctx)
+            copies.append(remote(
+                out.at[section, ctx, rows], out.at[section, ctx, rows],
+                (sem_g.at[0], sem_g.at[1]), (index, k - 1), (section, row, other),
+            ))
+        return copies
+
+    def forward_copy(index, k):
+        rows = at(index)
+        piece = turn(ctx, plan.ctx - k, plan.ctx)
+        return remote(
+            out.at[section, piece, rows], out.at[section, piece, rows],
+            (sem_f.at[0], sem_f.at[1]), (index, k), (mate, row, ctx),
+        )
+
+    def add_last(index):
+        rows = at(index)
+        for copy in z_copies(index):
+            copy.wait()
+        total = own[row, py, px, rows, :].astype(jnp.float32)
+        for k in range(dp - 1):
+            total = total + rz[k, rows, :].astype(jnp.float32)
+        out[section, ctx, rows, :] = total.astype(jnp.bfloat16)
+        for copy in gather_copies(index):
+            copy.start()
+        forward_copy(index, 0).start()
+
+    def pass_on(index):
+        for k, copy in enumerate(gather_copies(index)):
+            copy.wait()
+            forward_copy(index, k + 1).start()
+
+    def finish_all(index):
+        for k in range(plan.ctx):
+            forward_copy(index, k).wait()
+
+    stages = (make_partner, make_own, add_first, add_second, add_last, pass_on, finish_all)
+    for step in range(count + len(stages) - 1):
+        for number, stage in enumerate(stages):
+            if 0 <= step - number < count:
+                stage(step - number)
+    for index in range(max(count - 2, 0), count):
+        send_partner(index).wait_send()
+
+
+def reduce_grads(plan, *operands):
+    dp, ctx, total = plan.dp, plan.ctx, plan.total
+    low, high = plan.low, max(plan.dp - plan.low, 1)
+    widest, count = max(c[4] for c in plan.chunks), len(plan.chunks)
+    nx, ny, nz = max(plan.cx - 1, 1), max(plan.cy - 1, 1), max(dp - 1, 1)
+    low_type = jnp.bfloat16
+    dma = pltpu.SemaphoreType.DMA
+    return pl.pallas_call(
+        functools.partial(reduce_kernel, plan),
+        out_shape=jax.ShapeDtypeStruct((2, ctx, total, LANES), low_type),
+        in_specs=[pl.BlockSpec(memory_space=pltpu.VMEM)] * len(operands),
+        out_specs=pl.BlockSpec(memory_space=pltpu.VMEM),
+        scratch_shapes=[
+            pltpu.VMEM((2, dp, ctx, widest, LANES), low_type),
+            pltpu.VMEM((dp, ctx, total, LANES), low_type),
+            pltpu.VMEM((dp, plan.cy, plan.cx, total, LANES), low_type),
+            pltpu.VMEM((nx, low, plan.cy, total, LANES), low_type),
+            pltpu.VMEM((ny, high, plan.cx, total, LANES), low_type),
+            pltpu.VMEM((nx, high, total, LANES), low_type),
+            pltpu.VMEM((ny, low, total, LANES), low_type),
+            pltpu.VMEM((nz, total, LANES), low_type),
+            dma((count,)),
+            dma((count,)),
+            dma((2, count, nx)),
+            dma((2, count, ny)),
+            dma((2, count, nx)),
+            dma((2, count, ny)),
+            dma((2, count, nz)),
+            dma((2, count, max(ctx - 1, 1))),
+            dma((2, count, ctx)),
+        ],
+        compiler_params=pltpu.CompilerParams(
+            collective_id=0, has_side_effects=True, vmem_limit_bytes=64 << 20
+        ),
+        cost_estimate=pl.CostEstimate(flops=10**10, bytes_accessed=20 * 10**6, transcendentals=0),
+    )(*operands)
 
 
 def body(
@@ -203,20 +517,11 @@
         ) = saved
         grad_low = grad_out.astype(jnp.bfloat16)
         grad_inner = jnp.einsum("rcd,fd->rcf", grad_low, w_down, preferred_element_type=jnp.float32)
-        backward_sum_down = jnp.einsum(
-            "rcf,rcd->fd", backward_inner_act, grad_low, preferred_element_type=jnp.float32
-        )
         sigmoid = jax.nn.sigmoid(backward_gate_pre)
         grad_gate = (
             grad_inner * backward_upward * sigmoid * (1.0 + backward_gate_pre * (1.0 - sigmoid))
         ).astype(jnp.bfloat16)
         grad_up = (grad_inner * backward_gate_pre * sigmoid).astype(jnp.bfloat16)
-        backward_sum_gate = jnp.einsum(
-            "rcd,rcf->df", backward_ffn_low, grad_gate, preferred_element_type=jnp.float32
-        )
-        backward_sum_up = jnp.einsum(
-            "rcd,rcf->df", backward_ffn_low, grad_up, preferred_element_type=jnp.float32
-        )
         grad_norm_ffn = jnp.einsum(
             "rcf,df->rcd", grad_gate, w_gate, preferred_element_type=jnp.float32
         ) + jnp.einsum("rcf,df->rcd", grad_up, w_up, preferred_element_type=jnp.float32)
@@ -225,9 +530,6 @@
         )
         grad_middle = grad_out + grad_mid_norm
         grad_branch = grad_middle.astype(jnp.bfloat16)
-        backward_sum_out = jnp.einsum(
-            "rce,rcd->ed", backward_attn_low, grad_branch, preferred_element_type=jnp.float32
-        )
         grad_attn = jnp.einsum(
             "rcd,ed->rce", grad_branch, w_out, preferred_element_type=jnp.float32
         ).astype(jnp.bfloat16)
@@ -311,29 +613,17 @@
             [key_back.reshape(row_count, tok_local, kv_width), pair_share[..., kv_width:]], -1
         )
         pair_low = pair_low.astype(jnp.bfloat16)
-        backward_sum_query = jnp.einsum(
-            "rcd,rce->de", backward_normed_low, query_back, preferred_element_type=jnp.float32
-        )
-        sum_pair = jnp.einsum(
-            "rcd,rce->de", backward_normed_low, pair_low, preferred_element_type=jnp.float32
-        )
         grad_normed = jnp.einsum(
             "rce,de->rcd", query_back, w_query, preferred_element_type=jnp.float32
         ) + jnp.einsum("rce,de->rcd", pair_low, w_pair, preferred_element_type=jnp.float32)
         grad_front, backward_sum_gain_attn = rms_backward(
             hidden, gain_attn, backward_inverse, grad_normed
         )
-        tick_grads = (
-            backward_sum_gain_attn,
-            backward_sum_query,
-            sum_pair[:, :kv_width],
-            sum_pair[:, kv_width:],
-            backward_sum_out,
-            backward_sum_gain_ffn,
-            backward_sum_gate,
-            backward_sum_up,
-            backward_sum_down,
-        )
+        factors = (
+            backward_normed_low, backward_attn_low, backward_ffn_low, backward_inner_act,
+            query_back, pair_low, grad_branch, grad_gate, grad_up, grad_low,
+        )
+        tick_grads = (backward_sum_gain_attn, backward_sum_gain_ffn, factors)
         return grad_middle + grad_front, tick_grads
 
     def exchange(for_first, for_last):
@@ -349,56 +639,79 @@
     grad_mid, second_grads = backward(mine(cotangent).astype(jnp.float32), second_kept)
     grad_mid_low = grad_mid.astype(jnp.bfloat16)
     grad_in, first_grads = backward(grad_mid_low.astype(jnp.float32), first_kept)
-    (
-        sum_gain_attn,
-        sum_query,
-        sum_key,
-        sum_value,
-        sum_out,
-        sum_gain_ffn,
-        sum_gate,
-        sum_up,
-        sum_down,
-    ) = tuple(one + other for one, other in zip(second_grads, first_grads))
-    shares = (
-        lax.psum_scatter(
-            sum_gain_attn.astype(jnp.bfloat16), "dp", scatter_dimension=0, tiled=True
-        ).astype(jnp.float32),
-        lax.psum_scatter(
-            sum_query.astype(jnp.bfloat16), "dp", scatter_dimension=0, tiled=True
-        ).astype(jnp.float32),
-        lax.psum_scatter(
-            sum_key.astype(jnp.bfloat16), "dp", scatter_dimension=0, tiled=True
-        ).astype(jnp.float32),
-        lax.psum_scatter(
-            sum_value.astype(jnp.bfloat16), "dp", scatter_dimension=0, tiled=True
-        ).astype(jnp.float32),
-        lax.psum_scatter(
-            sum_out.astype(jnp.bfloat16), "dp", scatter_dimension=0, tiled=True
-        ).astype(jnp.float32),
-        lax.psum_scatter(
-            sum_gain_ffn.astype(jnp.bfloat16), "dp", scatter_dimension=0, tiled=True
-        ).astype(jnp.float32),
-        lax.psum_scatter(
-            sum_gate.astype(jnp.bfloat16), "dp", scatter_dimension=0, tiled=True
-        ).astype(jnp.float32),
-        lax.psum_scatter(sum_up.astype(jnp.bfloat16), "dp", scatter_dimension=0, tiled=True).astype(
-            jnp.float32
+    plan = Plan(
+        lax.axis_size("dp"), lax.axis_size("ctx"), model_width, w_gate.shape[1], kv_width
+    )
+    dp = plan.dp
+
+    def stacked(one, other):
+        return jnp.concatenate([one, other], 1).reshape(-1, one.shape[-1])
+
+    normed, attn, ffn, inner, d_query, d_pair, d_branch, d_gate, d_up, d_out = (
+        stacked(one, other) for one, other in zip(first_grads[2], second_grads[2])
+    )
+    tokens = normed.shape[0]
+
+    def sides(values, rows):
+        cut = values.reshape(tokens, dp, -1)
+        cut = jnp.pad(cut, ((0, 0), (0, 0), (0, rows - cut.shape[2])))
+        return cut.transpose(1, 2, 0)
+
+    normed_t = sides(normed, plan.rows)
+    halves = inner.reshape(tokens, dp, 2, -1)
+    inner_t = jnp.stack([sides(halves[:, :, h], plan.down_rows) for h in range(2)])
+    wide = plan.width_tiles * LANES
+    spare = wide - model_width
+    extra = jnp.stack([
+        jnp.pad((one + other).reshape(dp, -1), ((0, 0), (0, 16 * LANES - model_width // dp)))
+        for one, other in zip(first_grads[:2], second_grads[:2])
+    ]).reshape(2, dp, 16, LANES)
+    summed = reduce_grads(
+        plan,
+        sides(ffn, plan.rows),
+        jnp.stack([d_gate, d_up]),
+        inner_t,
+        jnp.pad(d_out, ((0, 0), (0, spare))),
+        jnp.stack([normed_t, sides(attn, plan.rows)]),
+        jnp.pad(jnp.stack([d_query, d_branch]), ((0, 0), (0, 0), (0, spare))),
+        jnp.pad(
+            jnp.stack([d_pair[:, :kv_width], d_pair[:, kv_width:]]),
+            ((0, 0), (0, 0), (LANES - spare, 0)),
         ),
-        lax.psum_scatter(
-            sum_down.astype(jnp.bfloat16), "dp", scatter_dimension=0, tiled=True
-        ).astype(jnp.float32),
-    )
+        extra,
+    )
+
+    def tiles_of(kind):
+        found = []
+        for index, (name, start, tiles, rows, piece) in enumerate(plan.chunks):
+            if name == kind:
+                first = plan.offsets[index]
+                flat = summed[:, :, first : first + piece].reshape(2, -1, LANES)
+                found.append(flat[:, : tiles * rows].reshape(2, tiles, rows, LANES))
+        return jnp.concatenate(found, 1)
+
+    def joined(values, rows):
+        values = values[:, :, :rows].transpose(0, 2, 1, 3)
+        return values.reshape(2, rows, -1).astype(jnp.float32)
+
+    ffn_sum = joined(tiles_of("ffn"), model_width // dp)
+    down_sum = joined(tiles_of("down"), w_down.shape[0] // dp // 2)[:, :, :model_width]
+    attn_sum = joined(
+        jnp.concatenate([tiles_of("attn"), tiles_of("mixed")], 1), model_width // dp
+    )
+    kind, start, tiles, rows, piece = plan.chunks[-1]
+    flat = summed[:, :, plan.offsets[-1] : plan.offsets[-1] + piece].reshape(2, -1)
+    flat = flat[:, tiles * rows * LANES :][:, : model_width // dp].astype(jnp.float32)
     totals = (
-        lax.psum(shares[0].astype(jnp.bfloat16), ("section", "ctx")).astype(jnp.float32),
-        lax.psum(shares[1].astype(jnp.bfloat16), ("section", "ctx")).astype(jnp.float32),
-        lax.psum(shares[2].astype(jnp.bfloat16), ("section", "ctx")).astype(jnp.float32),
-        lax.psum(shares[3].astype(jnp.bfloat16), ("section", "ctx")).astype(jnp.float32),
-        lax.psum(shares[4].astype(jnp.bfloat16), ("section", "ctx")).astype(jnp.float32),
-        lax.psum(shares[5].astype(jnp.bfloat16), ("section", "ctx")).astype(jnp.float32),
-        lax.psum(shares[6].astype(jnp.bfloat16), ("section", "ctx")).astype(jnp.float32),
-        lax.psum(shares[7].astype(jnp.bfloat16), ("section", "ctx")).astype(jnp.float32),
-        lax.psum(shares[8].astype(jnp.bfloat16), ("section", "ctx")).astype(jnp.float32),
+        flat[0],
+        attn_sum[0, :, :model_width],
+        attn_sum[0, :, model_width:],
+        attn_sum[1, :, model_width:],
+        attn_sum[1, :, :model_width],
+        flat[1],
+        ffn_sum[0],
+        ffn_sum[1],
+        down_sum.reshape(-1, model_width),
     )
     activations = exchange(first_low, second_low)[None]
     input_grads = exchange(grad_in.astype(jnp.bfloat16), grad_mid_low).astype(jnp.float32)[None]

time: 892 us -> 558 us (0.63)
  waiting for transfers between devices: 530 us -> 69.7 us
  Pallas kernels: 0 us -> 132 us
  local copies, waits for them, and re-layouts: 59 us -> 114 us
  matrix products: 188 us -> 150 us
  blocking collectives: 26.5 us -> 0 us
    reduce_scatter x6 -> x0, waiting for transfers between devices: 317 us -> none  [the longest x1 91.4 us: body(): lax.psum_scatter(sum_up.astype(jnp.bfloat16), 'dp', scatter_dimension=0,...]
    pallas_call x0 -> x1, Pallas kernels: none -> 132 us  [reduce_grads(): pl.pallas_call(functools.partial(reduce_kernel, plan), out_shape=jax.Shap...]
    unnamed x13 -> x4, waiting for transfers between devices: 75.2 us -> 0.07 us
    psum x1 -> x0, waiting for transfers between devices: 59.3 us -> none  [body(): lax.psum(shares[2].astype(jnp.bfloat16), ('section', 'ctx'))]
    dot_general x12 -> x0, matrix products: 32.2 us -> none  [the longest x2 6.7 us: backward(): jnp.einsum('rcf,rcd->fd', backward_inner_act, grad_low, preferred_element...]
    psum x1 -> x0, blocking collectives: 15.5 us -> none  [body(): lax.psum(shares[0].astype(jnp.bfloat16), ('section', 'ctx'))]
    reduce_sum x4, other arithmetic: 21.1 us -> 7.45 us  [fold_inner_step(): run_sum = run_sum * rescale + jnp.sum(weights, -1)]
    convert_element_type x0 -> x9, local copies, waits for them, and re-layouts: none -> 13.3 us  [the longest x2 4.3 us: rear(): inner_act = (jax.nn.silu(gate_pre) * upward).astype(jnp.bfloat16)]
  transfers between devices with their start and end apart: 14 -> 6, of which waited for: 12 -> 4; matrix products, arithmetic and copies ran while one was open for 8% -> 12% of each run, Pallas kernels for 0% -> 0%
where the time goes in v2:
time: 558 us; the launch traced here: 550 us
  matrix products  150 us (27%)
  Pallas kernels  132 us (24%)
  local copies, waits for them, and re-layouts  114 us (20%)
  waiting for transfers between devices  69.7 us (12%)
  other arithmetic  66.5 us (12%)
  between operations  15.9 us (3%)
    pallas_call x1, Pallas kernels, reduce_grads(): pl.pallas_call(functools.partial(reduce_kernel, plan), out_shape=jax.Shap...  132 us
    all_gather x2, waiting for transfers between devices, forward(): arrived = lax.all_gather(packed, 'ctx', axis=1, tiled=True)  52.1 us
    unnamed x267, local copies, waits for them, and re-layouts  31.9 us
    dot_general x4, matrix products, fold_inner_step(): jnp.einsum('rkgcn,rnkd->rkgcd', weights.astype(jnp.bfloat16), value_part,...  26.1 us
    dot_general x8, matrix products, block_scores(): jnp.einsum('rckgd,rnkd->rkgcn', queries, key_part, preferred_element_type...  22.9 us
    reduce_scatter x2, waiting for transfers between devices, backward(): lax.psum_scatter(grad_pair.astype(jnp.bfloat16), 'ctx', scatter_dimension...  17.6 us
    dot_general x4, matrix products, piece_inner_step(): jnp.einsum('rkgcn,rkgcd->rnkd', chances.astype(jnp.bfloat16), grad_heads,...  12.2 us
    dot_general x4, matrix products, piece_inner_step(): jnp.einsum('rkgcn,rnkd->rkgcd', grad_scores, key_part, preferred_element_...  12.2 us
  transfers between devices with their start and end apart: 6, of which 4 were waited for; matrix products, arithmetic and copies ran while one was open for 12% of the time, Pallas kernels for 0%

profile of v2, /device:TPU:0, one launch (start us, length us, event | category | flops | bytes accessed | tf_op | source)
XLA Modules:
  0.0 549.9 jit_solution(8723960123315602484)
XLA Ops:
  16.1 3.8 copy.78
  22.6 25.1 %all-gather.3.cloned.1.call-done = bf16[1,1024,640]{2,1,0:T(8,128)(2,1)} async-done(((bf16[1,256,640]{2,1,0:T(8,128)(2,1)}), bf16[1,1024,640]{2,1,0:T(8,128)(2,1)}) %all-gather.3.cloned.1.call-update) | async-done | bytes 1310736 | tf_op jit(solution)/shard_map/all_gather | solution.py:490
  49.3 28.4 %while.68 = (s32[]{:T(128)}, f32[1,5,3,256]{3,2,1,0:T(4,128)S(1)}, f32[1,5,3,256]{3,2,1,0:T(4,128)S(1)}, f32[1,5,3,256,64]{3,4,2,1,0:T(8,128)}, s32[1,256]{1,0:T...) while((s32[]{:T(128)}, f32[1,5,3,256]{3,2,1,0:T(4,128)S(1)}, ...), condition=%wide.region_4.5_spmd.clone, body=%wide.region_1.4_spmd.clone.sunk | while | flops 530029824 | bytes 60257528 | solution.py:456
  50.4 4.5 fusion.262
  54.9 6.5 %fusion.265 = f32[1,5,3,256,64]{3,4,2,1,0:T(8,128)} fusion(bf16[512,5,64,1]{0,2,3,1:T(8,128)(2,1)} %bitcast.720, f32[5,512,256,3]{2,1,3,0:T(8,128)} %get-tuple-element.1357, f32[5,3,256]{2,1,0:T(4,128)S(1)} %bitcast.716, pred[256,512]{0,1:T(8,128)(4,1)S(1)} %compare_and_fusion.8, f32[1,5,3,256,64]{3,4,2,1,0:T(8,128)} %get-tuple-element.1418, ...), kind=kOutput, calls=%fused_computation.13.clone.1 | convolution fusion | flops 262225920 | bytes 10319873 | tf_op jit(solution)/shard_map/while/body/eval_jaxpr/rkgcn,rnkd->rkgcd/dot_general | solution.py:448
  64.4 4.5 fusion.262
  68.9 6.7 %fusion.265 = f32[1,5,3,256,64]{3,4,2,1,0:T(8,128)} fusion(bf16[512,5,64,1]{0,2,3,1:T(8,128)(2,1)} %bitcast.720, f32[5,512,256,3]{2,1,3,0:T(8,128)} %get-tuple-element.1357, f32[5,3,256]{2,1,0:T(4,128)S(1)} %bitcast.716, pred[256,512]{0,1:T(8,128)(4,1)S(1)} %compare_and_fusion.8, f32[1,5,3,256,64]{3,4,2,1,0:T(8,128)} %get-tuple-element.1418, ...), kind=kOutput, calls=%fused_computation.13.clone.1 | convolution fusion | flops 262225920 | bytes 10319873 | tf_op jit(solution)/shard_map/while/body/eval_jaxpr/rkgcn,rnkd->rkgcd/dot_general | solution.py:448
  83.3 4.1 fusion.154
  87.5 3.2 multiply_convert_fusion.5
  102.6 26.9 %all-gather.5.cloned.1.call-done = bf16[1,1024,640]{2,1,0:T(8,128)(2,1)} async-done(((bf16[1,256,640]{2,1,0:T(8,128)(2,1)}), bf16[1,1024,640]{2,1,0:T(8,128)(2,1)}) %all-gather.5.cloned.1.call-update) | async-done | bytes 1310736 | tf_op jit(solution)/shard_map/all_gather | solution.py:490
  131.5 26.6 %while.69 = (s32[]{:T(128)}, f32[1,5,3,256]{3,2,1,0:T(4,128)S(1)}, f32[1,5,3,256]{3,2,1,0:T(4,128)S(1)}, f32[1,5,3,256,64]{3,4,2,1,0:T(8,128)}, s32[1,256]{1,0:T...) while((s32[]{:T(128)}, f32[1,5,3,256]{3,2,1,0:T(4,128)S(1)}, ...), condition=%wide.region_10.11_spmd.clone, body=%wide.region_7.10_spmd.clone.sunk | while | flops 530029824 | bytes 60257528 | solution.py:456
  131.9 4.5 fusion.269
  136.4 6.4 %fusion.272 = f32[1,5,3,256,64]{3,4,2,1,0:T(8,128)} fusion(bf16[512,5,64,1]{0,2,3,1:T(8,128)(2,1)S(1)} %bitcast.721, f32[5,512,256,3]{2,1,3,0:T(8,128)} %get-tuple-element.1372, f32[5,3,256]{2,1,0:T(4,128)S(1)} %bitcast.718, pred[256,512]{0,1:T(8,128)(4,1)S(1)} %compare_and_fusion.9, f32[1,5,3,256,64]{3,4,2,1,0:T(8,128)} %get-tuple-element.1460, ...), kind=kOutput, calls=%fused_computation.40.clone.1 | convolution fusion | flops 262225920 | bytes 10319873 | tf_op jit(solution)/shard_map/while/body/eval_jaxpr/rkgcn,rnkd->rkgcd/dot_general | solution.py:448
  145.1 4.5 fusion.269
  149.6 6.6 %fusion.272 = f32[1,5,3,256,64]{3,4,2,1,0:T(8,128)} fusion(bf16[512,5,64,1]{0,2,3,1:T(8,128)(2,1)S(1)} %bitcast.721, f32[5,512,256,3]{2,1,3,0:T(8,128)} %get-tuple-element.1372, f32[5,3,256]{2,1,0:T(4,128)S(1)} %bitcast.718, pred[256,512]{0,1:T(8,128)(4,1)S(1)} %compare_and_fusion.9, f32[1,5,3,256,64]{3,4,2,1,0:T(8,128)} %get-tuple-element.1460, ...), kind=kOutput, calls=%fused_computation.40.clone.1 | convolution fusion | flops 262225920 | bytes 10319873 | tf_op jit(solution)/shard_map/while/body/eval_jaxpr/rkgcn,rnkd->rkgcd/dot_general | solution.py:448
  163.0 4.3 fusion.155
  169.0 3.7 multiply_convert_fusion.2
  181.6 43.5 %while.70 = (s32[]{:T(128)}, f32[1,5,3,256,64]{3,4,2,1,0:T(8,128)}, f32[1,1024,640]{2,1,0:T(8,128)}, s32[1,256]{1,0:T(1,128)S(1)}, s32[1,1024]{1,0:T(1,128)S(1)}...) while((s32[]{:T(128)}, f32[1,5,3,256,64]{3,4,2,1,0:T(8,128)}, ...), condition=%wide.region_15.16_spmd.clone, body=%wide.region_14.15_spmd.clone.sunk | while | flops 1283834624 | bytes 104327600 | solution.py:592
  199.3 3.1 fusion.285
  221.1 3.1 fusion.285
  238.4 5.2 select_bitcast_fusion.3
  243.6 14.0 %reduce-scatter.3.cloned.1.call-done = bf16[1,256,640]{2,1,0:T(8,128)(2,1)} async-done(((bf16[1,1024,640]{2,1,0:T(8,128)(2,1)}), bf16[1,256,640]{2,1,0:T(8,128)(2,1)}) %reduce-scatter.3.cloned.1.call-update) | async-done | bytes 327696 | tf_op jit(solution)/shard_map/reduce_scatter | solution.py:597
  263.2 5.5 multiply_convert_fusion
  277.9 46.0 %while.71 = (s32[]{:T(128)}, f32[1,5,3,256,64]{3,4,2,1,0:T(8,128)}, f32[1,1024,640]{2,1,0:T(8,128)}, s32[1,256]{1,0:T(1,128)S(1)}, s32[1,1024]{1,0:T(1,128)S(1)}...) while((s32[]{:T(128)}, f32[1,5,3,256,64]{3,4,2,1,0:T(8,128)}, ...), condition=%wide.region_21.22_spmd.clone, body=%wide.region_20.21_spmd.clone.sunk | while | flops 1283834624 | bytes 95930848 | solution.py:592
  287.9 3.1 fusion.301
  310.7 3.1 fusion.301
  323.9 3.1 convert_element_type.438
  349.6 3.3 maximum_maximum_fusion.ffn_dy
  352.9 3.6 reduce-scatter.5.cloned.1.call-done
  362.2 3.3 fusion.124
  369.2 131.8 %shard_map.203 = bf16[2,4,2464,128]{3,2,1,0:T(8,128)(2,1)} custom-call(bf16[4,240,512]{2,1,0:T(8,128)(2,1)} %maximum_bitcast_fusion.2.ffn_x, bf16[2,512,2560]{2,1,0:T(8,128)(2,1)} %maximum_maximum_fusion.ffn_dy, bf16[2,4,320,512]{3,2,1,0:T(8,128)(2,1)} %pad_maximum_fusion.down_x, bf16[512,1024]{1,0:T(8,128)(2,1)} %pad.19.down_dy, ...), custom_call_target="tpu_custom_call" | custom-call | flops 10000000000 | bytes 20000000 | tf_op jit(solution)/shard_map/pallas_call | solution.py:340
  514.5 3.4 copy.119
  (589 shorter events, 231.6 us)
Async XLA Ops:
  7.2 40.5 %all-gather.3.cloned.1.call-start = ((), (), s32[]{:S(2)}) async-start(), calls=%async_computation.2 | async-start | bytes 1638400 | tf_op jit(solution)/shard_map/all_gather | solution.py:490
  9.6 10.5 %copy-start.22 = (bf16[1,1,256,960]{3,2,1,0:T(8,128)(2,1)}, bf16[1,1,256,960]{3,2,1,0:T(8,128)(2,1)S(1)}, u32[]{:S(2)}) copy-start(bf16[1,1,256,960]{3,2,1,0:T(8,128)(2,1)S(1)} %copy.173) | copy-start | bytes 1474564
  10.3 9.7 %copy-start.102 = (f32[256]{0:T(256)}, f32[256]{0:T(256)S(1)}, u32[]{:S(2)}) copy-start(f32[256]{0:T(256)S(1)} %get-tuple-element.1104) | copy-start | bytes 3076
  10.3 82.7 %copy-start.98 = (f32[960]{0:T(1024)}, f32[960]{0:T(1024)S(1)}, u32[]{:S(2)}) copy-start(f32[960]{0:T(1024)S(1)} %convert_element_type.399) | copy-start | bytes 11524
  11.5 81.7 %copy-start.19 = (bf16[960,640]{0,1:T(8,128)(2,1)}, bf16[960,640]{0,1:T(8,128)(2,1)S(1)}, u32[]{:S(2)}) copy-start(bf16[960,640]{0,1:T(8,128)(2,1)S(1)} %constant_dynamic-update-slice_fusion.2) | copy-start | bytes 3686404
  14.0 88.4 %copy-start.60 = (f32[256,32]{0,1:T(8,128)}, f32[256,32]{0,1:T(8,128)S(1)}, u32[]{:S(2)}) copy-start(f32[256,32]{0,1:T(8,128)S(1)} %get-tuple-element.1102) | copy-start | bytes 98308
  16.1 113.5 %all-gather.5.cloned.1.call-start = ((), (), s32[]{:S(2)}) async-start(), calls=%async_computation.3 | async-start | bytes 1638400 | tf_op jit(solution)/shard_map/all_gather | solution.py:490
  79.7 7.7 %slice-start.8 = ((s8[4915200]{0:T(1024)(128)(4,1)}), s8[4194304]{0:T(1024)(128)(4,1)S(1)}, s32[]{:S(2)}) async-start(s8[4915200]{0:T(1024)(128)(4,1)} %bitcast.799), calls=%async_computation.14 | async-start | bytes 8388608
  82.4 8.3 %copy-start.31 = (f32[256,960]{1,0:T(8,128)}, f32[256,960]{1,0:T(8,128)S(1)}, u32[]{:S(2)}) copy-start(f32[256,960]{1,0:T(8,128)S(1)} %get-tuple-element.1112) | copy-start | bytes 2949124
  83.3 7.4 %slice-start = ((s8[4915200]{0:T(1024)(128)(4,1)}), s8[4194304]{0:T(1024)(128)(4,1)S(1)}, s32[]{:S(2)}) async-start(s8[4915200]{0:T(1024)(128)(4,1)} %bitcast.791), calls=%async_computation.6 | async-start | bytes 8388608
  94.0 7.7 %copy-start.39 = (bf16[960,960]{0,1:T(8,128)(2,1)S(1)}, bf16[960,960]{0,1:T(8,128)(2,1)}, u32[]{:S(2)}) copy-start(bf16[960,960]{0,1:T(8,128)(2,1)} %copy.78) | copy-start | bytes 5529604
  94.8 6.9 %copy-start.41 = (bf16[256,960]{1,0:T(8,128)(2,1)S(1)}, bf16[256,960]{1,0:T(8,128)(2,1)}, u32[]{:S(2)}) copy-start(bf16[256,960]{1,0:T(8,128)(2,1)} %copy-done.40) | copy-start | bytes 1474564
  100.6 157.0 %reduce-scatter.3.cloned.1.call-start = ((), (), s32[]{:S(2)}) async-start(), calls=%async_computation.4 | async-start | bytes 1638400 | tf_op jit(solution)/shard_map/reduce_scatter | solution.py:597
  160.2 7.2 %slice-start.10 = ((s8[4915200]{0:T(1024)(128)(4,1)}), s8[4194304]{0:T(1024)(128)(4,1)S(1)}, s32[]{:S(2)}) async-start(s8[4915200]{0:T(1024)(128)(4,1)} %bitcast.801), calls=%async_computation.16 | async-start | bytes 8388608
  162.8 14.0 %copy-start.33 = (f32[256,960]{1,0:T(8,128)}, f32[256,960]{1,0:T(8,128)S(1)}, u32[]{:S(2)}) copy-start(f32[256,960]{1,0:T(8,128)S(1)} %get-tuple-element.1118) | copy-start | bytes 2949124
  228.2 128.3 %reduce-scatter.5.cloned.1.call-start = ((), (), s32[]{:S(2)}) async-start(), calls=%async_computation.5 | async-start | bytes 1638400 | tf_op jit(solution)/shard_map/reduce_scatter | solution.py:597
  238.4 20.4 %copy-start.94 = (f32[256,32]{0,1:T(8,128)S(1)}, f32[256,32]{0,1:T(8,128)}, u32[]{:S(2)}) copy-start(f32[256,32]{0,1:T(8,128)} %get-tuple-element.1100) | copy-start | bytes 98308
  243.6 16.2 %copy-start.20 = (bf16[960,640]{0,1:T(8,128)(2,1)S(1)}, bf16[960,640]{0,1:T(8,128)(2,1)}, u32[]{:S(2)}) copy-start(bf16[960,640]{0,1:T(8,128)(2,1)} %copy-done.19) | copy-start | bytes 3686404
  243.6 16.3 %copy-start.99 = (f32[960]{0:T(1024)S(1)}, f32[960]{0:T(1024)}, u32[]{:S(2)}) copy-start(f32[960]{0:T(1024)} %copy-done.98) | copy-start | bytes 11524
  243.6 16.3 %copy-start.109 = (f32[256]{0:T(256)S(1)}, f32[256]{0:T(256)}, u32[]{:S(2)}) copy-start(f32[256]{0:T(256)} %copy-done.108) | copy-start | bytes 3076
  259.9 8.8 %slice-start.6 = ((s8[4915200]{0:T(1024)(128)(4,1)}), s8[4194304]{0:T(1024)(128)(4,1)S(1)}, s32[]{:S(2)}) async-start(s8[4915200]{0:T(1024)(128)(4,1)} %bitcast.797), calls=%async_computation.12 | async-start | bytes 8388608
  259.9 10.4 %slice-start.12 = ((s8[4915200]{0:T(1024)(128)(4,1)}), s8[4194304]{0:T(1024)(128)(4,1)S(1)}, s32[]{:S(2)}) async-start(s8[4915200]{0:T(1024)(128)(4,1)} %bitcast.803), calls=%async_computation.18 | async-start | bytes 8388608
  263.2 10.0 %copy-start.28 = (bf16[256,960]{1,0:T(8,128)(2,1)}, bf16[256,960]{1,0:T(8,128)(2,1)S(1)}, u32[]{:S(2)}) copy-start(bf16[256,960]{1,0:T(8,128)(2,1)S(1)} %fusion.108) | copy-start | bytes 1474564
  263.2 7.2 %slice-start.13 = ((s8[4915200]{0:T(1024)(128)(4,1)}), s8[720896]{0:T(1024)(128)(4,1)S(1)}, s32[]{:S(2)}) async-start(s8[4915200]{0:T(1024)(128)(4,1)} %bitcast.803), calls=%async_computation.19 | async-start | bytes 1441792
  278.4 9.6 %copy-start.73 = (bf16[1,5,3,256,64]{3,4,2,1,0:T(8,128)(2,1)}, bf16[1,5,3,256,64]{3,4,2,1,0:T(8,128)(2,1)S(1)}, u32[]{:S(2)}) copy-start(bf16[1,5,3,256,64]{3,4,2,1,0:T(8,128)(2,1)S(1)} %get-tuple-element.1573) | copy-start | bytes 1474564 | tf_op jit(solution)/shard_map/while
  301.1 9.6 %copy-start.73 = (bf16[1,5,3,256,64]{3,4,2,1,0:T(8,128)(2,1)}, bf16[1,5,3,256,64]{3,4,2,1,0:T(8,128)(2,1)S(1)}, u32[]{:S(2)}) copy-start(bf16[1,5,3,256,64]{3,4,2,1,0:T(8,128)(2,1)S(1)} %get-tuple-element.1573) | copy-start | bytes 1474564 | tf_op jit(solution)/shard_map/while
  333.3 4.2 collective-permute-start
  349.6 10.6 %copy-start.95 = (f32[256,32]{0,1:T(8,128)S(1)}, f32[256,32]{0,1:T(8,128)}, u32[]{:S(2)}) copy-start(f32[256,32]{0,1:T(8,128)} %get-tuple-element.1100) | copy-start | bytes 98308
  352.9 9.3 %copy-start.21 = (bf16[960,640]{0,1:T(8,128)(2,1)S(1)}, bf16[960,640]{0,1:T(8,128)(2,1)}, u32[]{:S(2)}) copy-start(bf16[960,640]{0,1:T(8,128)(2,1)} %copy-done.19) | copy-start | bytes 3686404
  352.9 9.3 %copy-start.24 = (bf16[1,1,256,960]{3,2,1,0:T(8,128)(2,1)S(1)}, bf16[1,1,256,960]{3,2,1,0:T(8,128)(2,1)}, u32[]{:S(2)}) copy-start(bf16[1,1,256,960]{3,2,1,0:T(8,128)(2,1)} %copy-done.22) | copy-start | bytes 1474564
  352.9 9.3 %copy-start.104 = (f32[256]{0:T(256)S(1)}, f32[256]{0:T(256)}, u32[]{:S(2)}) copy-start(f32[256]{0:T(256)} %copy-done.102) | copy-start | bytes 3076
  522.8 17.1 %collective-permute-start.1 = (bf16[1,256,960]{2,1,0:T(8,128)(2,1)}, bf16[1,256,960]{2,1,0:T(8,128)(2,1)}, u32[]{:S(2)}, u32[]{:S(2)}) collective-permute-start(bf16[1,256,960]{2,1,0:T(8,128)(2,1)} %select_bitcast_fusion), channel_id=1, source_target_pairs={{0,16},{16,0},{1,17},{17,1},{2,18},{18,2},{3,19},{19,3},{4,20},{20... | collective-permute-start | bytes 1474568 | tf_op jit(solution)/shard_map/ppermute | solution.py:632
  (131 other events, 420.2 us)
Sparse Core Ops, SparseCore 0:
  16.2 31.4 all-gather.2
  100.7 28.7 all-gather.4
  228.3 29.2 reduce-scatter.2
  327.1 29.3 reduce-scatter.4

commit v3 on v2

--- a/solution.py
+++ b/solution.py
@@ -3,6 +3,7 @@
 
 import jax
 import jax.numpy as jnp
+import numpy as np
 from jax import lax
 from jax.experimental import pallas as pl
 from jax.experimental.pallas import tpu as pltpu
@@ -17,6 +18,7 @@
 
 epsilon = 1e-05
 score_scale = 0.125
+score_unit = score_scale / math.log(2.0)
 mask_floor = -1e30
 
 
@@ -142,7 +144,7 @@
                 )
             elif kind == "down":
                 value = jnp.dot(
-                    down_x[half, j], down_dy[:, start * LANES : (start + tiles) * LANES],
+                    down_x[2 * j + half], down_dy[:, start * LANES : (start + tiles) * LANES],
                     preferred_element_type=jnp.float32,
                 )
             elif kind == "attn":
@@ -368,19 +370,403 @@
     )(*operands)
 
 
-def body(
-    inputs,
-    segment_ids,
-    cotangent,
-    gain_attn,
-    w_query,
-    w_key,
-    w_value,
-    w_out,
-    gain_ffn,
-    w_gate,
-    w_up,
-    w_down,
+class Block:
+    def __init__(self, tokens, length, width, hidden, kv_width, ctx):
+        self.tokens, self.length, self.width, self.hidden = tokens, length, width, hidden
+        self.kv_width, self.ctx = kv_width, ctx
+        self.kv_heads = kv_width // HEAD_DIM
+        self.group = width // kv_width
+        self.step = 512
+
+
+def dot(one, other, over=(1, 0)):
+    return lax.dot_general(
+        one, other, (((over[0],), (over[1],)), ((), ())), preferred_element_type=jnp.float32
+    )
+
+
+def block_kernel(
+    size, inputs, cotangent, segments, cos_q, sin_q, cos_kv, sin_kv, gain_attn, gain_ffn,
+    wq_in, wk_in, wv_in, wo_in, wg_in, wu_in, wd_in,
+    acts, grad_mid, grad_in, x_attn, n2_t, inner_t, d_attn, d_pair, d_ffn, d_out, gain_sums,
+    wq, wk, wv, wo, wg, wu, wd, xin, cot, mid, q_t, kv, kv_send, kv_recv, lse, o_t, do_t, dq_t, bias, accum, dmid,
+    sem_w, sem_k, sem_d,
+):
+    tokens, ctx_count, groups, group = size.tokens, size.ctx, size.kv_heads, size.group
+    low_type = jnp.bfloat16
+    section, row, ctx = (lax.axis_index(name) for name in ("section", "dp", "ctx"))
+    loads = [
+        pltpu.make_async_copy(source, target, sem_w.at[number])
+        for number, (source, target) in enumerate((
+            (inputs.at[section], xin.at[0]), (wk_in, wk), (wv_in, wv), (wq_in, wq), (wo_in, wo),
+            (wg_in, wg), (wu_in, wu), (wd_in, wd), (cotangent.at[section], cot),
+        ))
+    ]
+    for load in loads:
+        load.start()
+    barrier = pltpu.get_barrier_semaphore()
+    for k in range(1, ctx_count):
+        pl.semaphore_signal(
+            barrier, 1, device_id=(section, row, lax.rem(ctx + k, ctx_count)), device_id_type=MESH
+        )
+    pl.semaphore_wait(barrier, ctx_count - 1)
+
+    lane = lax.broadcasted_iota(jnp.int32, (tokens, LANES), 1)
+    lower = lane < HEAD_DIM
+    turn_up = (lane % HEAD_DIM) < HEAD_DIM // 2
+
+    key_seg = jnp.broadcast_to(segments[section].astype(jnp.float32), (LANES, size.length)).T
+    key_pos = lax.broadcasted_iota(jnp.int32, (size.length, LANES), 0)
+    query_seg = segments[section, :, pl.ds(pl.multiple_of(ctx * tokens, tokens), tokens)]
+    for part in range(tokens // LANES):
+        cols = slice(part * LANES, (part + 1) * LANES)
+        query_pos = (
+            lax.broadcasted_iota(jnp.int32, (size.length, LANES), 1) + part * LANES + ctx * tokens
+        )
+        allowed = (key_seg == query_seg[:, cols].astype(jnp.float32)) & (key_pos <= query_pos)
+        bias[:, cols] = jnp.where(allowed, 0.0, mask_floor)
+
+    for k in range(1, ctx_count):
+        @pl.when(ctx + k < ctx_count)
+        def _():
+            rows = pl.ds(pl.multiple_of((ctx + k) * tokens, tokens), tokens)
+            for app in range(2):
+                kv[app, :, rows, :] = jnp.zeros((groups, tokens, LANES), low_type)
+
+    own_rows = pl.ds(pl.multiple_of(ctx * tokens, tokens), tokens)
+
+    def kv_copy(app, g, k):
+        return pltpu.make_async_remote_copy(
+            kv.at[app, g, own_rows], kv.at[app, g, own_rows],
+            sem_k.at[0, app, g, k - 1], sem_k.at[1, app, g, k - 1],
+            device_id=(section, row, jnp.minimum(ctx + k, ctx_count - 1)), device_id_type=MESH,
+        )
+
+    def grad_copy(app, g, k):
+        owner = jnp.maximum(ctx - k, 0)
+        rows = pl.ds(pl.multiple_of(owner * tokens, tokens), tokens)
+        return pltpu.make_async_remote_copy(
+            kv_send.at[app, g, rows], kv_recv.at[app, k - 1, g],
+            sem_d.at[0, app, g, k - 1], sem_d.at[1, app, g, k - 1],
+            device_id=(section, row, owner), device_id_type=MESH,
+        )
+
+    def norm(values):
+        return lax.rsqrt(jnp.mean(values * values, -1, keepdims=True) + epsilon)
+
+    def norm_back(values, gain_vec, grad_normed):
+        inverse = norm(values)
+        weighted = grad_normed * gain_vec
+        gain_grad = jnp.sum(grad_normed * values * inverse, axis=0, keepdims=True)
+        cubed = inverse * inverse * inverse
+        return inverse * weighted - values * cubed * jnp.mean(
+            weighted * values, -1, keepdims=True
+        ), gain_grad
+
+    def rope_lanes(tile, sine):
+        partner = jnp.where(turn_up, pltpu.roll(tile, 96, 1), pltpu.roll(tile, 32, 1))
+        return tile * cos_kv[...] + partner * sine
+
+    def rope_rows(values, sign):
+        half = HEAD_DIM // 2
+        out = []
+        for start in range(0, values.shape[0], HEAD_DIM):
+            former = values[start : start + half]
+            latter = values[start + half : start + HEAD_DIM]
+            out.append(former * cos_q[...] - latter * (sign * sin_q[...]))
+            out.append(latter * cos_q[...] + former * (sign * sin_q[...]))
+        return jnp.concatenate(out, 0)
+
+    def half_tiles(values):
+        spare = (-values.shape[1]) % LANES
+        if spare:
+            values = jnp.concatenate([values, jnp.zeros((values.shape[0], spare), values.dtype)], 1)
+        out = []
+        for g in range(groups):
+            tile = values[:, g // 2 * LANES : (g // 2 + 1) * LANES]
+            turned = pltpu.roll(tile, HEAD_DIM, 1)
+            out.append((tile, turned) if g % 2 == 0 else (turned, tile))
+        return out
+
+    def app_tokens(app):
+        return slice(app * tokens, (app + 1) * tokens)
+
+    def forward(app):
+        x = xin[app].astype(jnp.float32)
+        normed = (x * norm(x) * gain_attn[...]).astype(low_type)
+        if app == 0:
+            loads[1].wait()
+            loads[2].wait()
+        keys = half_tiles(dot(normed, wk[...]))
+        values = half_tiles(dot(normed, wv[...]))
+        for g in range(groups):
+            tile = rope_lanes(jnp.where(lower, keys[g][0], values[g][1]), sin_kv[...])
+            kv[app, g, own_rows, :] = tile.astype(low_type)
+            for k in range(1, ctx_count):
+                @pl.when(ctx + k < ctx_count)
+                def _():
+                    kv_copy(app, g, k).start()
+        x_attn[0, :, app_tokens(app)] = normed.T
+        if app == 0:
+            loads[3].wait()
+        for start in range(0, size.width, LANES):
+            stop = min(start + LANES, size.width)
+            tile = dot(normed, wq[:, start:stop])
+            q_t[app, start:stop, :] = rope_rows(tile.T, 1.0).astype(low_type)
+
+        def heads(g, carry):
+            for k in range(1, ctx_count):
+                @pl.when(ctx - k >= 0)
+                def _():
+                    kv_copy(app, g, k).wait_recv()
+            kv_g = kv[app, g]
+            v_t = kv_g.T[HEAD_DIM:]
+            for h in range(group):
+                rows = pl.ds(pl.multiple_of((g * group + h) * HEAD_DIM, HEAD_DIM), HEAD_DIM)
+                query = q_t[app, rows, :]
+                query = jnp.concatenate([query, jnp.zeros_like(query)], 0)
+                scores = dot(kv_g, query) * score_unit + bias[...]
+                largest = jnp.max(scores, 0, keepdims=True)
+                weights = jnp.exp2(scores - largest)
+                total = jnp.sum(weights, 0, keepdims=True)
+                out = dot(v_t, weights.astype(low_type)) / total
+                lse[app, g, h : h + 1, :] = largest + jnp.log(total) * (1.0 / math.log(2.0))
+                o_t[app, rows, :] = out
+                x_attn[1, rows, app_tokens(app)] = out.astype(low_type)
+            return carry
+
+        lax.fori_loop(0, groups, heads, 0)
+        if app == 0:
+            loads[4].wait()
+        x = xin[app].astype(jnp.float32)
+        middle = x + dot(x_attn[1, :, app_tokens(app)], wo[...], (0, 0))
+        mid[app] = middle
+        ffn = (middle * norm(middle) * gain_ffn[...]).astype(low_type)
+        n2_t[:, app_tokens(app)] = ffn.T
+        if app == 0:
+            for load in loads[5:8]:
+                load.wait()
+        accum[...] = middle
+
+        def chunk(i, carry):
+            cols = pl.ds(pl.multiple_of(i * size.step, size.step), size.step)
+            gate = dot(ffn, wg[:, cols])
+            upward = dot(ffn, wu[:, cols])
+            inner = (gate / (1.0 + jnp.exp(-gate)) * upward).astype(low_type)
+            d_ffn[0, app_tokens(app), cols] = gate.astype(low_type)
+            d_ffn[1, app_tokens(app), cols] = upward.astype(low_type)
+            inner_t[cols, app_tokens(app)] = inner.T
+            accum[...] += dot(inner, wd[cols, :])
+            return carry
+
+        lax.fori_loop(0, size.hidden // size.step, chunk, 0)
+        acts[app] = accum[...].astype(low_type)
+        if app == 0:
+            xin[1] = accum[...].astype(low_type)
+
+    def backward(app, grad_low):
+        d_out[app_tokens(app), : size.width] = grad_low
+        d_out[app_tokens(app), size.width :] = jnp.zeros(
+            (tokens, d_out.shape[1] - size.width), low_type
+        )
+        accum[...] = jnp.zeros_like(accum)
+
+        def chunk(i, carry):
+            cols = pl.ds(pl.multiple_of(i * size.step, size.step), size.step)
+            gate = d_ffn[0, app_tokens(app), cols].astype(jnp.float32)
+            upward = d_ffn[1, app_tokens(app), cols].astype(jnp.float32)
+            grad_inner = dot(d_out[app_tokens(app), : size.width], wd[cols, :], (1, 1))
+            sigmoid = 1.0 / (1.0 + jnp.exp(-gate))
+            scaled = grad_inner * sigmoid
+            grad_gate = (scaled * upward * (1.0 + gate * (1.0 - sigmoid))).astype(low_type)
+            grad_up = (scaled * gate).astype(low_type)
+            d_ffn[0, app_tokens(app), cols] = grad_gate
+            d_ffn[1, app_tokens(app), cols] = grad_up
+            accum[...] += dot(grad_gate, wg[:, cols], (1, 1)) + dot(grad_up, wu[:, cols], (1, 1))
+            return carry
+
+        lax.fori_loop(0, size.hidden // size.step, chunk, 0)
+        grad, gain_grad = norm_back(mid[app], gain_ffn[...], accum[...])
+        gain_sums[1:2] += gain_grad
+        dmid[...] = d_out[app_tokens(app), : size.width].astype(jnp.float32) + grad
+        branch = dmid[...].astype(low_type)
+        d_attn[1, app_tokens(app), : size.width] = branch
+        do_t[...] = dot(wo[...], branch, (1, 1)).astype(low_type)
+
+        def heads(g, carry):
+            kv_g = kv[app, g]
+            k_t = kv_g.T[:HEAD_DIM]
+            total = jnp.zeros((size.length, LANES), jnp.float32)
+            for h in range(group):
+                rows = pl.ds(pl.multiple_of((g * group + h) * HEAD_DIM, HEAD_DIM), HEAD_DIM)
+                query, grad_head = q_t[app, rows, :], do_t[rows, :]
+                empty = jnp.zeros_like(query)
+                grad_pad = jnp.concatenate([empty, grad_head], 0)
+                scores = dot(kv_g, jnp.concatenate([query, empty], 0)) * score_unit + bias[...]
+                chances = jnp.exp2(scores - lse[app, g, h : h + 1, :])
+                delta = jnp.sum(
+                    grad_head.astype(jnp.float32) * o_t[app, rows, :], 0, keepdims=True
+                )
+                grad_scores = (chances * (dot(kv_g, grad_pad) - delta)).astype(low_type)
+                small = (query.astype(jnp.float32) * score_scale).astype(low_type)
+                total = total + dot(
+                    grad_scores, jnp.concatenate([small, empty], 0), (1, 1)
+                ) + dot(chances.astype(low_type), grad_pad, (1, 1))
+                dq_t[rows, :] = dot(k_t, grad_scores) * score_scale
+            kv_send[app, g] = total.astype(low_type)
+            for k in range(1, ctx_count):
+                @pl.when(ctx - k >= 0)
+                def _():
+                    grad_copy(app, g, k).start()
+            return carry
+
+        lax.fori_loop(0, groups, heads, 0)
+        for start in range(0, size.width, LANES):
+            stop = min(start + LANES, size.width)
+            tile = rope_rows(dq_t[start:stop, :], -1.0)
+            d_attn[0, app_tokens(app), start:stop] = tile.astype(low_type).T
+        d_attn[:, app_tokens(app), size.width :] = jnp.zeros(
+            (2, tokens, d_attn.shape[2] - size.width), low_type
+        )
+        turned = []
+        for g in range(groups):
+            tile = kv_send[app, g, own_rows, :].astype(jnp.float32)
+            for k in range(1, ctx_count):
+                @pl.when(ctx + k < ctx_count)
+                def _():
+                    grad_copy(app, g, k).wait_recv()
+                tile = tile + jnp.where(
+                    ctx + k < ctx_count, kv_recv[app, k - 1, g].astype(jnp.float32), 0.0
+                )
+            tile = rope_lanes(tile, -sin_kv[...])
+            turned.append((tile, pltpu.roll(tile, HEAD_DIM, 1)))
+        empty = jnp.zeros((tokens, LANES), jnp.float32)
+        pairs = []
+        for half in range(2):
+            pieces = [(one, other) if half == 0 else (other, one) for one, other in turned]
+            tiles = [jnp.where(lower, 0.0, pieces[0][1])]
+            for g in range(1, groups, 2):
+                tiles.append(jnp.where(lower, pieces[g][0], pieces[g + 1][1]))
+            for number, tile in enumerate(tiles):
+                d_pair[half, app_tokens(app), number * LANES : (number + 1) * LANES] = tile.astype(
+                    low_type
+                )
+            straight = [
+                jnp.where(lower, pieces[g][0], pieces[g + 1][1] if g + 1 < groups else empty)
+                for g in range(0, groups, 2)
+            ]
+            pairs.append(
+                jnp.concatenate(straight, 1)[:, : size.kv_width].astype(low_type)
+            )
+        grad_normed = (
+            dot(d_attn[0, app_tokens(app), : size.width], wq[...], (1, 1))
+            + dot(pairs[0], wk[...], (1, 1))
+            + dot(pairs[1], wv[...], (1, 1))
+        )
+        grad, gain_grad = norm_back(xin[app].astype(jnp.float32), gain_attn[...], grad_normed)
+        gain_sums[0:1] += gain_grad
+        return dmid[...] + grad
+
+    gain_sums[...] = jnp.zeros_like(gain_sums)
+    loads[0].wait()
+    forward(0)
+    forward(1)
+    loads[8].wait()
+    low = backward(1, cot[...]).astype(low_type)
+    grad_mid[...] = low
+    grad_in[...] = backward(0, low)
+
+    def drain(g, carry):
+        for app in range(2):
+            for k in range(1, ctx_count):
+                @pl.when(ctx + k < ctx_count)
+                def _():
+                    kv_copy(app, g, k).wait_send()
+
+                @pl.when(ctx - k >= 0)
+                def _():
+                    grad_copy(app, g, k).wait_send()
+        return carry
+
+    lax.fori_loop(0, groups, drain, 0)
+
+
+def run_block(size, plan, *operands):
+    tokens, width, hidden, groups = size.tokens, size.width, size.hidden, size.kv_heads
+    low, full = jnp.bfloat16, jnp.float32
+    wide, kv_wide = plan.width_tiles * LANES, (plan.pair_tiles - plan.width_tiles + 1) * LANES
+    both = 2 * tokens
+    vmem = pl.BlockSpec(memory_space=pltpu.VMEM)
+    far = pl.BlockSpec(memory_space=pl.ANY)
+    dma = pltpu.SemaphoreType.DMA
+    others = max(size.ctx - 1, 1)
+    shapes = [
+        ((2, tokens, width), low),
+        ((tokens, width), low),
+        ((tokens, width), full),
+        ((2, width, both), low),
+        ((width, both), low),
+        ((hidden, both), low),
+        ((2, both, wide), low),
+        ((2, both, kv_wide), low),
+        ((2, both, hidden), low),
+        ((both, wide), low),
+        ((2, width), full),
+    ]
+    scratch = [
+        ((width, width), low),
+        ((width, size.kv_width), low),
+        ((width, size.kv_width), low),
+        ((width, width), low),
+        ((width, hidden), low),
+        ((width, hidden), low),
+        ((hidden, width), low),
+        ((2, tokens, width), low),
+        ((tokens, width), low),
+        ((2, tokens, width), full),
+        ((2, width, tokens), low),
+        ((2, groups, size.length, LANES), low),
+        ((2, groups, size.length, LANES), low),
+        ((2, others, groups, tokens, LANES), low),
+        ((2, groups, 8, tokens), full),
+        ((2, width, tokens), full),
+        ((width, tokens), low),
+        ((width, tokens), full),
+        ((size.length, tokens), full),
+        ((tokens, width), full),
+        ((tokens, width), full),
+    ]
+    return pl.pallas_call(
+        functools.partial(block_kernel, size),
+        out_shape=[jax.ShapeDtypeStruct(*shape) for shape in shapes],
+        in_specs=[far, far] + [vmem] * 7 + [far] * 7,
+        out_specs=[vmem] * len(shapes),
+        scratch_shapes=[pltpu.VMEM(*shape) for shape in scratch] + [
+            dma((9,)), dma((2, 2, groups, others)), dma((2, 2, groups, others)),
+        ],
+        compiler_params=pltpu.CompilerParams(
+            collective_id=1, has_side_effects=True, vmem_limit_bytes=64 << 20
+        ),
+        cost_estimate=pl.CostEstimate(
+            flops=4 * 10**10, bytes_accessed=40 * 10**6, transcendentals=3 * 10**7
+        ),
+    )(*operands)
+
+
+def rotary(length):
+    half = HEAD_DIM // 2
+    frequency = 10000.0 ** (-2.0 * np.arange(half) / HEAD_DIM)
+    angles = np.arange(length)[:, None] * frequency[None, :]
+    cos, sine = np.cos(angles), np.sin(angles)
+    kept, none = np.ones((length, HEAD_DIM)), np.zeros((length, HEAD_DIM))
+    cos_kv = np.concatenate([cos, cos, kept], 1)
+    sin_kv = np.concatenate([-sine, sine, none], 1)
+    return [np.asarray(table, np.float32) for table in (cos, sine, cos_kv, sin_kv)]
+
+
+def plain_block(
+    plan, inputs, segment_ids, cotangent,
+    gain_attn, w_query, w_key, w_value, w_out, gain_ffn, w_gate, w_up, w_down,
 ):
     micro_count, row_count, tok_local, model_width = inputs.shape
     kv_width = w_key.shape[1]
@@ -626,6 +1012,113 @@
         tick_grads = (backward_sum_gain_attn, backward_sum_gain_ffn, factors)
         return grad_middle + grad_front, tick_grads
 
+    first_low, first_kept = forward(mine(inputs).astype(jnp.float32))
+    second_low, second_kept = forward(first_low.astype(jnp.float32))
+    grad_mid, second_grads = backward(mine(cotangent).astype(jnp.float32), second_kept)
+    grad_mid_low = grad_mid.astype(jnp.bfloat16)
+    grad_in, first_grads = backward(grad_mid_low.astype(jnp.float32), first_kept)
+    dp = plan.dp
+
+    def stacked(one, other):
+        return jnp.concatenate([one, other], 1).reshape(-1, one.shape[-1])
+
+    normed, attn, ffn, inner, d_query, d_pair, d_branch, d_gate, d_up, d_out = (
+        stacked(one, other) for one, other in zip(first_grads[2], second_grads[2])
+    )
+    tokens = normed.shape[0]
+
+    def sides(values, rows):
+        cut = values.reshape(tokens, dp, -1)
+        cut = jnp.pad(cut, ((0, 0), (0, 0), (0, rows - cut.shape[2])))
+        return cut.transpose(1, 2, 0)
+
+    halves = inner.reshape(tokens, dp, 2, -1)
+    inner_t = jnp.stack([sides(halves[:, :, h], plan.down_rows) for h in range(2)], 1)
+    spare = plan.width_tiles * LANES - model_width
+    gain_sums = jnp.stack([one + other for one, other in zip(first_grads[:2], second_grads[:2])])
+    factors = (
+        sides(ffn, plan.rows),
+        jnp.stack([d_gate, d_up]),
+        inner_t.reshape(2 * dp, plan.down_rows, tokens),
+        jnp.pad(d_out, ((0, 0), (0, spare))),
+        jnp.stack([sides(normed, plan.rows), sides(attn, plan.rows)]),
+        jnp.pad(jnp.stack([d_query, d_branch]), ((0, 0), (0, 0), (0, spare))),
+        jnp.pad(
+            jnp.stack([d_pair[:, :kv_width], d_pair[:, kv_width:]]),
+            ((0, 0), (0, 0), (LANES - spare, 0)),
+        ),
+    )
+    acts = (first_low, second_low)
+    return acts, (grad_in, grad_mid_low), gain_sums, factors
+
+
+def fused_block(
+    size, plan, inputs, segment_ids, cotangent,
+    gain_attn, w_query, w_key, w_value, w_out, gain_ffn, w_gate, w_up, w_down,
+):
+    tokens, width, dp = size.tokens, size.width, plan.dp
+    first_token = lax.axis_index("ctx") * tokens
+    cos_q, sin_q, cos_kv, sin_kv = (
+        lax.dynamic_slice_in_dim(jnp.asarray(table), first_token, tokens, 0)
+        for table in rotary(size.length)
+    )
+    (
+        acts, grad_mid, grad_in, x_attn, n2_t, inner_t, d_attn, d_pair, d_ffn, d_out, gain_sums
+    ) = run_block(
+        size, plan, inputs[:, 0], cotangent[:, 0], segment_ids, cos_q.T, sin_q.T, cos_kv, sin_kv,
+        gain_attn.astype(jnp.float32)[None], gain_ffn.astype(jnp.float32)[None],
+        w_query, w_key, w_value, w_out, w_gate, w_up, w_down,
+    )
+    factors = (
+        n2_t.reshape(dp, plan.rows, -1),
+        d_ffn,
+        inner_t.reshape(2 * dp, plan.down_rows, -1),
+        d_out,
+        x_attn.reshape(2, dp, plan.rows, -1),
+        d_attn,
+        d_pair,
+    )
+    return (acts[0][None], acts[1][None]), (grad_in[None], grad_mid[None]), gain_sums, factors
+
+
+def body(
+    inputs,
+    segment_ids,
+    cotangent,
+    gain_attn,
+    w_query,
+    w_key,
+    w_value,
+    w_out,
+    gain_ffn,
+    w_gate,
+    w_up,
+    w_down,
+):
+    micro_count, row_count, tok_local, model_width = inputs.shape
+    kv_width, hidden = w_key.shape[1], w_gate.shape[1]
+    assert micro_count == lax.axis_size("section")
+    on_first = lax.axis_index("section") == 0
+    plan = Plan(lax.axis_size("dp"), lax.axis_size("ctx"), model_width, hidden, kv_width)
+    dp = plan.dp
+    size = Block(tok_local, segment_ids.shape[2], model_width, hidden, kv_width, plan.ctx)
+    fits = (
+        row_count == 1
+        and size.length <= 1024
+        and tok_local % LANES == 0
+        and plan.rows * dp == model_width
+        and plan.down_rows * dp * 2 == hidden
+    )
+    run = functools.partial(fused_block, size) if fits else plain_block
+    acts, grads, gain_sums, factors = run(
+        plan, inputs, segment_ids, cotangent,
+        gain_attn, w_query, w_key, w_value, w_out, gain_ffn, w_gate, w_up, w_down,
+    )
+    extra = jnp.pad(
+        gain_sums.reshape(2, dp, -1), ((0, 0), (0, 0), (0, 16 * LANES - model_width // dp))
+    ).reshape(2, dp, 16, LANES)
+    summed = reduce_grads(plan, *factors, extra)
+
     def exchange(for_first, for_last):
         kept = jnp.where(on_first, for_first, for_last)
         sent = jnp.where(on_first, for_last, for_first)
@@ -633,53 +1126,6 @@
         return jnp.where(
             on_first, jnp.stack([kept, got]), jnp.stack([got, kept])
         )
-
-    first_low, first_kept = forward(mine(inputs).astype(jnp.float32))
-    second_low, second_kept = forward(first_low.astype(jnp.float32))
-    grad_mid, second_grads = backward(mine(cotangent).astype(jnp.float32), second_kept)
-    grad_mid_low = grad_mid.astype(jnp.bfloat16)
-    grad_in, first_grads = backward(grad_mid_low.astype(jnp.float32), first_kept)
-    plan = Plan(
-        lax.axis_size("dp"), lax.axis_size("ctx"), model_width, w_gate.shape[1], kv_width
-    )
-    dp = plan.dp
-
-    def stacked(one, other):
-        return jnp.concatenate([one, other], 1).reshape(-1, one.shape[-1])
-
-    normed, attn, ffn, inner, d_query, d_pair, d_branch, d_gate, d_up, d_out = (
-        stacked(one, other) for one, other in zip(first_grads[2], second_grads[2])
-    )
-    tokens = normed.shape[0]
-
-    def sides(values, rows):
-        cut = values.reshape(tokens, dp, -1)
-        cut = jnp.pad(cut, ((0, 0), (0, 0), (0, rows - cut.shape[2])))
-        return cut.transpose(1, 2, 0)
-
-    normed_t = sides(normed, plan.rows)
-    halves = inner.reshape(tokens, dp, 2, -1)
-    inner_t = jnp.stack([sides(halves[:, :, h], plan.down_rows) for h in range(2)])
-    wide = plan.width_tiles * LANES
-    spare = wide - model_width
-    extra = jnp.stack([
-        jnp.pad((one + other).reshape(dp, -1), ((0, 0), (0, 16 * LANES - model_width // dp)))
-        for one, other in zip(first_grads[:2], second_grads[:2])
-    ]).reshape(2, dp, 16, LANES)
-    summed = reduce_grads(
-        plan,
-        sides(ffn, plan.rows),
-        jnp.stack([d_gate, d_up]),
-        inner_t,
-        jnp.pad(d_out, ((0, 0), (0, spare))),
-        jnp.stack([normed_t, sides(attn, plan.rows)]),
-        jnp.pad(jnp.stack([d_query, d_branch]), ((0, 0), (0, 0), (0, spare))),
-        jnp.pad(
-            jnp.stack([d_pair[:, :kv_width], d_pair[:, kv_width:]]),
-            ((0, 0), (0, 0), (LANES - spare, 0)),
-        ),
-        extra,
-    )
 
     def tiles_of(kind):
         found = []
@@ -713,8 +1159,8 @@
         ffn_sum[1],
         down_sum.reshape(-1, model_width),
     )
-    activations = exchange(first_low, second_low)[None]
-    input_grads = exchange(grad_in.astype(jnp.bfloat16), grad_mid_low).astype(jnp.float32)[None]
+    activations = exchange(*acts)[None]
+    input_grads = exchange(grads[0].astype(jnp.bfloat16), grads[1]).astype(jnp.float32)[None]
     return (
         activations,
         input_grads,

time: 558 us -> 330 us (0.59)
  matrix products: 150 us -> 0 us
  Pallas kernels: 132 us -> 246 us
  waiting for transfers between devices: 69.7 us -> 0.01 us
  other arithmetic: 66.5 us -> 14.8 us
  local copies, waits for them, and re-layouts: 114 us -> 63 us
  between operations: 15.9 us -> 0.99 us
    dot_general x52 -> x0, matrix products: 150 us -> none  [the longest x4 26.1 us: fold_inner_step(): jnp.einsum('rkgcn,rnkd->rkgcd', weights.astype(jnp.bfloat16), value_part,...]
    pallas_call x0 -> x1, Pallas kernels: none -> 114 us  [run_block(): pl.pallas_call(functools.partial(block_kernel, size), out_shape=[jax.Shap...]
    all_gather x2 -> x0, waiting for transfers between devices: 52.1 us -> none  [forward(): arrived = lax.all_gather(packed, 'ctx', axis=1, tiled=True)]
    reduce_scatter x2 -> x0, waiting for transfers between devices: 17.6 us -> none  [backward(): lax.psum_scatter(grad_pair.astype(jnp.bfloat16), 'ctx', scatter_dimension...]
    another operation x15 -> x0, other arithmetic: 14 us -> none  [the longest x3 3.52 us: body(): jnp.stack([normed_t, sides(attn, plan.rows)])]
    slice x20 -> x0, local copies, waits for them, and re-layouts: 13.7 us -> none  [the longest x4 4.81 us: backward(): pair_share[..., :kv_width].reshape(row_count, tok_local, KV_HEADS, HEAD_DIM)]
    convert_element_type x17 -> x1, other arithmetic: 14.3 us -> 1.57 us  [body(): exchange(grads[0].astype(jnp.bfloat16), grads[1]).astype(jnp.float32)[None]]
    dynamic_update_slice x8 -> x0, local copies, waits for them, and re-layouts: 12 us -> none  [piece_inner_step(): lax.dynamic_update_slice_in_dim(local_pair, current + update, inside, 1)]
  transfers between devices with their start and end apart: 6 -> 2, of which waited for: 4 -> 0; matrix products, arithmetic and copies ran while one was open for 12% -> 16% of each run, Pallas kernels for 0% -> 41%
where the time goes in v3:
time: 330 us; the launch traced here: 325 us
  Pallas kernels  246 us (75%)
  local copies, waits for them, and re-layouts  63 us (19%)
  other arithmetic  14.8 us (4%)
    pallas_call x1, Pallas kernels, reduce_grads(): pl.pallas_call(functools.partial(reduce_kernel, plan), out_shape=jax.Shap...  132 us
    pallas_call x1, Pallas kernels, run_block(): pl.pallas_call(functools.partial(block_kernel, size), out_shape=[jax.Shap...  114 us
    unnamed x31, local copies, waits for them, and re-layouts  40.5 us
  transfers between devices with their start and end apart: 2, of which 0 were waited for; matrix products, arithmetic and copies ran while one was open for 16% of the time, Pallas kernels for 41%

profile of v3, /device:TPU:0, one launch (start us, length us, event | category | flops | bytes accessed | tf_op | source)
XLA Modules:
  0.0 325.0 jit_solution(181254106169912283)
XLA Ops:
  0.7 1.4 broadcast_in_dim.18
  3.3 2.2 copy.36.wk_in
  5.6 2.2 copy.37.wv_in
  9.1 1.3 copy.35
  10.4 7.9 %copy.38.wd_in = bf16[2560,960]{1,0:T(8,128)(2,1)} copy(bf16[2560,960]{0,1:T(8,128)(2,1)} %param.27) | data formatting | bytes 9830400 | tf_op args[11]
  18.3 1.4 dynamic-slice_bitcast_fusion
  19.7 1.7 constant_dynamic-slice_fusion
  21.4 114.0 %shard_map.239 = (bf16[2,256,960]{2,1,0:T(8,128)(2,1)}, bf16[256,960]{1,0:T(8,128)(2,1)}, f32[256,960]{1,0:T(8,128)}, bf16[2,960,512]{2,1,0:T(8,128)(2,1)}, bf16...) custom-call(bf16[2,256,960]{2,1,0:T(8,128)(2,1)} %bitcast.65, ...), custom_call_target="tpu_custom_call" | custom-call | flops 40000000000 | bytes 40000000 | tf_op jit(solution)/shard_map/pallas_call | solution.py:739
  135.5 2.4 select_bitcast_fusion.2
  140.2 131.7 %shard_map.240 = bf16[2,4,2464,128]{3,2,1,0:T(8,128)(2,1)} custom-call(bf16[4,240,512]{2,1,0:T(8,128)(2,1)} %bitcast.74, bf16[2,512,2560]{2,1,0:T(8,128)(2,1)} %get-tuple-element.26.ffn_dy, bf16[8,320,512]{2,1,0:T(8,128)(2,1)} %bitcast.72, bf16[512,1024]{1,0:T(8,128)(2,1)} %get-tuple-element.28.down_dy, bf16[2,4,240,512]{3,2,1,0:T(8,128)(2,1)} %bitcast.73, ...), custom_call_target="tpu_custom_call" | custom-call | flops 10000000000 | bytes 20000000 | tf_op jit(solution)/shard_map/pallas_call | solution.py:342
  273.1 1.4 fusion.1
  274.4 1.9 slice_dynamic-update-slice_fusion.4
  277.0 1.9 bitcast_convert_fusion
  278.9 1.9 slice_dynamic-update-slice_fusion.3
  280.8 1.9 slice_dynamic-update-slice_fusion.2
  282.7 1.9 slice_dynamic-update-slice_fusion.1
  284.6 2.1 slice_dynamic-update-slice_fusion
  286.7 1.6 convert_bitcast_fusion.1
  288.3 2.1 copy.39
  290.5 1.4 slice_bitcast_fusion
  291.9 2.0 convert_bitcast_fusion
  293.9 2.6 fusion.3
  297.0 3.2 copy.49
  300.2 2.5 copy.46
  302.7 2.5 copy.45
  305.1 3.2 copy.41
  308.3 3.2 copy.48
  311.5 3.2 copy.40
  314.7 3.2 copy.47
  318.8 1.5 maximum_select_fusion
  321.5 1.6 fusion
  323.1 1.8 copy.44
  (33 shorter events, 9.5 us)
Async XLA Ops:
  0.6 7.2 %copy-start.3 = (bf16[2,1,256,960]{2,3,1,0:T(8,128)(2,1)S(1)}, bf16[2,1,256,960]{2,3,1,0:T(8,128)(2,1)}, u32[]{:S(2)}) copy-start(bf16[2,1,256,960]{2,3,1,0:T(8,128)(2,1)} %param.16) | copy-start | bytes 2949124
  0.7 8.5 %copy-start.4 = (bf16[2,1,256,960]{2,3,1,0:T(8,128)(2,1)S(1)}, bf16[2,1,256,960]{2,3,1,0:T(8,128)(2,1)}, u32[]{:S(2)}) copy-start(bf16[2,1,256,960]{2,3,1,0:T(8,128)(2,1)} %param.18) | copy-start | bytes 2949124
  135.5 2.4 copy-start.2
  135.5 2.4 copy-start.5
  135.5 3.9 %copy-start.6 = (f32[2,960]{1,0:T(2,128)S(1)}, f32[2,960]{1,0:T(2,128)}, u32[]{:S(2)}) copy-start(f32[2,960]{1,0:T(2,128)} %get-tuple-element.32) | copy-start | bytes 23044
  137.8 180.9 %collective-permute-start = (bf16[1,256,960]{2,1,0:T(8,128)(2,1)}, bf16[1,256,960]{2,1,0:T(8,128)(2,1)}, u32[]{:S(2)}, u32[]{:S(2)}) collective-permute-start(bf16[1,256,960]{2,1,0:T(8,128)(2,1)} %get-tuple-element.70), channel_id=1, source_target_pairs={{0,16},{16,0},{1,17},{17,1},{2,18},{18,2},{3,19},{19,3},{4,20},{20... | collective-permute-start | bytes 1474568 | tf_op jit(solution)/shard_map/ppermute | solution.py:1125
  138.9 182.6 %collective-permute-start.1 = (bf16[1,256,960]{2,1,0:T(8,128)(2,1)}, bf16[1,256,960]{2,1,0:T(8,128)(2,1)}, u32[]{:S(2)}, u32[]{:S(2)}) collective-permute-start(bf16[1,256,960]{2,1,0:T(8,128)(2,1)} %get-tuple-element.68), channel_id=1, source_target_pairs={{0,16},{16,0},{1,17},{17,1},{2,18},{18,2},{3,19},{19,3},{4,20},{20... | collective-permute-start | bytes 1474568 | tf_op jit(solution)/shard_map/ppermute | solution.py:1125
  314.7 4.1 %copy-start = (bf16[1,1,1,256,960]{4,3,2,1,0:T(8,128)(2,1)S(1)}, bf16[1,1,1,256,960]{4,3,2,1,0:T(8,128)(2,1)}, u32[]{:S(2)}) copy-start(bf16[1,1,1,256,960]{4,3,2,1,0:T(8,128)(2,1)} %get-tuple-element.69) | copy-start | bytes 1474564
  318.8 2.8 copy-start.1

commit v4 on v3

--- a/solution.py
+++ b/solution.py
@@ -71,15 +71,17 @@
         self.cx = 1 << (ctx.bit_length() // 2) if ctx & (ctx - 1) == 0 else ctx
         self.cy = ctx // self.cx
         self.low = max(dp // 2, 1)
+        self.shard = width // dp
         self.rows = up_to(width // dp, 16)
-        self.down_rows = up_to(hidden // dp // 2, 16)
+        self.down_rows = up_to(width // 2, 16)
+        self.down_tiles = up_to(hidden // dp, LANES) // LANES
         self.up_tiles = hidden // LANES
         self.width_tiles = up_to(width, LANES) // LANES
         self.pair_tiles = (width + kv_width) // LANES
         chunks = []
         for kind, count, rows, step in (
             ("ffn", self.up_tiles, self.rows, 4),
-            ("down", self.width_tiles, self.down_rows, 4),
+            ("down", self.down_tiles, self.down_rows, 2),
             ("attn", self.width_tiles - 1, self.rows, 4),
             ("mixed", self.pair_tiles - self.width_tiles + 1, self.rows, 4),
         ):
@@ -104,8 +106,8 @@
 
 
 def reduce_kernel(
-    plan, ffn_x, ffn_dy, down_x, down_dy, attn_x, attn_dy, pair_dy, extra, out,
-    sent, partner, own, rx1, ry1, rx2, ry2, rz,
+    plan, ffn_x, ffn_dy, down_x, down_dy, attn_x, attn_dy, pair_dy, gain_sums, out,
+    extra, sent, partner, own, rx1, ry1, rx2, ry2, rz,
     sem_ps, sem_pr, sem_x1, sem_y1, sem_x2, sem_y2, sem_z, sem_g, sem_f,
 ):
     dp, cx, cy, low = plan.dp, plan.cx, plan.cy, plan.low
@@ -128,6 +130,14 @@
         pl.semaphore_signal(barrier, 1, device_id=friend, device_id_type=MESH)
     pl.semaphore_wait(barrier, len(friends))
 
+    for half in range(2):
+        for j in range(dp):
+            for number in range(-(-plan.shard // LANES)):
+                start = j * plan.shard + number * LANES
+                extra[half, j, number : number + 1, :] = gain_sums[
+                    half : half + 1, start : start + LANES
+                ]
+
     def remote(source, target, sems, place, device):
         return pltpu.make_async_remote_copy(
             source, target, sems[0].at[place], sems[1].at[place], device_id=device, device_id_type=MESH
@@ -143,8 +153,9 @@
                     preferred_element_type=jnp.float32,
                 )
             elif kind == "down":
+                first = pl.multiple_of(j * (plan.down_tiles * LANES) + start * LANES, LANES)
                 value = jnp.dot(
-                    down_x[2 * j + half], down_dy[:, start * LANES : (start + tiles) * LANES],
+                    down_x[half], down_dy[:, pl.ds(first, tiles * LANES)],
                     preferred_element_type=jnp.float32,
                 )
             elif kind == "attn":
@@ -345,6 +356,7 @@
         in_specs=[pl.BlockSpec(memory_space=pltpu.VMEM)] * len(operands),
         out_specs=pl.BlockSpec(memory_space=pltpu.VMEM),
         scratch_shapes=[
+            pltpu.VMEM((2, dp, 16, LANES), jnp.float32),
             pltpu.VMEM((2, dp, ctx, widest, LANES), low_type),
             pltpu.VMEM((dp, ctx, total, LANES), low_type),
             pltpu.VMEM((dp, plan.cy, plan.cx, total, LANES), low_type),
@@ -385,55 +397,60 @@
     )
 
 
+def fold_rows(values, combine):
+    return combine(values.reshape(values.shape[0] // 8, 8, values.shape[1]), 0)
+
+
 def block_kernel(
-    size, inputs, cotangent, segments, cos_q, sin_q, cos_kv, sin_kv, gain_attn, gain_ffn,
+    size, inputs, cotangent, segments, cos_in, sin_in, gains,
     wq_in, wk_in, wv_in, wo_in, wg_in, wu_in, wd_in,
-    acts, grad_mid, grad_in, x_attn, n2_t, inner_t, d_attn, d_pair, d_ffn, d_out, gain_sums,
-    wq, wk, wv, wo, wg, wu, wd, xin, cot, mid, q_t, kv, kv_send, kv_recv, lse, o_t, do_t, dq_t, bias, accum, dmid,
-    sem_w, sem_k, sem_d,
+    acts, grads, x_attn, n2_t, df_t, inner, d_attn, d_pair, d_ffn, gain_sums,
+    wq, wk, wv, wo, wg, wu, wd, cos_q, sin_q, columns, xin, cot, last, grad_stage, mid, q_t,
+    kv, kv_send, kv_recv, lse, do_t, bias, accum, dmid, natural, scores, chances, grad_scores,
+    sem_w, sem_k, sem_d, sem_e,
 ):
     tokens, ctx_count, groups, group = size.tokens, size.ctx, size.kv_heads, size.group
-    low_type = jnp.bfloat16
+    width, low_type, full = size.width, jnp.bfloat16, jnp.float32
     section, row, ctx = (lax.axis_index(name) for name in ("section", "dp", "ctx"))
+    mate = (1 - section, row, ctx)
+    own_rows = pl.ds(pl.multiple_of(ctx * tokens, tokens), tokens)
     loads = [
         pltpu.make_async_copy(source, target, sem_w.at[number])
         for number, (source, target) in enumerate((
-            (inputs.at[section], xin.at[0]), (wk_in, wk), (wv_in, wv), (wq_in, wq), (wo_in, wo),
+            (inputs.at[section], xin.at[0]), (cos_in.at[:, own_rows], cos_q),
+            (sin_in.at[:, own_rows], sin_q), (wk_in, wk), (wv_in, wv), (wq_in, wq), (wo_in, wo),
             (wg_in, wg), (wu_in, wu), (wd_in, wd), (cotangent.at[section], cot),
         ))
     ]
     for load in loads:
         load.start()
     barrier = pltpu.get_barrier_semaphore()
-    for k in range(1, ctx_count):
-        pl.semaphore_signal(
-            barrier, 1, device_id=(section, row, lax.rem(ctx + k, ctx_count)), device_id_type=MESH
-        )
-    pl.semaphore_wait(barrier, ctx_count - 1)
-
-    lane = lax.broadcasted_iota(jnp.int32, (tokens, LANES), 1)
-    lower = lane < HEAD_DIM
-    turn_up = (lane % HEAD_DIM) < HEAD_DIM // 2
-
-    key_seg = jnp.broadcast_to(segments[section].astype(jnp.float32), (LANES, size.length)).T
-    key_pos = lax.broadcasted_iota(jnp.int32, (size.length, LANES), 0)
-    query_seg = segments[section, :, pl.ds(pl.multiple_of(ctx * tokens, tokens), tokens)]
-    for part in range(tokens // LANES):
-        cols = slice(part * LANES, (part + 1) * LANES)
-        query_pos = (
-            lax.broadcasted_iota(jnp.int32, (size.length, LANES), 1) + part * LANES + ctx * tokens
-        )
-        allowed = (key_seg == query_seg[:, cols].astype(jnp.float32)) & (key_pos <= query_pos)
-        bias[:, cols] = jnp.where(allowed, 0.0, mask_floor)
-
+    friends = [mate] + [(section, row, lax.rem(ctx + k, ctx_count)) for k in range(1, ctx_count)]
+    for friend in friends:
+        pl.semaphore_signal(barrier, 1, device_id=friend, device_id_type=MESH)
+
+    for which in range(2):
+        for start in range(0, width, LANES):
+            rows = min(LANES, width - start)
+            tile = jnp.broadcast_to(gains[which : which + 1, start : start + LANES], (LANES, LANES))
+            columns[which, start : start + rows, :] = tile.T[:rows]
+    query_seg = segments[section, :, own_rows].astype(full)
+    query_pos = lax.broadcasted_iota(jnp.int32, (1, tokens), 1) + ctx * tokens
+    for start in range(0, size.length, LANES):
+        key_seg = jnp.broadcast_to(
+            segments[section, :, start : start + LANES].astype(full), (LANES, LANES)
+        ).T
+        key_pos = lax.broadcasted_iota(jnp.int32, (LANES, tokens), 0) + start
+        key_seg = jnp.concatenate([key_seg] * (tokens // LANES), 1)
+        allowed = (key_seg == query_seg) & (key_pos <= query_pos)
+        bias[start : start + LANES, :] = jnp.where(allowed, 0.0, mask_floor)
     for k in range(1, ctx_count):
         @pl.when(ctx + k < ctx_count)
         def _():
             rows = pl.ds(pl.multiple_of((ctx + k) * tokens, tokens), tokens)
             for app in range(2):
                 kv[app, :, rows, :] = jnp.zeros((groups, tokens, LANES), low_type)
-
-    own_rows = pl.ds(pl.multiple_of(ctx * tokens, tokens), tokens)
+    pl.semaphore_wait(barrier, len(friends))
 
     def kv_copy(app, g, k):
         return pltpu.make_async_remote_copy(
@@ -451,169 +468,199 @@
             device_id=(section, row, owner), device_id_type=MESH,
         )
 
+    act_copies = [
+        pltpu.make_async_remote_copy(
+            source, acts.at[section], sem_e.at[0], sem_e.at[1], device_id=mate, device_id_type=MESH
+        )
+        for source in (xin.at[1], last)
+    ]
+    back_copy = pltpu.make_async_remote_copy(
+        grad_stage, grads.at[section], sem_e.at[2], sem_e.at[3], device_id=mate, device_id_type=MESH
+    )
+
+    def wide(which):
+        return jnp.concatenate([columns[which]] * (tokens // LANES), 1)
+
     def norm(values):
-        return lax.rsqrt(jnp.mean(values * values, -1, keepdims=True) + epsilon)
-
-    def norm_back(values, gain_vec, grad_normed):
+        return lax.rsqrt(jnp.mean(values * values, 0, keepdims=True) + epsilon)
+
+    def norm_back(values, which, grad_normed):
         inverse = norm(values)
-        weighted = grad_normed * gain_vec
-        gain_grad = jnp.sum(grad_normed * values * inverse, axis=0, keepdims=True)
+        product = grad_normed * values * inverse
+        folded = product[:, :LANES]
+        for start in range(LANES, tokens, LANES):
+            folded = folded + product[:, start : start + LANES]
+        for start in range(0, width, LANES):
+            stop = min(start + LANES, width)
+            part = folded[start:stop]
+            if stop - start < LANES:
+                part = jnp.concatenate([part, jnp.zeros((LANES - stop + start, LANES), full)], 0)
+            gain_sums[which : which + 1, start : start + LANES] += jnp.sum(part.T, 0, keepdims=True)
+        weighted = grad_normed * wide(which)
         cubed = inverse * inverse * inverse
-        return inverse * weighted - values * cubed * jnp.mean(
-            weighted * values, -1, keepdims=True
-        ), gain_grad
-
-    def rope_lanes(tile, sine):
-        partner = jnp.where(turn_up, pltpu.roll(tile, 96, 1), pltpu.roll(tile, 32, 1))
-        return tile * cos_kv[...] + partner * sine
-
-    def rope_rows(values, sign):
+        return inverse * weighted - values * (
+            cubed * jnp.mean(weighted * values, 0, keepdims=True)
+        )
+
+    def rope(values, sign):
         half = HEAD_DIM // 2
+        cos, sine = cos_q[...], sin_q[...] * sign
         out = []
         for start in range(0, values.shape[0], HEAD_DIM):
             former = values[start : start + half]
             latter = values[start + half : start + HEAD_DIM]
-            out.append(former * cos_q[...] - latter * (sign * sin_q[...]))
-            out.append(latter * cos_q[...] + former * (sign * sin_q[...]))
+            out += [former * cos - latter * sine, latter * cos + former * sine]
         return jnp.concatenate(out, 0)
-
-    def half_tiles(values):
-        spare = (-values.shape[1]) % LANES
-        if spare:
-            values = jnp.concatenate([values, jnp.zeros((values.shape[0], spare), values.dtype)], 1)
-        out = []
-        for g in range(groups):
-            tile = values[:, g // 2 * LANES : (g // 2 + 1) * LANES]
-            turned = pltpu.roll(tile, HEAD_DIM, 1)
-            out.append((tile, turned) if g % 2 == 0 else (turned, tile))
-        return out
 
     def app_tokens(app):
         return slice(app * tokens, (app + 1) * tokens)
 
+    def head_rows(g, h):
+        return pl.ds(pl.multiple_of((g * group + h) * HEAD_DIM, HEAD_DIM), HEAD_DIM)
+
     def forward(app):
-        x = xin[app].astype(jnp.float32)
-        normed = (x * norm(x) * gain_attn[...]).astype(low_type)
+        x = xin[app].astype(full)
+        normed = (x * norm(x) * wide(0)).astype(low_type)
+        x_attn[0, :, app_tokens(app)] = normed
         if app == 0:
-            loads[1].wait()
-            loads[2].wait()
-        keys = half_tiles(dot(normed, wk[...]))
-        values = half_tiles(dot(normed, wv[...]))
+            for load in loads[1:5]:
+                load.wait()
+        keys = rope(dot(wk[...], normed), 1.0).astype(low_type)
+        values = dot(wv[...], normed).astype(low_type)
         for g in range(groups):
-            tile = rope_lanes(jnp.where(lower, keys[g][0], values[g][1]), sin_kv[...])
-            kv[app, g, own_rows, :] = tile.astype(low_type)
+            piece = slice(g * HEAD_DIM, (g + 1) * HEAD_DIM)
+            kv[app, g, own_rows, :] = jnp.concatenate([keys[piece], values[piece]], 0).T
             for k in range(1, ctx_count):
                 @pl.when(ctx + k < ctx_count)
                 def _():
                     kv_copy(app, g, k).start()
-        x_attn[0, :, app_tokens(app)] = normed.T
         if app == 0:
-            loads[3].wait()
-        for start in range(0, size.width, LANES):
-            stop = min(start + LANES, size.width)
-            tile = dot(normed, wq[:, start:stop])
-            q_t[app, start:stop, :] = rope_rows(tile.T, 1.0).astype(low_type)
+            loads[5].wait()
+        for start in range(0, width, 2 * LANES):
+            stop = min(start + 2 * LANES, width)
+            tile = dot(wq[:, start:stop], normed, (0, 0))
+            q_t[app, start:stop, :] = rope(tile, 1.0).astype(low_type)
 
         def heads(g, carry):
             for k in range(1, ctx_count):
                 @pl.when(ctx - k >= 0)
                 def _():
                     kv_copy(app, g, k).wait_recv()
-            kv_g = kv[app, g]
-            v_t = kv_g.T[HEAD_DIM:]
+            v_t = kv[app, g].T[HEAD_DIM:]
             for h in range(group):
-                rows = pl.ds(pl.multiple_of((g * group + h) * HEAD_DIM, HEAD_DIM), HEAD_DIM)
-                query = q_t[app, rows, :]
+                query = q_t[app, head_rows(g, h), :]
                 query = jnp.concatenate([query, jnp.zeros_like(query)], 0)
-                scores = dot(kv_g, query) * score_unit + bias[...]
-                largest = jnp.max(scores, 0, keepdims=True)
-                weights = jnp.exp2(scores - largest)
-                total = jnp.sum(weights, 0, keepdims=True)
-                out = dot(v_t, weights.astype(low_type)) / total
+                largest = None
+                for start in range(0, size.length, 256):
+                    keys_at = slice(start, start + 256)
+                    part = dot(kv[app, g, keys_at, :], query) * score_unit + bias[keys_at, :]
+                    scores[h, keys_at, :] = part
+                    most = fold_rows(part, jnp.max)
+                    largest = most if largest is None else jnp.maximum(largest, most)
+                largest = jnp.max(largest, 0, keepdims=True)
+                total = jnp.zeros((8, tokens), full)
+                for start in range(0, size.length, 64):
+                    keys_at = slice(start, start + 64)
+                    weights = jnp.exp2(scores[h, keys_at, :] - largest)
+                    total = total + fold_rows(weights, jnp.sum)
+                    chances[keys_at, h * tokens : (h + 1) * tokens] = weights.astype(low_type)
+                total = jnp.sum(total, 0, keepdims=True)
+                out = dot(v_t, chances[:, h * tokens : (h + 1) * tokens]) / total
                 lse[app, g, h : h + 1, :] = largest + jnp.log(total) * (1.0 / math.log(2.0))
-                o_t[app, rows, :] = out
-                x_attn[1, rows, app_tokens(app)] = out.astype(low_type)
+                x_attn[1, head_rows(g, h), app_tokens(app)] = out.astype(low_type)
             return carry
 
         lax.fori_loop(0, groups, heads, 0)
         if app == 0:
-            loads[4].wait()
-        x = xin[app].astype(jnp.float32)
-        middle = x + dot(x_attn[1, :, app_tokens(app)], wo[...], (0, 0))
+            loads[6].wait()
+        middle = xin[app].astype(full) + dot(wo[...], x_attn[1, :, app_tokens(app)], (0, 0))
         mid[app] = middle
-        ffn = (middle * norm(middle) * gain_ffn[...]).astype(low_type)
-        n2_t[:, app_tokens(app)] = ffn.T
+        ffn = (middle * norm(middle) * wide(1)).astype(low_type)
+        n2_t[:, app_tokens(app)] = ffn
+        natural[...] = ffn.T
         if app == 0:
-            for load in loads[5:8]:
+            for load in loads[7:10]:
                 load.wait()
         accum[...] = middle
 
         def chunk(i, carry):
             cols = pl.ds(pl.multiple_of(i * size.step, size.step), size.step)
-            gate = dot(ffn, wg[:, cols])
-            upward = dot(ffn, wu[:, cols])
-            inner = (gate / (1.0 + jnp.exp(-gate)) * upward).astype(low_type)
+            gate = dot(natural[...], wg[:, cols])
+            upward = dot(natural[...], wu[:, cols])
+            hidden = (gate / (1.0 + jnp.exp(-gate)) * upward).astype(low_type)
             d_ffn[0, app_tokens(app), cols] = gate.astype(low_type)
             d_ffn[1, app_tokens(app), cols] = upward.astype(low_type)
-            inner_t[cols, app_tokens(app)] = inner.T
-            accum[...] += dot(inner, wd[cols, :])
+            inner[app_tokens(app), cols] = hidden
+            accum[...] += dot(wd[:, cols], hidden, (1, 1))
             return carry
 
         lax.fori_loop(0, size.hidden // size.step, chunk, 0)
-        acts[app] = accum[...].astype(low_type)
+        output = accum[...].astype(low_type)
         if app == 0:
-            xin[1] = accum[...].astype(low_type)
+            xin[1] = output
+        else:
+            last[...] = output
+
+        @pl.when(section == app)
+        def _():
+            acts[section] = output
+
+        @pl.when(section != app)
+        def _():
+            act_copies[app].start()
 
     def backward(app, grad_low):
-        d_out[app_tokens(app), : size.width] = grad_low
-        d_out[app_tokens(app), size.width :] = jnp.zeros(
-            (tokens, d_out.shape[1] - size.width), low_type
-        )
+        df_t[:, app_tokens(app)] = grad_low
+        natural[...] = grad_low.T
         accum[...] = jnp.zeros_like(accum)
 
         def chunk(i, carry):
             cols = pl.ds(pl.multiple_of(i * size.step, size.step), size.step)
-            gate = d_ffn[0, app_tokens(app), cols].astype(jnp.float32)
-            upward = d_ffn[1, app_tokens(app), cols].astype(jnp.float32)
-            grad_inner = dot(d_out[app_tokens(app), : size.width], wd[cols, :], (1, 1))
+            gate = d_ffn[0, app_tokens(app), cols].astype(full)
+            upward = d_ffn[1, app_tokens(app), cols].astype(full)
             sigmoid = 1.0 / (1.0 + jnp.exp(-gate))
-            scaled = grad_inner * sigmoid
+            scaled = dot(natural[...], wd[:, cols]) * sigmoid
             grad_gate = (scaled * upward * (1.0 + gate * (1.0 - sigmoid))).astype(low_type)
             grad_up = (scaled * gate).astype(low_type)
             d_ffn[0, app_tokens(app), cols] = grad_gate
             d_ffn[1, app_tokens(app), cols] = grad_up
-            accum[...] += dot(grad_gate, wg[:, cols], (1, 1)) + dot(grad_up, wu[:, cols], (1, 1))
+            accum[...] += dot(wg[:, cols], grad_gate, (1, 1)) + dot(wu[:, cols], grad_up, (1, 1))
             return carry
 
         lax.fori_loop(0, size.hidden // size.step, chunk, 0)
-        grad, gain_grad = norm_back(mid[app], gain_ffn[...], accum[...])
-        gain_sums[1:2] += gain_grad
-        dmid[...] = d_out[app_tokens(app), : size.width].astype(jnp.float32) + grad
-        branch = dmid[...].astype(low_type)
-        d_attn[1, app_tokens(app), : size.width] = branch
-        do_t[...] = dot(wo[...], branch, (1, 1)).astype(low_type)
+        grad_middle = grad_low.astype(full) + norm_back(mid[app], 1, accum[...])
+        dmid[...] = grad_middle
+        branch = grad_middle.astype(low_type)
+        d_attn[1, app_tokens(app), :width] = branch.T
+        do_t[...] = dot(wo[...], branch).astype(low_type)
 
         def heads(g, carry):
-            kv_g = kv[app, g]
-            k_t = kv_g.T[:HEAD_DIM]
-            total = jnp.zeros((size.length, LANES), jnp.float32)
+            k_t = kv[app, g].T[:HEAD_DIM]
+            sides = []
             for h in range(group):
-                rows = pl.ds(pl.multiple_of((g * group + h) * HEAD_DIM, HEAD_DIM), HEAD_DIM)
+                rows, cols = head_rows(g, h), slice(h * tokens, (h + 1) * tokens)
                 query, grad_head = q_t[app, rows, :], do_t[rows, :]
                 empty = jnp.zeros_like(query)
+                query = jnp.concatenate([query, empty], 0)
                 grad_pad = jnp.concatenate([empty, grad_head], 0)
-                scores = dot(kv_g, jnp.concatenate([query, empty], 0)) * score_unit + bias[...]
-                chances = jnp.exp2(scores - lse[app, g, h : h + 1, :])
                 delta = jnp.sum(
-                    grad_head.astype(jnp.float32) * o_t[app, rows, :], 0, keepdims=True
+                    grad_head.astype(full) * x_attn[1, rows, app_tokens(app)].astype(full),
+                    0, keepdims=True,
                 )
-                grad_scores = (chances * (dot(kv_g, grad_pad) - delta)).astype(low_type)
-                small = (query.astype(jnp.float32) * score_scale).astype(low_type)
-                total = total + dot(
-                    grad_scores, jnp.concatenate([small, empty], 0), (1, 1)
-                ) + dot(chances.astype(low_type), grad_pad, (1, 1))
-                dq_t[rows, :] = dot(k_t, grad_scores) * score_scale
-            kv_send[app, g] = total.astype(low_type)
+                log_sum = lse[app, g, h : h + 1, :]
+                for start in range(0, size.length, 256):
+                    keys_at = slice(start, start + 256)
+                    part = dot(kv[app, g, keys_at, :], query) * score_unit + bias[keys_at, :]
+                    chance = jnp.exp2(part - log_sum)
+                    chances[keys_at, cols] = chance.astype(low_type)
+                    change = dot(kv[app, g, keys_at, :], grad_pad) - delta
+                    grad_scores[keys_at, cols] = (chance * change).astype(low_type)
+                sides.append(((query.astype(full) * score_scale).astype(low_type), grad_pad))
+                accum[rows, :] = dot(k_t, grad_scores[:, cols]) * score_scale
+            small, grad_pad = (jnp.concatenate(side, 1) for side in zip(*sides))
+            kv_send[app, g] = (
+                dot(grad_scores[...], small, (1, 1)) + dot(chances[...], grad_pad, (1, 1))
+            ).astype(low_type)
             for k in range(1, ctx_count):
                 @pl.when(ctx - k >= 0)
                 def _():
@@ -621,60 +668,57 @@
             return carry
 
         lax.fori_loop(0, groups, heads, 0)
-        for start in range(0, size.width, LANES):
-            stop = min(start + LANES, size.width)
-            tile = rope_rows(dq_t[start:stop, :], -1.0)
-            d_attn[0, app_tokens(app), start:stop] = tile.astype(low_type).T
-        d_attn[:, app_tokens(app), size.width :] = jnp.zeros(
-            (2, tokens, d_attn.shape[2] - size.width), low_type
-        )
-        turned = []
+        for start in range(0, width, 2 * LANES):
+            stop = min(start + 2 * LANES, width)
+            tile = rope(accum[start:stop, :], -1.0).astype(low_type)
+            natural[:, start:stop] = tile.T
+            do_t[start:stop, :] = tile
+        d_attn[0, app_tokens(app), :width] = natural[...]
+        pairs = [[], []]
         for g in range(groups):
-            tile = kv_send[app, g, own_rows, :].astype(jnp.float32)
+            tile = kv_send[app, g, own_rows, :].astype(full)
             for k in range(1, ctx_count):
                 @pl.when(ctx + k < ctx_count)
                 def _():
                     grad_copy(app, g, k).wait_recv()
                 tile = tile + jnp.where(
-                    ctx + k < ctx_count, kv_recv[app, k - 1, g].astype(jnp.float32), 0.0
+                    ctx + k < ctx_count, kv_recv[app, k - 1, g].astype(full), 0.0
                 )
-            tile = rope_lanes(tile, -sin_kv[...])
-            turned.append((tile, pltpu.roll(tile, HEAD_DIM, 1)))
-        empty = jnp.zeros((tokens, LANES), jnp.float32)
-        pairs = []
+            tile = tile.T
+            pairs[0].append(rope(tile[:HEAD_DIM], -1.0).astype(low_type))
+            pairs[1].append(tile[HEAD_DIM:].astype(low_type))
+        spare = d_pair.shape[2] - size.kv_width
         for half in range(2):
-            pieces = [(one, other) if half == 0 else (other, one) for one, other in turned]
-            tiles = [jnp.where(lower, 0.0, pieces[0][1])]
-            for g in range(1, groups, 2):
-                tiles.append(jnp.where(lower, pieces[g][0], pieces[g + 1][1]))
-            for number, tile in enumerate(tiles):
-                d_pair[half, app_tokens(app), number * LANES : (number + 1) * LANES] = tile.astype(
-                    low_type
-                )
-            straight = [
-                jnp.where(lower, pieces[g][0], pieces[g + 1][1] if g + 1 < groups else empty)
-                for g in range(0, groups, 2)
-            ]
-            pairs.append(
-                jnp.concatenate(straight, 1)[:, : size.kv_width].astype(low_type)
-            )
+            pairs[half] = jnp.concatenate(pairs[half], 0)
+            d_pair[half, app_tokens(app), :] = jnp.concatenate(
+                [jnp.zeros((spare, tokens), low_type), pairs[half]], 0
+            ).T
         grad_normed = (
-            dot(d_attn[0, app_tokens(app), : size.width], wq[...], (1, 1))
-            + dot(pairs[0], wk[...], (1, 1))
-            + dot(pairs[1], wv[...], (1, 1))
-        )
-        grad, gain_grad = norm_back(xin[app].astype(jnp.float32), gain_attn[...], grad_normed)
-        gain_sums[0:1] += gain_grad
-        return dmid[...] + grad
+            dot(wq[...], do_t[...])
+            + dot(wk[...], pairs[0], (0, 0))
+            + dot(wv[...], pairs[1], (0, 0))
+        )
+        return dmid[...] + norm_back(xin[app].astype(full), 0, grad_normed)
+
+    def keep_grad(app, value):
+        @pl.when(section == app)
+        def _():
+            grads[section] = value
+
+        @pl.when(section != app)
+        def _():
+            grad_stage[...] = value
+            back_copy.start()
 
     gain_sums[...] = jnp.zeros_like(gain_sums)
+    d_attn[:, :, width:] = jnp.zeros((2, 2 * tokens, d_attn.shape[2] - width), low_type)
     loads[0].wait()
     forward(0)
     forward(1)
-    loads[8].wait()
+    loads[10].wait()
     low = backward(1, cot[...]).astype(low_type)
-    grad_mid[...] = low
-    grad_in[...] = backward(0, low)
+    keep_grad(1, low.astype(full))
+    keep_grad(0, backward(0, low))
 
     def drain(g, carry):
         for app in range(2):
@@ -689,60 +733,68 @@
         return carry
 
     lax.fori_loop(0, groups, drain, 0)
+    act_copies[0].wait()
+    back_copy.wait()
 
 
 def run_block(size, plan, *operands):
     tokens, width, hidden, groups = size.tokens, size.width, size.hidden, size.kv_heads
     low, full = jnp.bfloat16, jnp.float32
-    wide, kv_wide = plan.width_tiles * LANES, (plan.pair_tiles - plan.width_tiles + 1) * LANES
+    padded, kv_wide = plan.width_tiles * LANES, (plan.pair_tiles - plan.width_tiles + 1) * LANES
     both = 2 * tokens
     vmem = pl.BlockSpec(memory_space=pltpu.VMEM)
     far = pl.BlockSpec(memory_space=pl.ANY)
     dma = pltpu.SemaphoreType.DMA
     others = max(size.ctx - 1, 1)
     shapes = [
-        ((2, tokens, width), low),
-        ((tokens, width), low),
-        ((tokens, width), full),
+        ((2, width, tokens), low),
+        ((2, width, tokens), full),
         ((2, width, both), low),
         ((width, both), low),
-        ((hidden, both), low),
-        ((2, both, wide), low),
+        ((width, both), low),
+        ((both, hidden), low),
+        ((2, both, padded), low),
         ((2, both, kv_wide), low),
         ((2, both, hidden), low),
-        ((both, wide), low),
-        ((2, width), full),
+        ((8, padded), full),
     ]
     scratch = [
         ((width, width), low),
-        ((width, size.kv_width), low),
-        ((width, size.kv_width), low),
+        ((size.kv_width, width), low),
+        ((size.kv_width, width), low),
         ((width, width), low),
         ((width, hidden), low),
         ((width, hidden), low),
-        ((hidden, width), low),
-        ((2, tokens, width), low),
-        ((tokens, width), low),
-        ((2, tokens, width), full),
+        ((width, hidden), low),
+        ((HEAD_DIM // 2, tokens), full),
+        ((HEAD_DIM // 2, tokens), full),
+        ((2, width, LANES), full),
+        ((2, width, tokens), low),
+        ((width, tokens), low),
+        ((width, tokens), low),
+        ((width, tokens), full),
+        ((2, width, tokens), full),
         ((2, width, tokens), low),
         ((2, groups, size.length, LANES), low),
         ((2, groups, size.length, LANES), low),
         ((2, others, groups, tokens, LANES), low),
         ((2, groups, 8, tokens), full),
-        ((2, width, tokens), full),
         ((width, tokens), low),
+        ((size.length, tokens), full),
         ((width, tokens), full),
-        ((size.length, tokens), full),
-        ((tokens, width), full),
-        ((tokens, width), full),
+        ((width, tokens), full),
+        ((tokens, width), low),
+        ((size.group, size.length, tokens), full),
+        ((size.length, size.group * tokens), low),
+        ((size.length, size.group * tokens), low),
     ]
     return pl.pallas_call(
         functools.partial(block_kernel, size),
         out_shape=[jax.ShapeDtypeStruct(*shape) for shape in shapes],
-        in_specs=[far, far] + [vmem] * 7 + [far] * 7,
+        in_specs=[far, far, vmem, far, far, vmem] + [far] * 7,
         out_specs=[vmem] * len(shapes),
         scratch_shapes=[pltpu.VMEM(*shape) for shape in scratch] + [
-            dma((9,)), dma((2, 2, groups, others)), dma((2, 2, groups, others)),
+            dma((11,)), dma((2, 2, groups, others)), dma((2, 2, groups, others)), dma((4,)),
         ],
         compiler_params=pltpu.CompilerParams(
             collective_id=1, has_side_effects=True, vmem_limit_bytes=64 << 20
@@ -756,12 +808,72 @@
 def rotary(length):
     half = HEAD_DIM // 2
     frequency = 10000.0 ** (-2.0 * np.arange(half) / HEAD_DIM)
-    angles = np.arange(length)[:, None] * frequency[None, :]
-    cos, sine = np.cos(angles), np.sin(angles)
-    kept, none = np.ones((length, HEAD_DIM)), np.zeros((length, HEAD_DIM))
-    cos_kv = np.concatenate([cos, cos, kept], 1)
-    sin_kv = np.concatenate([-sine, sine, none], 1)
-    return [np.asarray(table, np.float32) for table in (cos, sine, cos_kv, sin_kv)]
+    angles = frequency[:, None] * np.arange(length)[None, :]
+    return np.asarray(np.cos(angles), np.float32), np.asarray(np.sin(angles), np.float32)
+
+
+def unpack_kernel(plan, sizes, *refs):
+    width, hidden, kv_width, through = sizes
+    summed, refs = refs[0], refs[1:]
+    (query, key_t, value_t, out, gate, up, down_t, *gains), rest = refs[through : through + 9], refs[through + 9 :]
+    for source, target in zip(refs[:through], rest):
+        target[...] = source[...]
+    full, rows, half_width = jnp.float32, width // plan.dp, width // 2
+
+    def tile(half, index, first, count):
+        parts = [
+            summed[half, p, place : place + size, :]
+            for p, place, inside, size in plan.spans(index, first, count)
+        ]
+        return (parts[0] if len(parts) == 1 else jnp.concatenate(parts, 0)).astype(full)
+
+    def put(target, at, cols, value):
+        count = min(LANES, target.shape[1] - cols)
+        target[at : at + value.shape[0], cols : cols + count] = value[:, :count]
+
+    for index, (kind, start, tiles, height, piece) in enumerate(plan.chunks):
+        for half in range(2):
+            for number in range(tiles):
+                value = tile(half, index, number * height, height)
+                cols = (start + number) * LANES
+                if kind == "ffn":
+                    put((gate, up)[half], 0, cols, value[:rows])
+                elif kind == "down":
+                    put(down_t, half * half_width, cols, value[:half_width])
+                elif kind == "attn":
+                    put((query, out)[half], 0, cols, value[:rows])
+                else:
+                    spare = plan.width_tiles * LANES - width
+                    if number == 0:
+                        put((query, out)[half], 0, width + spare - LANES, value[:rows])
+                    pair_t = value.T[:, :rows]
+                    first = number * LANES - LANES + spare
+                    if first < 0:
+                        pair_t = pair_t[LANES - spare :]
+                        first = 0
+                    (key_t, value_t)[half][first : first + pair_t.shape[0], :] = pair_t
+            if kind == "mixed":
+                lines = tile(half, index, tiles * height, 16)
+                for number in range(-(-rows // LANES)):
+                    put(gains[half], 0, number * LANES, lines[number : number + 1])
+
+
+def unpack(plan, sizes, summed, *through):
+    width, hidden, kv_width = sizes
+    rows, full = width // plan.dp, jnp.float32
+    shapes = [
+        (rows, width), (kv_width, rows), (kv_width, rows), (rows, width),
+        (rows, hidden), (rows, hidden), (width, hidden // plan.dp), (1, rows), (1, rows),
+    ]
+    vmem = pl.BlockSpec(memory_space=pltpu.VMEM)
+    return pl.pallas_call(
+        functools.partial(unpack_kernel, plan, (*sizes, len(through))),
+        out_shape=[jax.ShapeDtypeStruct(shape, full) for shape in shapes]
+        + [jax.ShapeDtypeStruct(value.shape, value.dtype) for value in through],
+        in_specs=[vmem] * (1 + len(through)),
+        out_specs=[vmem] * (len(shapes) + len(through)),
+        compiler_params=pltpu.CompilerParams(vmem_limit_bytes=60 << 20),
+    )(summed, *through)
 
 
 def plain_block(
@@ -1032,15 +1144,18 @@
         cut = jnp.pad(cut, ((0, 0), (0, 0), (0, rows - cut.shape[2])))
         return cut.transpose(1, 2, 0)
 
-    halves = inner.reshape(tokens, dp, 2, -1)
-    inner_t = jnp.stack([sides(halves[:, :, h], plan.down_rows) for h in range(2)], 1)
+    inner = inner.reshape(tokens, dp, -1)
+    inner = jnp.pad(
+        inner, ((0, 0), (0, 0), (0, plan.down_tiles * LANES - inner.shape[2]))
+    ).reshape(tokens, -1)
     spare = plan.width_tiles * LANES - model_width
     gain_sums = jnp.stack([one + other for one, other in zip(first_grads[:2], second_grads[:2])])
+    gain_sums = jnp.pad(gain_sums, ((0, 6), (0, plan.width_tiles * LANES - model_width)))
     factors = (
         sides(ffn, plan.rows),
         jnp.stack([d_gate, d_up]),
-        inner_t.reshape(2 * dp, plan.down_rows, tokens),
-        jnp.pad(d_out, ((0, 0), (0, spare))),
+        d_out.T.reshape(2, plan.down_rows, tokens),
+        inner,
         jnp.stack([sides(normed, plan.rows), sides(attn, plan.rows)]),
         jnp.pad(jnp.stack([d_query, d_branch]), ((0, 0), (0, 0), (0, spare))),
         jnp.pad(
@@ -1057,28 +1172,23 @@
     gain_attn, w_query, w_key, w_value, w_out, gain_ffn, w_gate, w_up, w_down,
 ):
     tokens, width, dp = size.tokens, size.width, plan.dp
-    first_token = lax.axis_index("ctx") * tokens
-    cos_q, sin_q, cos_kv, sin_kv = (
-        lax.dynamic_slice_in_dim(jnp.asarray(table), first_token, tokens, 0)
-        for table in rotary(size.length)
-    )
-    (
-        acts, grad_mid, grad_in, x_attn, n2_t, inner_t, d_attn, d_pair, d_ffn, d_out, gain_sums
-    ) = run_block(
-        size, plan, inputs[:, 0], cotangent[:, 0], segment_ids, cos_q.T, sin_q.T, cos_kv, sin_kv,
-        gain_attn.astype(jnp.float32)[None], gain_ffn.astype(jnp.float32)[None],
-        w_query, w_key, w_value, w_out, w_gate, w_up, w_down,
+    cos_in, sin_in = rotary(size.length)
+    gains = jnp.stack([gain_attn, gain_ffn]).astype(jnp.float32)
+    gains = jnp.pad(gains, ((0, 0), (0, plan.width_tiles * LANES - width)))
+    acts, grads, x_attn, n2_t, df_t, inner, d_attn, d_pair, d_ffn, gain_sums = run_block(
+        size, plan, inputs[:, 0].swapaxes(1, 2), cotangent[:, 0].swapaxes(1, 2), segment_ids,
+        cos_in, sin_in, gains, w_query, w_key.T, w_value.T, w_out, w_gate, w_up, w_down.T,
     )
     factors = (
         n2_t.reshape(dp, plan.rows, -1),
         d_ffn,
-        inner_t.reshape(2 * dp, plan.down_rows, -1),
-        d_out,
+        df_t.reshape(2, plan.down_rows, -1),
+        inner,
         x_attn.reshape(2, dp, plan.rows, -1),
         d_attn,
         d_pair,
     )
-    return (acts[0][None], acts[1][None]), (grad_in[None], grad_mid[None]), gain_sums, factors
+    return acts, grads, gain_sums, factors
 
 
 def body(
@@ -1107,17 +1217,15 @@
         and size.length <= 1024
         and tok_local % LANES == 0
         and plan.rows * dp == model_width
-        and plan.down_rows * dp * 2 == hidden
+        and plan.down_tiles * LANES * dp == hidden
     )
     run = functools.partial(fused_block, size) if fits else plain_block
     acts, grads, gain_sums, factors = run(
         plan, inputs, segment_ids, cotangent,
         gain_attn, w_query, w_key, w_value, w_out, gain_ffn, w_gate, w_up, w_down,
     )
-    extra = jnp.pad(
-        gain_sums.reshape(2, dp, -1), ((0, 0), (0, 0), (0, 16 * LANES - model_width // dp))
-    ).reshape(2, dp, 16, LANES)
-    summed = reduce_grads(plan, *factors, extra)
+    summed = reduce_grads(plan, *factors, gain_sums)
+    sizes = (model_width, hidden, kv_width)
 
     def exchange(for_first, for_last):
         kept = jnp.where(on_first, for_first, for_last)
@@ -1127,52 +1235,29 @@
             on_first, jnp.stack([kept, got]), jnp.stack([got, kept])
         )
 
-    def tiles_of(kind):
-        found = []
-        for index, (name, start, tiles, rows, piece) in enumerate(plan.chunks):
-            if name == kind:
-                first = plan.offsets[index]
-                flat = summed[:, :, first : first + piece].reshape(2, -1, LANES)
-                found.append(flat[:, : tiles * rows].reshape(2, tiles, rows, LANES))
-        return jnp.concatenate(found, 1)
-
-    def joined(values, rows):
-        values = values[:, :, :rows].transpose(0, 2, 1, 3)
-        return values.reshape(2, rows, -1).astype(jnp.float32)
-
-    ffn_sum = joined(tiles_of("ffn"), model_width // dp)
-    down_sum = joined(tiles_of("down"), w_down.shape[0] // dp // 2)[:, :, :model_width]
-    attn_sum = joined(
-        jnp.concatenate([tiles_of("attn"), tiles_of("mixed")], 1), model_width // dp
-    )
-    kind, start, tiles, rows, piece = plan.chunks[-1]
-    flat = summed[:, :, plan.offsets[-1] : plan.offsets[-1] + piece].reshape(2, -1)
-    flat = flat[:, tiles * rows * LANES :][:, : model_width // dp].astype(jnp.float32)
-    totals = (
-        flat[0],
-        attn_sum[0, :, :model_width],
-        attn_sum[0, :, model_width:],
-        attn_sum[1, :, model_width:],
-        attn_sum[1, :, :model_width],
-        flat[1],
-        ffn_sum[0],
-        ffn_sum[1],
-        down_sum.reshape(-1, model_width),
-    )
-    activations = exchange(*acts)[None]
-    input_grads = exchange(grads[0].astype(jnp.bfloat16), grads[1]).astype(jnp.float32)[None]
+    def turned(values):
+        return values[None, :, None].swapaxes(3, 4)
+
+    if fits:
+        *parts, acts, grads = unpack(plan, sizes, summed, acts, grads)
+        activations, input_grads = turned(acts), turned(grads)
+    else:
+        parts = unpack(plan, sizes, summed)
+        activations = exchange(*acts)[None]
+        input_grads = exchange(grads[0].astype(jnp.bfloat16), grads[1]).astype(jnp.float32)[None]
+    query, key_t, value_t, out, gate, up, down_t, gain_one, gain_two = parts
     return (
         activations,
         input_grads,
-        totals[0],
-        totals[1],
-        totals[2],
-        totals[3],
-        totals[4],
-        totals[5],
-        totals[6],
-        totals[7],
-        totals[8],
+        gain_one.reshape(-1),
+        query,
+        key_t.T,
+        value_t.T,
+        out,
+        gain_two.reshape(-1),
+        gate,
+        up,
+        down_t.T,
     )
 
 

time: 330 us -> 251 us (0.76); the launches traced: 325 us -> 251 us
  local copies, waits for them, and re-layouts: 63 us -> 1.37 us
  other arithmetic: 14.8 us -> 0.61 us
    unnamed x31 -> x0, local copies, waits for them, and re-layouts: 40.5 us -> none
    slice x8 -> x0, local copies, waits for them, and re-layouts: 12.1 us -> none  [the longest x2 5.75 us: body(): ffn_sum[1]]
    pallas_call x0 -> x1, Pallas kernels: none -> 8.24 us  [unpack(): pl.pallas_call(functools.partial(unpack_kernel, plan, (*sizes, len(throug...]
    pallas_call x1, Pallas kernels: 114 us -> 108 us  [run_block(): pl.pallas_call(functools.partial(block_kernel, size), out_shape=[jax.Shap...]
    convert_element_type x5 -> x0, other arithmetic: 5.39 us -> none  [the longest x3 3.82 us: joined(): return values.reshape(2, rows, -1).astype(jnp.float32)]
    another operation x2 -> x0, other arithmetic: 3.42 us -> none  [exchange(): return jnp.where(on_first, jnp.stack([kept, got]), jnp.stack([got, kept]))]
  transfers between devices with their start and end apart: 2 -> 0, of which waited for: 0 -> 0; matrix products, arithmetic and copies ran while one was open for 16% -> 0% of each run, Pallas kernels for 41% -> 0%
where the time goes in v4:
time: 251 us
  Pallas kernels  248 us (99%)
    pallas_call x1, Pallas kernels, reduce_grads(): pl.pallas_call(functools.partial(reduce_kernel, plan), out_shape=jax.Shap...  132 us
    pallas_call x1, Pallas kernels, run_block(): pl.pallas_call(functools.partial(block_kernel, size), out_shape=[jax.Shap...  108 us
    pallas_call x1, Pallas kernels, unpack(): pl.pallas_call(functools.partial(unpack_kernel, plan, (*sizes, len(throug...  8.24 us

profile of v4, /device:TPU:0, one launch (start us, length us, event | category | flops | bytes accessed | tf_op | source)
XLA Modules:
  0.0 250.6 jit_solution(16407213427851606716)
XLA Ops:
  0.6 0.7 stack.9
  1.3 0.7 stack.10
  2.0 0.6 fusion.3.gains
  2.6 108.2 %shard_map.221 = (bf16[2,960,256]{2,1,0:T(8,128)(2,1)}, f32[2,960,256]{2,1,0:T(8,128)}, bf16[2,960,512]{2,1,0:T(8,128)(2,1)}, bf16[960,512]{1,0:T(8,128)(2,1)}, ...) custom-call(bf16[2,960,256]{2,1,0:T(8,128)(2,1)} %bitcast.30, ...), custom_call_target="tpu_custom_call" | custom-call | flops 40000000000 | bytes 40000000 | tf_op jit(solution)/shard_map/pallas_call | solution.py:791
  110.9 131.5 %shard_map.222.refs_0_ = bf16[2,4,2432,128]{3,2,1,0:T(8,128)(2,1)} custom-call(bf16[4,240,512]{2,1,0:T(8,128)(2,1)} %bitcast.40, bf16[2,512,2560]{2,1,0:T(8,128)(2,1)} %get-tuple-element.33.ffn_dy, bf16[2,480,512]{2,1,0:T(8,128)(2,1)} %bitcast.41, bf16[512,2560]{1,0:T(8,128)(2,1)} %get-tuple-element.35.down_dy, bf16[2,4,240,512]{3,2,1,0:T(8,128)(2,1)} %bitcast.39, ...), custom_call_target="tpu_custom_call" | custom-call | flops 10000000000 | bytes 20000000 | tf_op jit(solution)/shard_map/pallas_call | solution.py:353
  242.4 8.2 %shard_map.223 = (f32[240,960]{1,0:T(8,128)}, f32[320,240]{1,0:T(8,128)}, f32[320,240]{1,0:T(8,128)}, f32[240,960]{1,0:T(8,128)}, f32[240,2560]{1,0:T(8,128)}, /...) custom-call(bf16[2,4,2432,128]{3,2,1,0:T(8,128)(2,1)} %shard_map.222, ...), custom_call_target="tpu_custom_call" | custom-call | tf_op jit(solution)/shard_map/pallas_call | solution.py:869
